TPU v7x, 256 devices: a whole 4x4x8 slice. The times are simulated.
256 devices in a mesh: real: 4 (over z_lo), sx: 8 (over x, z_hi), sy: 8 (over y, core).
Axes of the slice: x: 4, y: 4, z: 8 (z_hi: 2, z_lo: 4; z = z_hi * 4 + z_lo), core: 2. Of those that a mesh axis runs over, the one named last changes fastest.
Arguments:
- noise: float32 [64, 256, 512], P('sx', 'sy', 'real'), parts along dimension 2, may hold values from -6 to 6
- classes: int32 [64, 256, 64], P('sx', 'sy'), may hold values from 0 to 7
- table: float32 [8, 27], replicated, may hold values from 0 to 0.07
- obs_matrix: bfloat16 [512, 256, 512], P(('sx', 'sy')), may hold values from -0.25 to 0.25
- node_block: int32 [512], P(('sx', 'sy')), may hold values from 0 to 31
- sample_block: int32 [512], P(('sx', 'sy')), may hold values from 0 to 127
- sample_count: int32 [512], P(('sx', 'sy')), may hold values from 1 to 256, as said below
- drill_data: float32 [128, 256], P(('sx', 'sy')), may hold values from -6 to 6
- obs_gain: float32 [128, 256], P(('sx', 'sy')), may hold values from 0.1 to 1
Outputs:
- conditioned: float32 [64, 256, 512], P('sx', 'sy', 'real'), parts along dimension 2
- misfit: float32 [128, 8, 256], P(('sx', 'sy'), 'real'), parts along dimension 1
There are 4 independent parts, one for each index of `real`. A program takes and returns all parts, laid end to end along the dimension named above; an argument that names none is the same for every part. Nothing has to cross between parts.
Inputs may be any that keep to these rules, and one draw needn't show every extreme that they name: `sample_count`: the largest value is reached in every draw. `sample_block`: sample block k is held by tile k // 2.
All inputs are finite; a program needn't handle non-finite values.
Results may differ from a plain program's by a relative error of at most 0.0003.
Values sent between devices are 32-bit elements; how exact they have to be, the bound alone decides.
No kernel may reach another device: no remote copies, remote signals or barrier semaphores. Data moves between devices by JAX's collectives and lax.ppermute only.
A program may use at most 128 MiB of HBM per device.

v0:
```python
import jax
import jax.numpy as jnp
from jax import lax
from jax.sharding import PartitionSpec as P

CHEB = (0.6, 0.5, 0.3, 0.2)


def with_halo(block, sides, width):
    for axis, dim in sides:
        count = lax.axis_size(axis)
        forward = [(i, i + 1) for i in range(count - 1)]
        backward = [(target, source) for source, target in forward]
        low = lax.ppermute(
            lax.slice_in_dim(block, block.shape[dim] - width, None, axis=dim), axis, forward
        )
        high = lax.ppermute(lax.slice_in_dim(block, 0, width, axis=dim), axis, backward)
        block = jnp.concatenate([low, block, high], axis=dim)
    return block


def stencil(padded, classes, table):
    size_x = padded.shape[0] - 2
    size_y = padded.shape[1] - 2
    layers = classes.shape[2]
    width = padded.shape[2]
    copies = width // layers
    level = jnp.arange(width, dtype=jnp.int32) % layers
    below = jnp.where(level > 0, jnp.roll(padded, 1, axis=2), 0.0)
    above = jnp.where(level < layers - 1, jnp.roll(padded, -1, axis=2), 0.0)
    shifted = (below, padded, above)
    onehot = (classes[..., None] == jnp.arange(table.shape[0], dtype=jnp.int32)).astype(jnp.float32)
    coeffs = jnp.einsum("xyzc,co->oxyz", onehot, table, precision=lax.Precision.HIGHEST)
    summed = jnp.zeros((size_x, size_y, width), jnp.float32)
    offset = 0
    for shift_x in range(3):
        for shift_y in range(3):
            for shift_z in range(3):
                weight = jnp.tile(coeffs[offset], (1, 1, copies))
                summed = (
                    summed
                    + weight
                    * shifted[shift_z][shift_x : shift_x + size_x, shift_y : shift_y + size_y, :]
                )
                offset += 1
    return summed


def shards(
    noise, classes, table, obs_matrix, node_block, sample_block, sample_count, drill_data, obs_gain
):
    size_x, size_y, width = noise.shape
    layers = classes.shape[2]
    copies = width // layers

    def operate(field):
        padded = with_halo(field, (("sx", 0), ("sy", 1)), 1)
        return stencil(padded, classes, table)

    second = operate(noise)
    third = 2.0 * operate(second) - noise
    fourth = 2.0 * operate(third) - second
    smooth = CHEB[0] * noise + CHEB[1] * second + CHEB[2] * third + CHEB[3] * fourth
    grid = smooth.reshape(size_x * size_y // 8, 8, copies, layers)
    chosen = grid[node_block]
    block_count = obs_matrix.shape[0]
    samples = obs_matrix.shape[1]
    matrix = obs_matrix.astype(jnp.float32).reshape(block_count, samples, 8, layers)
    live = (jnp.arange(samples, dtype=jnp.int32)[None, :] < sample_count[:, None]).astype(
        jnp.float32
    )
    partial_value = (
        jnp.einsum("bsak,bark->brs", matrix, chosen, precision=lax.Precision.HIGHEST)
        * live[:, None, :]
    )
    samples_own = drill_data.shape[0]
    onehot = (
        sample_block[:, None]
        == jnp.arange(samples_own * lax.axis_size(("sx", "sy")), dtype=jnp.int32)[None, :]
    ).astype(jnp.float32)
    totals = lax.psum_scatter(
        jnp.einsum("bc,brs->crs", onehot, partial_value, precision=lax.Precision.HIGHEST),
        ("sx", "sy"),
        scatter_dimension=0,
        tiled=True,
    )
    misfit = drill_data[:, None, :] - totals
    scaled = obs_gain[:, None, :] * misfit
    every = lax.all_gather(scaled, ("sx", "sy"), axis=0, tiled=True)
    selector = (
        sample_block[:, None] == jnp.arange(every.shape[0], dtype=jnp.int32)[None, :]
    ).astype(jnp.float32)
    picked = (
        jnp.einsum("bc,crs->brs", selector, every, precision=lax.Precision.HIGHEST)
        * live[:, None, :]
    )
    update = jnp.einsum("bsak,brs->bark", matrix, picked, precision=lax.Precision.HIGHEST)
    placing = (jnp.arange(grid.shape[0], dtype=jnp.int32)[:, None] == node_block[None, :]).astype(
        jnp.float32
    )
    added = jnp.einsum("nb,bark->nark", placing, update, precision=lax.Precision.HIGHEST)
    conditioned = (grid + added).reshape(size_x, size_y, width)
    return (conditioned, misfit)


def solution(mesh):
    in_specs = (
        P("sx", "sy", "real"),
        P("sx", "sy", None),
        P(),
        P(("sx", "sy"), None, None),
        P(("sx", "sy")),
        P(("sx", "sy")),
        P(("sx", "sy")),
        P(("sx", "sy"), None),
        P(("sx", "sy"), None),
    )
    out_specs = (P("sx", "sy", "real"), P(("sx", "sy"), "real", None))
    return jax.shard_map(shards, mesh=mesh, in_specs=in_specs, out_specs=out_specs, check_vma=False)
```

profile of v0, /device:TPU:1, one launch (start us, length us, event | category | flops | bytes accessed | tf_op | source)
XLA Modules:
  0.0 979.5 jit_solution(6456218859606767925)
XLA Ops:
  7.2 0.7 fusion.131
  8.0 9.6 collective-permute-start
  17.6 1.3 collective-permute-start.1
  18.9 2.7 convolution_bitcast_fusion
  21.7 2.5 fusion.120
  24.2 1.5 fusion.121
  25.7 0.5 broadcast_compare_fusion.1
  26.3 0.2 tile.212
  26.6 0.7 fusion.128
  27.3 3.4 collective-permute-start.3
  30.7 3.3 collective-permute-start.2
  34.1 0.2 tile.185
  34.3 0.2 tile.194
  34.6 0.2 tile.167
  35.8 0.2 tile.233
  36.3 0.2 tile.227
  37.5 0.2 tile.215
  38.6 0.2 tile.197
  39.7 1.0 tile.178
  40.7 0.2 tile.179
  40.9 1.8 tile.175
  42.7 1.1 tile.176
  43.8 0.8 tile.172
  44.6 1.1 tile.173
  45.7 1.7 tile.169
  47.5 1.8 tile.170
  49.3 1.7 tile.163
  51.0 1.8 tile.164
  52.7 1.7 tile.202
  54.5 1.8 tile.203
  56.3 0.8 pad_maximum_fusion
  57.6 1.5 fusion.16
  59.1 1.4 collective-permute-start.5
  60.6 8.3 collective-permute-start.4
  68.8 0.8 collective-permute-done.4
  69.7 2.5 collective-permute-start.7
  72.2 3.1 collective-permute-start.6
  75.4 0.7 collective-permute-done.6
  76.8 0.6 fusion.72
  77.4 1.3 collective-permute-start.9
  78.7 8.8 collective-permute-start.8
  87.5 0.8 collective-permute-done.8
  88.3 0.6 pad_maximum_fusion.15
  88.9 2.4 collective-permute-start.11
  91.3 4.8 collective-permute-start.10
  96.1 2.9 copy.18
  99.3 1.0 pad_maximum_fusion.3
  100.5 0.8 maximum_select_fusion.5
  101.4 0.7 maximum_maximum_fusion.1
  102.3 1.3 fusion.42
  103.6 1.1 reshape.144
  104.8 0.6 gather_fusion
  105.4 1.0 fusion
  106.4 1.1 fusion.107
  107.5 0.6 dynamic-slice
  108.8 742.9 %all-reduce.3.cloned.1.call-done = f32[128,2,256]{2,0,1:T(8,128)} async-done(((f32[128,2,256]{2,0,1:T(8,128)}), f32[128,2,256]{2,0,1:T(8,128)}) %all-reduce.3.cloned.1.call-update) | async-done | bytes 262160
  851.6 0.7 broadcast_multiply_fusion
  852.4 115.5 %all_gather.3 = f32[128,2,256]{2,1,0:T(2,128)S(1)} all-gather(f32[2,2,256]{2,1,0:T(2,128)S(1)} %copy.21), channel_id=1, replica_groups=mesh['real'=4,'sx'=8,'sy'=8] {'sx','sy'}, dimensions={0}, use_global_device_ids=true | all-gather | bytes 266240 | tf_op jit(solution)/shard_map/all_gather | solution.py:89
  967.8 0.2 fusion.2
  968.0 2.5 convolution_bitcast_fusion.1
  970.6 0.4 convolution_add_fusion
  971.0 0.2 copy.26
  971.2 0.8 reshape.146
  972.1 0.6 copy.27
  (199 shorter events, 6.1 us)
Async XLA Ops:
  7.2 11.7 %copy-start = (f32[8,27]{1,0:T(8,128)S(1)}, f32[8,27]{1,0:T(8,128)}, u32[]{:S(2)}) copy-start(f32[8,27]{1,0:T(8,128)} %param.11) | copy-start | bytes 2596
  7.2 844.5 %all-reduce.3.cloned.1.call-start = ((), (), s32[]{:S(2)}) async-start(), calls=%async_computation | async-start | bytes 524288
  8.0 18.6 %collective-permute-start = (f32[1,32,128]{2,1,0:T(8,128)S(1)}, f32[1,32,128]{2,1,0:T(8,128)S(1)}, u32[]{:S(2)}, u32[]{:S(2)}) collective-permute-start(f32[1,32,128]{2,1,0:T(8,128)S(1)} %get-tuple-element.64), channel_id=1, source_target_pairs={{0,8},{8,16},{16,24},{24,32},{32,40},{40,48},{48,56},{1,9},{9,17},... | collective-permute-start | bytes 49160 | tf_op jit(solution)/shard_map/ppermute | solution.py:14
  17.6 9.0 collective-permute-start.1
  25.7 50.7 %copy-start.54 = (pred[128]{0:T(512)(128)(4,1)}, pred[128]{0:T(512)(128)(4,1)S(1)}, u32[]{:S(2)}) copy-start(pred[128]{0:T(512)(128)(4,1)S(1)} %broadcast_compare_fusion) | copy-start | bytes 388
  26.5 8.9 copy-start.50
  26.6 8.9 copy-start.52
  26.6 7.4 copy-start.42
  27.3 29.0 %collective-permute-start.3 = (f32[10,1,128]{2,1,0:T(1,128)}, f32[10,1,128]{2,1,0:T(1,128)S(1)}, u32[]{:S(2)}, u32[]{:S(2)}) collective-permute-start(f32[10,1,128]{2,1,0:T(1,128)} %get-tuple-element.58), channel_id=1, source_target_pairs={{1,0},{2,1},{3,2},{4,3},{5,4},{6,5},{7,6},{9,8},{10,9},{11,10},{12... | collective-permute-start | bytes 15368 | tf_op jit(solution)/shard_map/ppermute | solution.py:17
  30.7 25.6 %collective-permute-start.2 = (f32[10,1,128]{2,1,0:T(1,128)}, f32[10,1,128]{2,1,0:T(1,128)}, u32[]{:S(2)}, u32[]{:S(2)}) collective-permute-start(f32[10,1,128]{2,1,0:T(1,128)} %get-tuple-element.57), channel_id=1, source_target_pairs={{0,1},{1,2},{2,3},{3,4},{4,5},{5,6},{6,7},{8,9},{9,10},{10,11},{11... | collective-permute-start | bytes 15368 | tf_op jit(solution)/shard_map/ppermute | solution.py:14
  36.2 40.4 %copy-start.2 = (f32[8,32,128]{2,1,0:T(8,128)}, f32[8,32,128]{2,1,0:T(8,128)S(1)}, u32[]{:S(2)}) copy-start(f32[8,32,128]{2,1,0:T(8,128)S(1)} %tile.230) | copy-start | bytes 393220
  36.5 40.1 %copy-start.4 = (f32[8,32,128]{2,1,0:T(8,128)}, f32[8,32,128]{2,1,0:T(8,128)S(1)}, u32[]{:S(2)}) copy-start(f32[8,32,128]{2,1,0:T(8,128)S(1)} %tile.227) | copy-start | bytes 393220
  36.8 39.8 %copy-start.6 = (f32[8,32,128]{2,1,0:T(8,128)}, f32[8,32,128]{2,1,0:T(8,128)S(1)}, u32[]{:S(2)}) copy-start(f32[8,32,128]{2,1,0:T(8,128)S(1)} %tile.224) | copy-start | bytes 393220
  37.1 39.5 %copy-start.8 = (f32[8,32,128]{2,1,0:T(8,128)}, f32[8,32,128]{2,1,0:T(8,128)S(1)}, u32[]{:S(2)}) copy-start(f32[8,32,128]{2,1,0:T(8,128)S(1)} %tile.221) | copy-start | bytes 393220
  37.4 39.3 %copy-start.10 = (f32[8,32,128]{2,1,0:T(8,128)}, f32[8,32,128]{2,1,0:T(8,128)S(1)}, u32[]{:S(2)}) copy-start(f32[8,32,128]{2,1,0:T(8,128)S(1)} %tile.218) | copy-start | bytes 393220
  37.7 39.0 %copy-start.12 = (f32[8,32,128]{2,1,0:T(8,128)}, f32[8,32,128]{2,1,0:T(8,128)S(1)}, u32[]{:S(2)}) copy-start(f32[8,32,128]{2,1,0:T(8,128)S(1)} %tile.215) | copy-start | bytes 393220
  37.9 38.7 %copy-start.14 = (f32[8,32,128]{2,1,0:T(8,128)}, f32[8,32,128]{2,1,0:T(8,128)S(1)}, u32[]{:S(2)}) copy-start(f32[8,32,128]{2,1,0:T(8,128)S(1)} %tile.209) | copy-start | bytes 393220
  38.2 38.4 %copy-start.16 = (f32[8,32,128]{2,1,0:T(8,128)}, f32[8,32,128]{2,1,0:T(8,128)S(1)}, u32[]{:S(2)}) copy-start(f32[8,32,128]{2,1,0:T(8,128)S(1)} %tile.206) | copy-start | bytes 393220
  38.5 38.2 %copy-start.18 = (f32[8,32,128]{2,1,0:T(8,128)}, f32[8,32,128]{2,1,0:T(8,128)S(1)}, u32[]{:S(2)}) copy-start(f32[8,32,128]{2,1,0:T(8,128)S(1)} %tile.200) | copy-start | bytes 393220
  38.6 5.2 copy-start.45
  38.8 37.9 %copy-start.20 = (f32[8,32,128]{2,1,0:T(8,128)}, f32[8,32,128]{2,1,0:T(8,128)S(1)}, u32[]{:S(2)}) copy-start(f32[8,32,128]{2,1,0:T(8,128)S(1)} %tile.197) | copy-start | bytes 393220
  39.1 37.6 %copy-start.22 = (f32[8,32,128]{2,1,0:T(8,128)}, f32[8,32,128]{2,1,0:T(8,128)S(1)}, u32[]{:S(2)}) copy-start(f32[8,32,128]{2,1,0:T(8,128)S(1)} %tile.191) | copy-start | bytes 393220
  39.4 37.3 %copy-start.24 = (f32[8,32,128]{2,1,0:T(8,128)}, f32[8,32,128]{2,1,0:T(8,128)S(1)}, u32[]{:S(2)}) copy-start(f32[8,32,128]{2,1,0:T(8,128)S(1)} %tile.188) | copy-start | bytes 393220
  39.7 37.1 %copy-start.26 = (f32[8,32,128]{2,1,0:T(8,128)}, f32[8,32,128]{2,1,0:T(8,128)S(1)}, u32[]{:S(2)}) copy-start(f32[8,32,128]{2,1,0:T(8,128)S(1)} %tile.182) | copy-start | bytes 393220
  40.9 35.8 %copy-start.28 = (f32[8,32,128]{2,1,0:T(8,128)}, f32[8,32,128]{2,1,0:T(8,128)S(1)}, u32[]{:S(2)}) copy-start(f32[8,32,128]{2,1,0:T(8,128)S(1)} %tile.179) | copy-start | bytes 393220
  40.9 15.4 %copy-start.43 = (f32[10,32,128]{2,1,0:T(8,128)S(1)}, f32[10,32,128]{2,1,0:T(8,128)}, u32[]{:S(2)}) copy-start(f32[10,32,128]{2,1,0:T(8,128)} %copy-done.42) | copy-start | bytes 491524
  43.8 13.7 %copy-start.30 = (f32[8,32,128]{2,1,0:T(8,128)}, f32[8,32,128]{2,1,0:T(8,128)S(1)}, u32[]{:S(2)}) copy-start(f32[8,32,128]{2,1,0:T(8,128)S(1)} %tile.176) | copy-start | bytes 393220
  45.7 11.8 %copy-start.33 = (f32[8,32,128]{2,1,0:T(8,128)}, f32[8,32,128]{2,1,0:T(8,128)S(1)}, u32[]{:S(2)}) copy-start(f32[8,32,128]{2,1,0:T(8,128)S(1)} %tile.173) | copy-start | bytes 393220
  47.5 9.8 %copy-start.56 = (pred[128]{0:T(512)(128)(4,1)S(1)}, pred[128]{0:T(512)(128)(4,1)}, u32[]{:S(2)}) copy-start(pred[128]{0:T(512)(128)(4,1)} %broadcast_compare_fusion.1) | copy-start | bytes 388
  52.7 4.8 copy-start.51
  52.7 4.8 copy-start.53
  57.6 17.7 %copy-start.61 = (s32[8]{0:T(128)S(1)}, s32[8]{0:T(128)}, u32[]{:S(2)}) copy-start(s32[8]{0:T(128)} %param.15) | copy-start | bytes 100
  59.1 17.2 %copy-start.57 = (pred[128]{0:T(512)(128)(4,1)S(1)}, pred[128]{0:T(512)(128)(4,1)}, u32[]{:S(2)}) copy-start(pred[128]{0:T(512)(128)(4,1)} %broadcast_compare_fusion.1) | copy-start | bytes 388
  59.1 17.7 %copy-start.31 = (f32[8,32,128]{2,1,0:T(8,128)S(1)}, f32[8,32,128]{2,1,0:T(8,128)}, u32[]{:S(2)}) copy-start(f32[8,32,128]{2,1,0:T(8,128)} %copy-done.30) | copy-start | bytes 393220
  59.1 17.7 %copy-start.34 = (f32[8,32,128]{2,1,0:T(8,128)S(1)}, f32[8,32,128]{2,1,0:T(8,128)}, u32[]{:S(2)}) copy-start(f32[8,32,128]{2,1,0:T(8,128)} %copy-done.33) | copy-start | bytes 393220
  59.1 17.7 %copy-start.36 = (f32[8,32,128]{2,1,0:T(8,128)S(1)}, f32[8,32,128]{2,1,0:T(8,128)}, u32[]{:S(2)}) copy-start(f32[8,32,128]{2,1,0:T(8,128)} %tile.170) | copy-start | bytes 393220
  59.1 9.7 collective-permute-start.5
  60.6 9.1 collective-permute-start.4
  69.7 5.7 collective-permute-start.7
  72.2 3.8 collective-permute-start.6
  76.8 10.7 %copy-start.62 = (s32[8]{0:T(128)S(1)}, s32[8]{0:T(128)}, u32[]{:S(2)}) copy-start(s32[8]{0:T(128)} %param.13) | copy-start | bytes 100
  77.4 10.1 %collective-permute-start.9 = (f32[1,32,128]{2,1,0:T(8,128)S(1)}, f32[1,32,128]{2,1,0:T(8,128)S(1)}, u32[]{:S(2)}, u32[]{:S(2)}) collective-permute-start(f32[1,32,128]{2,1,0:T(8,128)S(1)} %get-tuple-element.60), channel_id=1, source_target_pairs={{8,0},{16,8},{24,16},{32,24},{40,32},{48,40},{56,48},{9,1},{17,9},... | collective-permute-start | bytes 49160 | tf_op jit(solution)/shard_map/ppermute | solution.py:17
  78.7 9.7 collective-permute-start.8
  87.5 8.6 copy-start.46
  88.3 7.8 copy-start.48
  88.9 10.3 %collective-permute-start.11 = (f32[10,1,128]{2,1,0:T(1,128)}, f32[10,1,128]{2,1,0:T(1,128)}, u32[]{:S(2)}, u32[]{:S(2)}) collective-permute-start(f32[10,1,128]{2,1,0:T(1,128)} %get-tuple-element.52), channel_id=1, source_target_pairs={{1,0},{2,1},{3,2},{4,3},{5,4},{6,5},{7,6},{9,8},{10,9},{11,10},{12... | collective-permute-start | bytes 15368 | tf_op jit(solution)/shard_map/ppermute | solution.py:17
  91.3 7.9 collective-permute-start.10
  99.0 3.1 copy-start.3
  99.0 3.1 copy-start.5
  99.1 3.1 copy-start.7
  99.1 3.1 copy-start.9
  99.1 3.1 copy-start.11
  99.1 3.1 copy-start.13
  99.1 3.1 copy-start.15
  99.1 3.1 copy-start.17
  99.1 3.1 copy-start.19
  99.1 3.1 copy-start.21
  99.1 3.1 copy-start.23
  99.1 3.1 copy-start.25
  99.2 3.1 copy-start.27
  103.6 3.9 copy-start.64
  103.6 748.0 %copy-start.59 = (f32[2,256]{1,0:T(2,128)S(1)}, f32[2,256]{1,0:T(2,128)}, u32[]{:S(2)}) copy-start(f32[2,256]{1,0:T(2,128)} %param.17) | copy-start | bytes 6148
  103.6 748.0 %copy-start.60 = (f32[2,256]{1,0:T(2,128)S(1)}, f32[2,256]{1,0:T(2,128)}, u32[]{:S(2)}) copy-start(f32[2,256]{1,0:T(2,128)} %param.16) | copy-start | bytes 6148
  106.4 864.2 %copy-start.63 = (s32[8]{0:T(128)S(1)}, s32[8]{0:T(128)}, u32[]{:S(2)}) copy-start(s32[8]{0:T(128)} %param.13) | copy-start | bytes 100
  (14 other events, 34.6 us)
Sparse Core Ops, SparseCore 0:
  107.6 743.9 all-reduce.2
where the time goes:
time: 981 us; the launch traced here: 980 us
  waiting for transfers between devices  745 us (76%)
  blocking collectives  115 us (12%)
  starting transfers between devices  50.1 us (5%)
  local copies, waits for them, and re-layouts  35.6 us (4%)
  between operations  15.9 us (2%)
    unnamed x2, waiting for transfers between devices  743 us
    all_gather x1, blocking collectives, shards(): every = lax.all_gather(scaled, ('sx', 'sy'), axis=0, tiled=True)  115 us
    ppermute x6, starting transfers between devices, with_halo(): lax.ppermute(lax.slice_in_dim(block, block.shape[dim] - width, None, axis...  37.8 us
    another operation x54, local copies, waits for them, and re-layouts, stencil(): weight = jnp.tile(coeffs[offset], (1, 1, copies))  22.4 us
  transfers between devices with their start and end apart: 13, of which 4 were waited for; matrix products, arithmetic and copies ran while one was open for 3% of the time, Pallas kernels for 0%

commit v1 on v0

v1 whole, which is shorter than its diff:
```python
import itertools

import jax
import jax.numpy as jnp
from jax import lax
from jax.experimental import pallas as pl
from jax.experimental.pallas import tpu as pltpu
from jax.sharding import Mesh, PartitionSpec as P

CHEB = (0.6, 0.5, 0.3, 0.2)
X, Y, Z = 8, 32, 64
W = 2 * Z
YP = 40
OFF = 4
BLOCKS = 8
SAMPLES = 256
NODES = 512
ROWS = 24
F32 = jnp.float32
VMEM = pl.BlockSpec(memory_space=pltpu.VMEM)
SMEM = pl.BlockSpec(memory_space=pltpu.SMEM)
ANY = pl.BlockSpec(memory_space=pl.ANY)
SIZES = {"x": 4, "zh": 2, "y": 4, "core": 2}


def permute(value, axes, target):
    dims = [SIZES[a] for a in axes]

    def flat(place):
        number = 0
        for coordinate, size in zip(place, dims):
            number = number * size + coordinate
        return number

    pairs = []
    for place in itertools.product(*[range(d) for d in dims]):
        other = target(*place)
        if other is not None:
            pairs.append((flat(place), flat(other)))
    return lax.ppermute(value, axes if len(axes) > 1 else axes[0], pairs)


def even_pair(a, b):
    return (a, b ^ 1)


def odd_pair(a, b):
    if b == 1:
        return (a + 1, 0) if a < 3 else None
    return (a - 1, 1) if a > 0 else None


def half_lanes(shape):
    return lax.broadcasted_iota(jnp.int32, shape, len(shape) - 1) < Z


def swap_halves(value):
    return pltpu.roll(value, Z, axis=value.ndim - 1)


def pack(first, second):
    return jnp.where(half_lanes(first.shape), first, second)


def unpack(row):
    low = half_lanes(row.shape)
    other = swap_halves(row)
    return jnp.where(low, row, other), jnp.where(low, other, row)


def edge_y_kernel(place, noise, classes, even, odd, doubled):
    kinds = (classes[...] + 1).astype(F32)
    doubled[...] = jnp.concatenate([kinds, kinds], axis=-1)
    core = place[1]

    def low(out):
        out[:, 0:3, :] = noise[:, 0:3, :]
        out[:, 3:4, :] = pack(doubled[:, 0:1, :], doubled[:, 1:2, :])

    def high(out):
        out[:, 0:3, :] = noise[:, Y - 3 : Y, :]
        out[:, 3:4, :] = pack(doubled[:, Y - 2 : Y - 1, :], doubled[:, Y - 1 : Y, :])

    @pl.when(core == 0)
    def _():
        high(even)
        low(odd)

    @pl.when(core == 1)
    def _():
        low(even)
        high(odd)


def edge_x_kernel(place, noise, doubled, even_in, odd_in, field, kinds, even, odd):
    core, half = place[1], place[0]
    field[:, 0:8, :] = jnp.zeros((X, 8, W), F32)
    field[:, 32:40, :] = jnp.zeros((X, 8, W), F32)
    kinds[:, 0:8, :] = jnp.zeros((X, 8, W), F32)
    kinds[:, 32:40, :] = jnp.zeros((X, 8, W), F32)
    field[:, OFF : OFF + Y, :] = noise[...]
    kinds[:, OFF : OFF + Y, :] = doubled[...]

    def sides(low, high):
        field[:, 1:4, :] = low[:, 0:3, :]
        first, second = unpack(low[:, 3:4, :])
        kinds[:, 2:3, :] = first
        kinds[:, 3:4, :] = second
        field[:, 36:39, :] = high[:, 0:3, :]
        first, second = unpack(high[:, 3:4, :])
        kinds[:, 36:37, :] = first
        kinds[:, 37:38, :] = second

    @pl.when(core == 0)
    def _():
        sides(odd_in, even_in)

    @pl.when(core == 1)
    def _():
        sides(even_in, odd_in)

    def low(out):
        out[0:3] = field[0:3]
        out[3] = pack(kinds[0], kinds[1])

    def high(out):
        out[0:3] = field[X - 3 : X]
        out[3] = pack(kinds[X - 2], kinds[X - 1])

    @pl.when(half == 0)
    def _():
        high(even)
        low(odd)

    @pl.when(half == 1)
    def _():
        low(even)
        high(odd)


def rows_by_column(block_rows):
    return [block_rows[pl.ds(c, 8, stride=8), :] for c in range(8)]


def split(value):
    high = value.astype(jnp.bfloat16)
    low = (value - high.astype(F32)).astype(jnp.bfloat16)
    return high, low


def smooth_kernel(
    place, node_block, field, kinds, even_in, odd_in, weights_of, matrix, count, owner, drill, gain,
    smooth, payload,
    grown, mask, weights, shifted, level, chosen, matrix_vmem, sem,
):
    copy = pltpu.make_async_copy(matrix, matrix_vmem, sem)
    copy.start()
    half = place[0]

    def sides(low, high):
        grown[0:3] = low[0:3]
        grown[11:14] = high[0:3]
        first, second = unpack(low[3])
        mask[0] = first
        mask[1] = second
        first, second = unpack(high[3])
        mask[10] = first
        mask[11] = second

    @pl.when(half == 0)
    def _():
        sides(odd_in, even_in)

    @pl.when(half == 1)
    def _():
        sides(even_in, odd_in)

    grown[3:11] = field[...]
    mask[2:10] = kinds[...]

    def weigh(x, carry):
        for g in range(YP // 8):
            rows = pl.ds(g * 8, 8)
            kind = mask[x, rows, :]
            index = jnp.maximum(kind.astype(jnp.int32) - 1, 0)
            for o in range(27):
                weights[o, x, rows, :] = jnp.take_along_axis(
                    weights_of[o], index, axis=0, mode="promise_in_bounds"
                )
            mask[x, rows, :] = jnp.minimum(kind, 1.0)
        return carry

    lax.fori_loop(0, 12, weigh, 0)

    lanes = lax.broadcasted_iota(jnp.int32, (YP, W), 1) % Z
    not_first = lanes > 0
    not_last = lanes < Z - 1

    def shift_row(x, value):
        below = jnp.where(not_first, pltpu.roll(value, 1, axis=1), 0.0)
        above = jnp.where(not_last, pltpu.roll(value, W - 1, axis=1), 0.0)
        for c, moved in enumerate((below, value, above)):
            shifted[c, x] = pltpu.roll(moved, 1, axis=0)
            shifted[3 + c, x] = moved
            shifted[6 + c, x] = pltpu.roll(moved, YP - 1, axis=0)

    def apply(first_row, rows, put):
        def one(i, carry):
            x = first_row + i
            for g in range(YP // 8):
                part = pl.ds(g * 8, 8)
                total = None
                for a in range(3):
                    for bc in range(9):
                        term = weights[9 * a + bc, x - 1, part, :] * shifted[bc, x + a - 1, part, :]
                        total = term if total is None else total + term
                put(x, part, total * mask[x - 1, part, :])
            return carry

        lax.fori_loop(0, rows, one, 0)

    def shift_all(source, first_row, rows):
        def one(i, carry):
            shift_row(first_row + i, source[first_row + i])
            return carry

        lax.fori_loop(0, rows, one, 0)

    def put_second(x, part, value):
        level[0, x, part, :] = value

    def put_third(x, part, value):
        level[1, x, part, :] = 2.0 * value - grown[x, part, :]

    def put_fourth(x, part, value):
        second = level[0, x, part, :]
        fourth = 2.0 * value - second
        level[2, x, part, :] = (
            CHEB[0] * grown[x, part, :]
            + CHEB[1] * second
            + CHEB[2] * level[1, x, part, :]
            + CHEB[3] * fourth
        )

    shift_all(grown, 0, 14)
    apply(1, 12, put_second)
    shift_all(level.at[0], 1, 12)
    apply(2, 10, put_third)
    shift_all(level.at[1], 2, 10)
    apply(3, 8, put_fourth)
    for x in range(X):
        for g in range(4):
            smooth[x * 4 + g] = level[2, x + 3, OFF + 8 * g : OFF + 8 * g + 8, :]

    for b in range(BLOCKS):
        chosen[pl.ds(8 * b, 8), :] = smooth[node_block[b]]
    columns = rows_by_column(chosen)
    low = half_lanes((8, W))
    parts = ([], [])
    for j in range(4):
        one, two = columns[2 * j], columns[2 * j + 1]
        parts[0].append(jnp.where(low, one, swap_halves(two)))
        parts[1].append(jnp.where(low, swap_halves(one), two))
    values = [jnp.concatenate(p, axis=1) for p in parts]
    pieces = [split(v) for v in values]
    left = jnp.concatenate([pieces[0][0], pieces[1][0], pieces[0][1], pieces[1][1]], axis=0)
    copy.wait()
    block = lax.broadcasted_iota(jnp.int32, (BLOCKS, SAMPLES), 0)
    sums = [jnp.zeros((BLOCKS, SAMPLES), F32) for _ in range(2)]
    for b in range(BLOCKS):
        product = lax.dot_general(
            left, matrix_vmem[b], (((1,), (1,)), ((), ())), preferred_element_type=F32
        )
        for r in range(2):
            both = product[8 * r : 8 * r + 8] + product[16 + 8 * r : 24 + 8 * r]
            sums[r] = jnp.where(block == b, both, sums[r])
    live = lax.broadcasted_iota(jnp.int32, (BLOCKS, SAMPLES), 1) < count[...]
    for r in range(2):
        payload[8 * r : 8 * r + 8, :] = jnp.where(live, sums[r], 0.0)
    for k in range(2):
        for h in range(2):
            payload[16 + 2 * k + h : 17 + 2 * k + h, 0:W] = drill[k : k + 1, h * W : h * W + W]
            payload[20 + 2 * k + h : 21 + 2 * k + h, 0:W] = gain[k : k + 1, h * W : h * W + W]
    payload[16:24, W : 2 * W] = jnp.broadcast_to(owner[...].astype(F32), (8, W))


def update_kernel(
    place, node_block, wanted, here, there, smooth, matrix, count, drill, gain,
    out, misfit,
    totals, update, matrix_vmem, sem,
):
    copy = pltpu.make_async_copy(matrix, matrix_vmem, sem)
    copy.start()
    targets = BLOCKS + 2

    def add(source):
        def one(n, sums):
            x, z = n // 2, n % 2
            kind = source[x, z, 16:24, W : 2 * W]
            fields = [
                [source[x, z, 8 * r : 8 * r + 8, h * W : h * W + W] for h in range(2)]
                for r in range(2)
            ]
            result = []
            for t in range(targets):
                hit = kind == wanted[t].astype(F32)
                for r in range(2):
                    for h in range(2):
                        result.append(sums[4 * t + 2 * r + h] + jnp.where(hit, fields[r][h], 0.0))
            return tuple(result)

        return one

    sums = tuple(jnp.zeros((8, W), F32) for _ in range(4 * targets))
    sums = lax.fori_loop(0, 32, add(here), sums)
    sums = lax.fori_loop(0, 32, add(there), sums)
    for t in range(targets):
        for r in range(2):
            for h in range(2):
                totals[r, t : t + 1, h * W : h * W + W] = jnp.sum(
                    sums[4 * t + 2 * r + h], axis=0, keepdims=True
                )
    half, core = place[0], place[1]
    for k in range(2):
        for r in range(2):
            misfit[k, r : r + 1, :] = drill[k : k + 1, :] - totals[r, BLOCKS + k : BLOCKS + k + 1, :]

    live = lax.broadcasted_iota(jnp.int32, (BLOCKS, SAMPLES), 1) < count[...]
    for b in range(BLOCKS):
        k = wanted[b]
        tile = k // 2
        sx, sy = tile // 8, tile % 8
        where_x = (sx // 2) * 4 + sy // 2
        where_z = (sx % 2) ^ half
        row = k % 2

        def fetch(source):
            held = source[where_x, where_z, 16:24, 0:W]
            for h in range(2):
                for which in range(2):
                    base = 4 * which + h
                    totals[2 + which, b : b + 1, h * W : h * W + W] = jnp.where(
                        row == 0, held[base : base + 1], held[base + 2 : base + 3]
                    )

        @pl.when(sy % 2 == core)
        def _():
            fetch(here)

        @pl.when(sy % 2 != core)
        def _():
            fetch(there)

    picked = [
        jnp.where(live, totals[3, 0:BLOCKS, :] * (totals[2, 0:BLOCKS, :] - totals[r, 0:BLOCKS, :]), 0.0)
        for r in range(2)
    ]
    pieces = [split(v) for v in picked]
    left = jnp.concatenate([pieces[0][0], pieces[1][0], pieces[0][1], pieces[1][1]], axis=0)
    copy.wait()
    block = lax.broadcasted_iota(jnp.int32, (BLOCKS, NODES), 0)
    sums = [jnp.zeros((BLOCKS, NODES), F32) for _ in range(2)]
    for b in range(BLOCKS):
        product = jnp.dot(left, matrix_vmem[b], preferred_element_type=F32)
        for r in range(2):
            both = product[8 * r : 8 * r + 8] + product[16 + 8 * r : 24 + 8 * r]
            sums[r] = jnp.where(block == b, both, sums[r])
    low = half_lanes((8, W))
    for j in range(4):
        one, two = sums[0][:, j * W : j * W + W], sums[1][:, j * W : j * W + W]
        update[pl.ds(2 * j, 8, stride=8), :] = jnp.where(low, one, swap_halves(two))
        update[pl.ds(2 * j + 1, 8, stride=8), :] = jnp.where(low, swap_halves(one), two)
    out[...] = smooth[...]
    for b in range(BLOCKS):
        n = node_block[b]
        out[n] = out[n] + update[8 * b : 8 * b + 8, :]


def shape(*dims, dtype=F32):
    return jax.ShapeDtypeStruct(dims, dtype)


def shards(
    noise, classes, table, obs_matrix, node_block, sample_block, sample_count, drill_data, obs_gain
):
    place = jnp.stack([lax.axis_index("zh"), lax.axis_index("core")]).astype(jnp.int32)
    tile = lax.axis_index(("x", "zh", "y", "core"))
    wanted = jnp.concatenate([sample_block, 2 * tile + jnp.arange(2, dtype=jnp.int32)])
    wanted = wanted.astype(jnp.int32)
    weights_of = jnp.broadcast_to(table.T[:, :, None], (27, 8, W))
    count = sample_count[:, None]
    owner = sample_block[:, None]

    even, odd, doubled = pl.pallas_call(
        edge_y_kernel,
        out_shape=(shape(X, 4, W), shape(X, 4, W), shape(X, Y, W)),
        in_specs=[SMEM, VMEM, VMEM],
        out_specs=(VMEM, VMEM, VMEM),
        name="edge_y",
    )(place, noise, classes)
    odd = permute(odd, ("y", "core"), odd_pair)
    even = permute(even, ("y", "core"), even_pair)
    field, kinds, even, odd = pl.pallas_call(
        edge_x_kernel,
        out_shape=(shape(X, YP, W), shape(X, YP, W), shape(4, YP, W), shape(4, YP, W)),
        in_specs=[SMEM] + [VMEM] * 4,
        out_specs=(VMEM,) * 4,
        name="edge_x",
    )(place, noise, doubled, even, odd)
    odd = permute(odd, ("x", "zh"), odd_pair)
    even = permute(even, ("x", "zh"), even_pair)
    smooth, payload = pl.pallas_call(
        smooth_kernel,
        out_shape=(shape(32, 8, W), shape(ROWS, SAMPLES)),
        in_specs=[SMEM, SMEM] + [VMEM] * 5 + [ANY] + [VMEM] * 4,
        out_specs=(VMEM, VMEM),
        scratch_shapes=[
            pltpu.VMEM((14, YP, W), F32),
            pltpu.VMEM((12, YP, W), F32),
            pltpu.VMEM((27, 12, YP, W), F32),
            pltpu.VMEM((9, 14, YP, W), F32),
            pltpu.VMEM((3, 14, YP, W), F32),
            pltpu.VMEM((64, W), F32),
            pltpu.VMEM((BLOCKS, SAMPLES, NODES), jnp.bfloat16),
            pltpu.SemaphoreType.DMA,
        ],
        compiler_params=pltpu.CompilerParams(vmem_limit_bytes=32 * 1024 * 1024),
        name="smooth",
    )(
        place, node_block, field, kinds, even, odd, weights_of, obs_matrix, count, owner,
        drill_data, obs_gain,
    )
    other = permute(payload, ("zh",), lambda z: (z ^ 1,))
    pair = jnp.stack([payload, other])
    here = lax.all_to_all(
        jnp.broadcast_to(pair[None], (16, 2, ROWS, SAMPLES)), ("x", "y"), 0, 0, tiled=True
    )
    there = permute(here, ("core",), lambda c: (c ^ 1,))
    out, misfit = pl.pallas_call(
        update_kernel,
        out_shape=(shape(32, 8, W), shape(2, 2, SAMPLES)),
        in_specs=[SMEM, SMEM, SMEM, VMEM, VMEM, VMEM, ANY, VMEM, VMEM, VMEM],
        out_specs=(VMEM, VMEM),
        scratch_shapes=[
            pltpu.VMEM((4, 16, SAMPLES), F32),
            pltpu.VMEM((64, W), F32),
            pltpu.VMEM((BLOCKS, SAMPLES, NODES), jnp.bfloat16),
            pltpu.SemaphoreType.DMA,
        ],
        compiler_params=pltpu.CompilerParams(vmem_limit_bytes=32 * 1024 * 1024),
        name="update",
    )(
        place, node_block, wanted, here, there, smooth, obs_matrix, count, drill_data, obs_gain
    )
    return out.reshape(X, Y, W), misfit


def solution(mesh):
    fine = Mesh(
        mesh.devices.reshape(4, 4, 2, 4, 2), ("real", "x", "zh", "y", "core")
    )
    sx, sy = ("x", "zh"), ("y", "core")
    both = sx + sy
    in_specs = (
        P(sx, sy, "real"),
        P(sx, sy, None),
        P(),
        P(both, None, None),
        P(both),
        P(both),
        P(both),
        P(both, None),
        P(both, None),
    )
    out_specs = (P(sx, sy, "real"), P(both, "real", None))
    return jax.shard_map(shards, mesh=fine, in_specs=in_specs, out_specs=out_specs, check_vma=False)
```

time: 981 us -> 79.4 us (0.08)
  waiting for transfers between devices: 745 us -> 6.72 us
  blocking collectives: 115 us -> 22.3 us
  local copies, waits for them, and re-layouts: 35.6 us -> 9.08 us
  starting transfers between devices: 50.1 us -> 23.6 us
  Pallas kernels: 0 us -> 15.8 us
  between operations: 15.9 us -> 0.75 us
    unnamed x2 -> x0, waiting for transfers between devices: 743 us -> none
    all_gather x1 -> x0, blocking collectives: 115 us -> none  [shards(): every = lax.all_gather(scaled, ('sx', 'sy'), axis=0, tiled=True)]
    ppermute x12 -> x6, starting transfers between devices: 50.1 us -> 23.6 us  [permute(): return lax.ppermute(value, axes if len(axes) > 1 else axes[0], pairs)]
    another operation x54 -> x0, local copies, waits for them, and re-layouts: 22.4 us -> none  [stencil(): weight = jnp.tile(coeffs[offset], (1, 1, copies))]
    all_to_all x0 -> x1, blocking collectives: none -> 22.3 us  [shards(): lax.all_to_all(jnp.broadcast_to(pair[None], (16, 2, ROWS, SAMPLES)), ('x'...]
    pallas_call x0 -> x4, Pallas kernels: none -> 15.8 us  [the longest x1 7.47 us: shards(): pl.pallas_call(smooth_kernel, out_shape=(shape(32, 8, W), shape(ROWS, SAM...]
  transfers between devices with their start and end apart: 13 -> 6, of which waited for: 4 -> 4; matrix products, arithmetic and copies ran while one was open for 3% -> 3% of each run, Pallas kernels for 0% -> 0%
where the time goes in v1:
time: 79.4 us; the launch traced here: 78.9 us
  starting transfers between devices  23.6 us (30%)
  blocking collectives  22.3 us (28%)
  Pallas kernels  15.8 us (20%)
  local copies, waits for them, and re-layouts  9.08 us (11%)
  waiting for transfers between devices  6.72 us (8%)
    ppermute x6, starting transfers between devices, permute(): return lax.ppermute(value, axes if len(axes) > 1 else axes[0], pairs)  23.6 us
    all_to_all x1, blocking collectives, shards(): lax.all_to_all(jnp.broadcast_to(pair[None], (16, 2, ROWS, SAMPLES)), ('x'...  22.3 us
    pallas_call x1, Pallas kernels, shards(): pl.pallas_call(smooth_kernel, out_shape=(shape(32, 8, W), shape(ROWS, SAM...  7.47 us
    ppermute x6, waiting for transfers between devices, permute(): return lax.ppermute(value, axes if len(axes) > 1 else axes[0], pairs)  6.72 us
    unnamed x30, local copies, waits for them, and re-layouts  6.69 us
    pallas_call x1, Pallas kernels, shards(): pl.pallas_call(update_kernel, out_shape=(shape(32, 8, W), shape(2, 2, SAM...  4.65 us
    pallas_call x1, Pallas kernels, shards(): pl.pallas_call(edge_x_kernel, out_shape=(shape(X, YP, W), shape(X, YP, W)...  1.91 us
    pallas_call x1, Pallas kernels, shards(): pl.pallas_call(edge_y_kernel, out_shape=(shape(X, 4, W), shape(X, 4, W),...  1.76 us
  transfers between devices with their start and end apart: 6, of which 4 were waited for; matrix products, arithmetic and copies ran while one was open for 3% of the time, Pallas kernels for 0%

profile of v1, /device:TPU:1, one launch (start us, length us, event | category | flops | bytes accessed | tf_op | source)
XLA Modules:
  0.0 78.9 jit_solution(8235212571386591774)
XLA Ops:
  0.6 0.6 pad_add_fusion.place
  1.2 1.8 %edge_y.1 = (f32[8,4,128]{2,1,0:T(4,128)}, f32[8,4,128]{2,1,0:T(4,128)}, f32[8,32,128]{2,1,0:T(8,128)}) custom-call(s32[2]{0:T(128)} %pad_add_fusion.place, f32[8,32,128]{2,1,0:T(8,128)} %noise.3, s32[8,32,64]{2,1,0:T(8,128)} %classes.1), custom_call_target="tpu_custom_call" | custom-call | tf_op jit(solution)/shard_map/edge_y/pallas_call | solution.py:394
  3.0 3.2 %collective-permute-start = (f32[8,4,128]{2,1,0:T(4,128)}, f32[8,4,128]{2,1,0:T(4,128)S(1)}, u32[]{:S(2)}, u32[]{:S(2)}) collective-permute-start(f32[8,4,128]{2,1,0:T(4,128)} %get-tuple-element.14), channel_id=1, source_target_pairs={{0,1},{1,0},{2,3},{3,2},{4,5},{5,4},{6,7},{7,6},{8,9},{9,8},{10,11... | collective-permute-start | bytes 49160 | tf_op jit(solution)/shard_map/ppermute | solution.py:40
  6.2 1.9 %collective-permute-start.1 = (f32[8,4,128]{2,1,0:T(4,128)}, f32[8,4,128]{2,1,0:T(4,128)S(1)}, u32[]{:S(2)}, u32[]{:S(2)}) collective-permute-start(f32[8,4,128]{2,1,0:T(4,128)} %get-tuple-element.15), channel_id=1, source_target_pairs={{1,2},{2,1},{3,4},{4,3},{5,6},{6,5},{9,10},{10,9},{11,12},{12,11},... | collective-permute-start | bytes 49160 | tf_op jit(solution)/shard_map/ppermute | solution.py:40
  8.2 0.0 collective-permute-done.even_in
  8.2 0.0 copy-start.12
  8.2 3.3 %collective-permute-done.1.odd_in = f32[8,4,128]{2,1,0:T(4,128)S(1)} collective-permute-done((f32[8,4,128]{2,1,0:T(4,128)}, f32[8,4,128]{2,1,0:T(4,128)S(1)}, u32[]{:S(2)}, u32[]{:S(2)}) %collective-permute-start.1) | collective-permute-done | bytes 16416 | tf_op jit(solution)/shard_map/ppermute | solution.py:40
  11.5 0.0 copy-start.13
  11.5 0.0 copy-done.12
  11.5 0.6 copy-done.13
  12.1 1.9 %edge_x.1 = (f32[8,40,128]{2,1,0:T(8,128)}, f32[8,40,128]{2,1,0:T(8,128)}, f32[4,40,128]{2,1,0:T(8,128)}, f32[4,40,128]{2,1,0:T(8,128)}) custom-call(s32[2]{0:T(128)} %pad_add_fusion.place, f32[8,32,128]{2,1,0:T(8,128)} %noise.3, f32[8,32,128]{2,1,0:T(8,128)} %get-tuple-element.13.doubled, f32[8,4,128]{2,1,0:T(4,128)} %copy-done.12, f32[8,4,128]{2,1,0:T(4,128)} %copy-done.13), custom_call_target="tpu_custom_call" | custom-call | tf_op jit(solution)/shard_map/edge_x/pallas_call | solution.py:403
  14.0 5.2 %collective-permute-start.2 = (f32[4,40,128]{2,1,0:T(8,128)}, f32[4,40,128]{2,1,0:T(8,128)S(1)}, u32[]{:S(2)}, u32[]{:S(2)}) collective-permute-start(f32[4,40,128]{2,1,0:T(8,128)} %get-tuple-element.18), channel_id=1, source_target_pairs={{0,8},{8,0},{16,24},{24,16},{32,40},{40,32},{48,56},{56,48},{1,9},... | collective-permute-start | bytes 245768 | tf_op jit(solution)/shard_map/ppermute | solution.py:40
  19.2 0.7 collective-permute-start.3
  19.8 0.7 copy.12.count
  20.6 0.7 copy.13.owner
  21.3 0.8 copy.11
  22.1 0.2 collective-permute-done.2.even_in
  22.3 0.0 collective-permute-done.3.odd_in
  22.3 0.1 broadcast_in_dim.8.weights_of
  22.4 0.0 copy-start
  22.4 1.6 %copy-done = bf16[8,256,512]{2,1,0:T(8,128)(2,1)S(1)} copy-done((bf16[8,256,512]{2,1,0:T(8,128)(2,1)S(1)}, bf16[8,256,512]{2,1,0:T(8,128)(2,1)}, u32[]{:S(2)}) %copy-start) | copy-done | bytes 2097176
  24.0 0.0 copy-start.2
  24.0 0.9 %copy-done.2 = f32[8,40,128]{2,1,0:T(8,128)S(1)} copy-done((f32[8,40,128]{2,1,0:T(8,128)S(1)}, f32[8,40,128]{2,1,0:T(8,128)}, u32[]{:S(2)}) %copy-start.2) | copy-done | bytes 163864
  24.9 0.0 copy-start.3
  24.9 0.9 %copy-done.3 = f32[8,40,128]{2,1,0:T(8,128)S(1)} copy-done((f32[8,40,128]{2,1,0:T(8,128)S(1)}, f32[8,40,128]{2,1,0:T(8,128)}, u32[]{:S(2)}) %copy-start.3) | copy-done | bytes 163864
  25.8 0.0 copy-start.4
  25.8 0.7 copy-done.4
  26.5 0.0 copy-start.6
  26.5 0.7 copy-done.6
  27.2 0.0 copy-start.8
  27.2 0.6 copy-done.8
  27.8 0.0 copy-start.10
  27.8 0.7 copy-done.10
  28.5 0.0 copy-start.14
  28.5 0.0 copy-start.1
  28.5 0.0 copy-start.5
  28.5 0.0 copy-start.7
  28.5 0.0 copy-start.9
  28.5 0.0 copy-start.11
  28.5 7.5 %smooth.1 = (f32[32,8,128]{2,1,0:T(8,128)S(1)}, f32[24,256]{1,0:T(8,128)S(1)}) custom-call(s32[2]{0:T(128)S(1)} %copy-done.8, s32[8]{0:T(128)S(1)} %copy-done.10, f32[8,40,128]{2,1,0:T(8,128)S(1)} %copy-done.2, f32[8,40,128]{2,1,0:T(8,128)S(1)} %copy-done.3, f32[4,40,128]{2,1,0:T(8,128)S(1)} %collective-permute-done.2.even_in, ...), custom_call_target="tpu_custom_call" | custom-call | tf_op jit(solution)/shard_map/smooth/pallas_call | solution.py:412
  36.0 7.5 %collective-permute-start.4 = (f32[24,256]{1,0:T(8,128)S(1)}, f32[24,256]{1,0:T(8,128)S(1)}, u32[]{:S(2)}, u32[]{:S(2)}) collective-permute-start(f32[24,256]{1,0:T(8,128)S(1)} %get-tuple-element.20), channel_id=1, source_target_pairs={{0,8},{8,0},{1,9},{9,1},{2,10},{10,2},{3,11},{11,3},{4,12},{12,4},... | collective-permute-start | bytes 73736 | tf_op jit(solution)/shard_map/ppermute | solution.py:40
  43.5 1.2 %collective-permute-done.4 = f32[24,256]{1,0:T(8,128)S(1)} collective-permute-done((f32[24,256]{1,0:T(8,128)S(1)}, f32[24,256]{1,0:T(8,128)S(1)}, u32[]{:S(2)}, u32[]{:S(2)}) %collective-permute-start.4) | collective-permute-done | bytes 24608 | tf_op jit(solution)/shard_map/ppermute | solution.py:40
  44.7 0.1 broadcast_in_dim.21
  44.8 22.3 %all_to_all.5.here = f32[16,2,24,256]{3,2,1,0:T(8,128)S(1)} all-to-all(f32[16,2,24,256]{3,2,1,0:T(8,128)S(1)} %broadcast_in_dim.21), channel_id=1, replica_groups=mesh['real'=4,'x'=4,'zh'=2,'y'=4,'core'=2] {'x','y'}, dimensions={0} | all-to-all | bytes 1572864 | tf_op jit(solution)/shard_map/all_to_all | solution.py:435
  67.0 5.2 %collective-permute-start.5 = (f32[16,2,24,256]{3,2,1,0:T(8,128)S(1)}, f32[16,2,24,256]{3,2,1,0:T(8,128)}, u32[]{:S(2)}, u32[]{:S(2)}) collective-permute-start(f32[16,2,24,256]{3,2,1,0:T(8,128)S(1)} %all_to_all.5.here), channel_id=1, source_target_pairs={{0,1},{1,0},{2,3},{3,2},{4,5},{5,4},{6,7},{7,6},{8,9},{9,8},{10,11... | collective-permute-start | bytes 2359304 | tf_op jit(solution)/shard_map/ppermute | solution.py:40
  72.2 0.0 copy-done.14
  72.2 0.1 pad_add_fusion.1.wanted
  72.3 2.0 %collective-permute-done.5.there = f32[16,2,24,256]{3,2,1,0:T(8,128)} collective-permute-done((f32[16,2,24,256]{3,2,1,0:T(8,128)S(1)}, f32[16,2,24,256]{3,2,1,0:T(8,128)}, u32[]{:S(2)}, u32[]{:S(2)}) %collective-permute-start.5) | collective-permute-done | bytes 786464 | tf_op jit(solution)/shard_map/ppermute | solution.py:40
  74.2 0.0 copy-done.1
  74.2 0.0 copy-done.5
  74.2 0.0 copy-done.7
  74.2 0.0 copy-done.9
  74.3 0.0 copy-done.11
  74.3 4.7 %update.1 = (f32[32,8,128]{2,1,0:T(8,128)}, f32[2,2,256]{2,1,0:T(2,128)}) custom-call(s32[2]{0:T(128)S(1)} %copy-done.9, s32[8]{0:T(128)S(1)} %copy-done.11, s32[10]{0:T(128)S(1)} %pad_add_fusion.1.wanted, f32[16,2,24,256]{3,2,1,0:T(8,128)S(1)} %all_to_all.5.here, f32[16,2,24,256]{3,2,1,0:T(8,128)} %collective-permute-done.5.there, ...), custom_call_target="tpu_custom_call" | custom-call | tf_op jit(solution)/shard_map/update/pallas_call | solution.py:439
  (2 shorter events, 0.0 us)
Async XLA Ops:
  3.0 5.2 %collective-permute-start = (f32[8,4,128]{2,1,0:T(4,128)}, f32[8,4,128]{2,1,0:T(4,128)S(1)}, u32[]{:S(2)}, u32[]{:S(2)}) collective-permute-start(f32[8,4,128]{2,1,0:T(4,128)} %get-tuple-element.14), channel_id=1, source_target_pairs={{0,1},{1,0},{2,3},{3,2},{4,5},{5,4},{6,7},{7,6},{8,9},{9,8},{10,11... | collective-permute-start | bytes 49160 | tf_op jit(solution)/shard_map/ppermute | solution.py:40
  6.2 5.3 %collective-permute-start.1 = (f32[8,4,128]{2,1,0:T(4,128)}, f32[8,4,128]{2,1,0:T(4,128)S(1)}, u32[]{:S(2)}, u32[]{:S(2)}) collective-permute-start(f32[8,4,128]{2,1,0:T(4,128)} %get-tuple-element.15), channel_id=1, source_target_pairs={{1,2},{2,1},{3,4},{4,3},{5,6},{6,5},{9,10},{10,9},{11,12},{12,11},... | collective-permute-start | bytes 49160 | tf_op jit(solution)/shard_map/ppermute | solution.py:40
  8.2 3.3 %copy-start.12 = (f32[8,4,128]{2,1,0:T(4,128)}, f32[8,4,128]{2,1,0:T(4,128)S(1)}, u32[]{:S(2)}) copy-start(f32[8,4,128]{2,1,0:T(4,128)S(1)} %collective-permute-done.even_in) | copy-start | bytes 49156
  11.5 0.6 copy-start.13
  14.0 8.3 %collective-permute-start.2 = (f32[4,40,128]{2,1,0:T(8,128)}, f32[4,40,128]{2,1,0:T(8,128)S(1)}, u32[]{:S(2)}, u32[]{:S(2)}) collective-permute-start(f32[4,40,128]{2,1,0:T(8,128)} %get-tuple-element.18), channel_id=1, source_target_pairs={{0,8},{8,0},{16,24},{24,16},{32,40},{40,32},{48,56},{56,48},{1,9},... | collective-permute-start | bytes 245768 | tf_op jit(solution)/shard_map/ppermute | solution.py:40
  19.2 3.1 %collective-permute-start.3 = (f32[4,40,128]{2,1,0:T(8,128)}, f32[4,40,128]{2,1,0:T(8,128)S(1)}, u32[]{:S(2)}, u32[]{:S(2)}) collective-permute-start(f32[4,40,128]{2,1,0:T(8,128)} %get-tuple-element.19), channel_id=1, source_target_pairs={{8,16},{16,8},{24,32},{32,24},{40,48},{48,40},{9,17},{17,9},{25,33... | collective-permute-start | bytes 245768 | tf_op jit(solution)/shard_map/ppermute | solution.py:40
  22.4 1.6 %copy-start = (bf16[8,256,512]{2,1,0:T(8,128)(2,1)S(1)}, bf16[8,256,512]{2,1,0:T(8,128)(2,1)}, u32[]{:S(2)}) copy-start(bf16[8,256,512]{2,1,0:T(8,128)(2,1)} %matrix.3) | copy-start | bytes 6291460
  24.0 0.9 %copy-start.2 = (f32[8,40,128]{2,1,0:T(8,128)S(1)}, f32[8,40,128]{2,1,0:T(8,128)}, u32[]{:S(2)}) copy-start(f32[8,40,128]{2,1,0:T(8,128)} %get-tuple-element.16.field) | copy-start | bytes 491524
  24.9 0.9 %copy-start.3 = (f32[8,40,128]{2,1,0:T(8,128)S(1)}, f32[8,40,128]{2,1,0:T(8,128)}, u32[]{:S(2)}) copy-start(f32[8,40,128]{2,1,0:T(8,128)} %get-tuple-element.17.kinds) | copy-start | bytes 491524
  25.8 0.7 copy-start.4
  26.5 0.7 copy-start.6
  27.2 0.6 copy-start.8
  27.8 0.7 copy-start.10
  28.5 43.7 %copy-start.14 = (s32[8]{0:T(128)S(1)}, s32[8]{0:T(128)}, u32[]{:S(2)}) copy-start(s32[8]{0:T(128)} %param.14) | copy-start | bytes 100
  28.5 45.8 %copy-start.1 = (bf16[8,256,512]{2,1,0:T(8,128)(2,1)S(1)}, bf16[8,256,512]{2,1,0:T(8,128)(2,1)}, u32[]{:S(2)}) copy-start(bf16[8,256,512]{2,1,0:T(8,128)(2,1)} %matrix.3) | copy-start | bytes 6291460
  28.5 45.8 %copy-start.5 = (f32[2,256]{1,0:T(2,128)S(1)}, f32[2,256]{1,0:T(2,128)}, u32[]{:S(2)}) copy-start(f32[2,256]{1,0:T(2,128)} %drill.3) | copy-start | bytes 6148
  28.5 45.8 %copy-start.7 = (f32[2,256]{1,0:T(2,128)S(1)}, f32[2,256]{1,0:T(2,128)}, u32[]{:S(2)}) copy-start(f32[2,256]{1,0:T(2,128)} %gain.3) | copy-start | bytes 6148
  28.5 45.8 %copy-start.9 = (s32[2]{0:T(128)S(1)}, s32[2]{0:T(128)}, u32[]{:S(2)}) copy-start(s32[2]{0:T(128)} %pad_add_fusion.place) | copy-start | bytes 28
  28.5 45.8 %copy-start.11 = (s32[8]{0:T(128)S(1)}, s32[8]{0:T(128)}, u32[]{:S(2)}) copy-start(s32[8]{0:T(128)} %node_block.3) | copy-start | bytes 100
  36.0 8.7 %collective-permute-start.4 = (f32[24,256]{1,0:T(8,128)S(1)}, f32[24,256]{1,0:T(8,128)S(1)}, u32[]{:S(2)}, u32[]{:S(2)}) collective-permute-start(f32[24,256]{1,0:T(8,128)S(1)} %get-tuple-element.20), channel_id=1, source_target_pairs={{0,8},{8,0},{1,9},{9,1},{2,10},{10,2},{3,11},{11,3},{4,12},{12,4},... | collective-permute-start | bytes 73736 | tf_op jit(solution)/shard_map/ppermute | solution.py:40
  67.0 7.2 %collective-permute-start.5 = (f32[16,2,24,256]{3,2,1,0:T(8,128)S(1)}, f32[16,2,24,256]{3,2,1,0:T(8,128)}, u32[]{:S(2)}, u32[]{:S(2)}) collective-permute-start(f32[16,2,24,256]{3,2,1,0:T(8,128)S(1)} %all_to_all.5.here), channel_id=1, source_target_pairs={{0,1},{1,0},{2,3},{3,2},{4,5},{5,4},{6,7},{7,6},{8,9},{9,8},{10,11... | collective-permute-start | bytes 2359304 | tf_op jit(solution)/shard_map/ppermute | solution.py:40

commit v2 on v1

v2 whole, which is shorter than its diff:
```python
import itertools

import jax
import jax.numpy as jnp
from jax import lax
from jax.experimental import pallas as pl
from jax.experimental.pallas import tpu as pltpu
from jax.sharding import Mesh, PartitionSpec as P

CHEB = (0.6, 0.5, 0.3, 0.2)
X, Y, Z = 8, 32, 64
W = 2 * Z
YP = 40
OFF = 4
BLOCKS = 8
SAMPLES = 256
NODES = 512
ROWS = 24
F32 = jnp.float32
VMEM = pl.BlockSpec(memory_space=pltpu.VMEM)
SMEM = pl.BlockSpec(memory_space=pltpu.SMEM)
HBM = pl.BlockSpec(memory_space=pltpu.HBM)
SIZES = {"x": 4, "zh": 2, "y": 4, "core": 2}


def permute(value, axes, target):
    dims = [SIZES[a] for a in axes]

    def flat(place):
        number = 0
        for coordinate, size in zip(place, dims):
            number = number * size + coordinate
        return number

    pairs = []
    for place in itertools.product(*[range(d) for d in dims]):
        other = target(*place)
        if other is not None:
            pairs.append((flat(place), flat(other)))
    return lax.ppermute(value, axes if len(axes) > 1 else axes[0], pairs)


def even_pair(a, b):
    return (a, b ^ 1)


def odd_pair(a, b):
    if b == 1:
        return (a + 1, 0) if a < 3 else None
    return (a - 1, 1) if a > 0 else None


def half_lanes(shape):
    return lax.broadcasted_iota(jnp.int32, shape, len(shape) - 1) < Z


def swap_halves(value):
    return pltpu.roll(value, Z, axis=value.ndim - 1)


def pack(first, second):
    return jnp.where(half_lanes(first.shape), first, second)


def unpack(row):
    low = half_lanes(row.shape)
    other = swap_halves(row)
    return jnp.where(low, row, other), jnp.where(low, other, row)


def edge_y_kernel(place, noise, classes, even, odd, doubled):
    kinds = (classes[...] + 1).astype(F32)
    doubled[...] = jnp.concatenate([kinds, kinds], axis=-1)
    core = place[1]

    def low(out):
        out[:, 0:3, :] = noise[:, 0:3, :]
        out[:, 3:4, :] = pack(doubled[:, 0:1, :], doubled[:, 1:2, :])

    def high(out):
        out[:, 0:3, :] = noise[:, Y - 3 : Y, :]
        out[:, 3:4, :] = pack(doubled[:, Y - 2 : Y - 1, :], doubled[:, Y - 1 : Y, :])

    @pl.when(core == 0)
    def _():
        high(even)
        low(odd)

    @pl.when(core == 1)
    def _():
        low(even)
        high(odd)


def edge_x_kernel(place, noise, doubled, even_in, odd_in, field, kinds, even, odd):
    core, half = place[1], place[0]
    field[:, 0:8, :] = jnp.zeros((X, 8, W), F32)
    field[:, 32:40, :] = jnp.zeros((X, 8, W), F32)
    kinds[:, 0:8, :] = jnp.zeros((X, 8, W), F32)
    kinds[:, 32:40, :] = jnp.zeros((X, 8, W), F32)
    field[:, OFF : OFF + Y, :] = noise[...]
    kinds[:, OFF : OFF + Y, :] = doubled[...]

    def sides(low, high):
        field[:, 1:4, :] = low[:, 0:3, :]
        first, second = unpack(low[:, 3:4, :])
        kinds[:, 2:3, :] = first
        kinds[:, 3:4, :] = second
        field[:, 36:39, :] = high[:, 0:3, :]
        first, second = unpack(high[:, 3:4, :])
        kinds[:, 36:37, :] = first
        kinds[:, 37:38, :] = second

    @pl.when(core == 0)
    def _():
        sides(odd_in, even_in)

    @pl.when(core == 1)
    def _():
        sides(even_in, odd_in)

    def low(out):
        out[0:3] = field[0:3]
        out[3] = pack(kinds[0], kinds[1])

    def high(out):
        out[0:3] = field[X - 3 : X]
        out[3] = pack(kinds[X - 2], kinds[X - 1])

    @pl.when(half == 0)
    def _():
        high(even)
        low(odd)

    @pl.when(half == 1)
    def _():
        low(even)
        high(odd)


def rows_by_column(block_rows):
    return [block_rows[pl.ds(c, 8, stride=8), :] for c in range(8)]


def split(value):
    high = value.astype(jnp.bfloat16)
    low = (value - high.astype(F32)).astype(jnp.bfloat16)
    return high, low


def weigh(kinds, table, put):
    for b in range(3):
        moved = kinds if b == 1 else pltpu.roll(kinds, (b - 1) % YP, axis=0)
        index = jnp.maximum(moved.astype(jnp.int32) - 1, 0)
        for g in range(YP // 8):
            part = index[8 * g : 8 * g + 8]
            for a in range(3):
                for c in range(3):
                    o = 9 * a + 3 * b + c
                    put(
                        o,
                        pl.ds(8 * g, 8),
                        jnp.take_along_axis(table[o], part, axis=0, mode="promise_in_bounds"),
                    )


def spread_table(table, out):
    held = table[...]
    for o in range(27):
        out[o] = jnp.broadcast_to(held[:, o : o + 1], (8, W))


def lean(row):
    lanes = lax.broadcasted_iota(jnp.int32, (YP, W), 1) % Z
    below = jnp.where(lanes > 0, pltpu.roll(row, 1, axis=1), 0.0)
    above = jnp.where(lanes < Z - 1, pltpu.roll(row, W - 1, axis=1), 0.0)
    return below, row, above


def operate(weight, moved, inside):
    sums = []
    for b in range(3):
        total = None
        for a in range(3):
            for c in range(3):
                term = weight(9 * a + 3 * b + c) * moved(a, c)
                total = term if total is None else total + term
        sums.append(total)
    result = pltpu.roll(sums[0], 1, axis=0) + sums[1] + pltpu.roll(sums[2], YP - 1, axis=0)
    return result * inside


def interior_kernel(
    field, kinds, table, matrix, drill, gain,
    weights, first, second, third, smooth, tables, held_matrix, held_rows,
    sems,
):
    copies = [
        pltpu.make_async_copy(matrix, held_matrix, sems.at[0]),
        pltpu.make_async_copy(drill, held_rows.at[0], sems.at[1]),
        pltpu.make_async_copy(gain, held_rows.at[1], sems.at[2]),
    ]
    for copy in copies:
        copy.start()
    spread_table(table, tables)
    for x in range(X):
        def put(o, rows, value, x=x):
            weights[o, x, rows, :] = value

        weigh(kinds[x], tables, put)
        for c, value in enumerate(lean(field[x])):
            first[c, x] = value

    def step(source, start, x):
        return operate(
            lambda o: weights[o, x],
            lambda a, c: source[c, x + a - 1 - start],
            jnp.minimum(kinds[x], 1.0),
        )

    for x in range(1, 7):
        for c, value in enumerate(lean(step(first, 0, x))):
            second[c, x - 1] = value
    for x in range(2, 6):
        value = 2.0 * step(second, 1, x) - first[1, x]
        for c, value in enumerate(lean(value)):
            third[c, x - 2] = value
    for x in range(3, 5):
        fourth = 2.0 * step(third, 2, x) - second[1, x - 1]
        result = (
            CHEB[0] * first[1, x] + CHEB[1] * second[1, x - 1] + CHEB[2] * third[1, x - 2] + CHEB[3] * fourth
        )
        for g in range(4):
            smooth[4 * (x - 3) + g] = result[OFF + 8 * g : OFF + 8 * g + 8]
    for copy in copies:
        copy.wait()


def finish_kernel(
    place, node_block, count, owner, kinds, even_in, odd_in,
    weights, first, second, third, middle, tables, matrix, rows,
    smooth, payload,
    halo, halo_kinds, halo_weights, edge_first, edge_second, edge_third, chosen,
):
    half = place[0]

    def sides(low, high):
        halo[0:3] = low[0:3]
        halo[3:6] = high[0:3]
        one, two = unpack(low[3])
        halo_kinds[0], halo_kinds[1] = one, two
        one, two = unpack(high[3])
        halo_kinds[2], halo_kinds[3] = one, two

    @pl.when(half == 0)
    def _():
        sides(odd_in, even_in)

    @pl.when(half == 1)
    def _():
        sides(even_in, odd_in)

    smooth[12:20] = middle[...]
    for i in range(4):
        def put(o, part, value, i=i):
            halo_weights[o, i, part, :] = value

        weigh(halo_kinds[i], tables, put)
    for i in range(6):
        for c, value in enumerate(lean(halo[i])):
            edge_first[c, i] = value

    def weight(x):
        if 0 <= x < X:
            return (lambda o: weights[o, x]), jnp.minimum(kinds[x], 1.0)
        i = x + 2 if x < 0 else x - 6
        return (lambda o: halo_weights[o, i]), jnp.minimum(halo_kinds[i], 1.0)

    def at_first(x, c):
        if 0 <= x < X:
            return first[c, x]
        return edge_first[c, x + 3 if x < 0 else x - 5]

    def at_second(x, c):
        if 1 <= x < 7:
            return second[c, x - 1]
        return edge_second[c, x + 2 if x < 1 else x - 4]

    def at_third(x, c):
        if 2 <= x < 6:
            return third[c, x - 2]
        return edge_third[c, x + 1 if x < 2 else x - 3]

    def step(at, x):
        of, inside = weight(x)
        return operate(of, lambda a, c: at(x + a - 1, c), inside)

    for x in (-2, -1, 0, 7, 8, 9):
        for c, value in enumerate(lean(step(at_first, x))):
            edge_second[c, x + 2 if x < 1 else x - 4] = value
    for x in (-1, 0, 1, 6, 7, 8):
        value = 2.0 * step(at_second, x) - at_first(x, 1)
        for c, value in enumerate(lean(value)):
            edge_third[c, x + 1 if x < 2 else x - 3] = value
    for x in (0, 1, 2, 5, 6, 7):
        fourth = 2.0 * step(at_third, x) - at_second(x, 1)
        result = (
            CHEB[0] * at_first(x, 1) + CHEB[1] * at_second(x, 1) + CHEB[2] * at_third(x, 1) + CHEB[3] * fourth
        )
        for g in range(4):
            smooth[4 * x + g] = result[OFF + 8 * g : OFF + 8 * g + 8]

    for b in range(BLOCKS):
        chosen[pl.ds(8 * b, 8), :] = smooth[node_block[b]]
    columns = rows_by_column(chosen)
    low = half_lanes((8, W))
    parts = ([], [])
    for j in range(4):
        one, two = columns[2 * j], columns[2 * j + 1]
        parts[0].append(jnp.where(low, one, swap_halves(two)))
        parts[1].append(jnp.where(low, swap_halves(one), two))
    values = [jnp.concatenate(p, axis=1) for p in parts]
    pieces = [split(v) for v in values]
    left = jnp.concatenate([pieces[0][0], pieces[1][0], pieces[0][1], pieces[1][1]], axis=0)
    block = lax.broadcasted_iota(jnp.int32, (BLOCKS, SAMPLES), 0)
    sums = [jnp.zeros((BLOCKS, SAMPLES), F32) for _ in range(2)]
    for b in range(BLOCKS):
        product = lax.dot_general(
            left, matrix[b], (((1,), (1,)), ((), ())), preferred_element_type=F32
        )
        for r in range(2):
            both = product[8 * r : 8 * r + 8] + product[16 + 8 * r : 24 + 8 * r]
            sums[r] = jnp.where(block == b, both, sums[r])
    live = is_live(count)
    for r in range(2):
        payload[8 * r : 8 * r + 8, :] = jnp.where(live, sums[r], 0.0)
    payload[16:24, :] = jnp.zeros((8, SAMPLES), F32)
    for k in range(2):
        for h in range(2):
            for kind in range(2):
                row = 16 + 4 * kind + 2 * k + h
                payload[row : row + 1, 0:W] = rows[kind, k : k + 1, h * W : h * W + W]
    lane = lax.broadcasted_iota(jnp.int32, (8, W), 1)
    names = jnp.zeros((8, W), F32)
    for b in range(BLOCKS):
        names = jnp.where(lane == 8 * place[2] + b, (owner[b] + 1).astype(F32), names)
    payload[16:17, W : 2 * W] = names[0:1]


def is_live(count):
    block = lax.broadcasted_iota(jnp.int32, (BLOCKS, SAMPLES), 0)
    limit = jnp.zeros((BLOCKS, SAMPLES), jnp.int32)
    for b in range(BLOCKS):
        limit = jnp.where(block == b, count[b], limit)
    return lax.broadcasted_iota(jnp.int32, (BLOCKS, SAMPLES), 1) < limit


def collect(source, owner, place, core, out):
    half = place[0]
    names = []
    for z in range(2):
        total = source[0, z, 16:24, W : 2 * W]
        for n in range(1, 16):
            total = total + source[n, z, 16:24, W : 2 * W]
        names.append(total[0:1])
    names = jnp.concatenate(names, axis=1)
    target = lax.broadcasted_iota(jnp.int32, (16, 2 * W), 0)
    lane = lax.broadcasted_iota(jnp.int32, (16, 2 * W), 1)
    name = jnp.full((16, 2 * W), -1.0, F32)
    spot = jnp.full((16, 2 * W), -1, jnp.int32)
    for t in range(BLOCKS):
        k = owner[t]
        tiles = k // 2
        sx, sy = tiles // 8, tiles % 8
        where = ((sx % 2) ^ half) * W + ((sx // 2) * 4 + sy // 2) * 8 + 2 * (k % 2)
        where = jnp.where(sy % 2 == core, where, -1024)
        name = jnp.where(target == t, (k + 1).astype(F32), name)
        spot = jnp.where(target == t, where, spot)
    for t in range(2):
        name = jnp.where(target == BLOCKS + t, (2 * place[4] + t + 1).astype(F32), name)
    hit = (name == names).astype(jnp.bfloat16)
    for r in range(2):
        data = jnp.concatenate(
            [source[n, z, 8 * r : 8 * r + 8, :] for z in range(2) for n in range(16)], axis=0
        )
        high, low = split(data)
        out[r] = jnp.dot(hit, high, preferred_element_type=F32) + jnp.dot(
            hit, low, preferred_element_type=F32
        )
    data = jnp.concatenate([source[n, z, 16:24, 0:W] for z in range(2) for n in range(16)], axis=0)
    high, low = split(data)
    choose = jnp.concatenate(
        [(lane == spot + 4 * kind + h).astype(jnp.bfloat16) for kind in range(2) for h in range(2)], axis=0
    )
    found = jnp.dot(choose, high, preferred_element_type=F32) + jnp.dot(
        choose, low, preferred_element_type=F32
    )
    for kind in range(2):
        for h in range(2):
            row = 32 * kind + 16 * h
            out[2 + kind, :, h * W : h * W + W] = found[row : row + 16]


def collect_kernel(place, owner, here, out):
    collect(here, owner, place, place[1], out)


def update_kernel(
    place, node_block, owner, count, mine, there, smooth, matrix, rows,
    out, misfit,
    other, update,
):
    collect(there, owner, place, 1 - place[1], other)
    for k in range(2):
        for r in range(2):
            t = BLOCKS + k
            misfit[k, r : r + 1, :] = rows[0, k : k + 1, :] - (mine[r, t : t + 1, :] + other[r, t : t + 1, :])
    live = is_live(count)
    drill, gain = [mine[i, 0:BLOCKS, :] + other[i, 0:BLOCKS, :] for i in (2, 3)]
    picked = [
        jnp.where(live, gain * (drill - (mine[r, 0:BLOCKS, :] + other[r, 0:BLOCKS, :])), 0.0)
        for r in range(2)
    ]
    pieces = [split(v) for v in picked]
    left = jnp.concatenate([pieces[0][0], pieces[1][0], pieces[0][1], pieces[1][1]], axis=0)
    block = lax.broadcasted_iota(jnp.int32, (BLOCKS, NODES), 0)
    sums = [jnp.zeros((BLOCKS, NODES), F32) for _ in range(2)]
    for b in range(BLOCKS):
        product = jnp.dot(left, matrix[b], preferred_element_type=F32)
        for r in range(2):
            both = product[8 * r : 8 * r + 8] + product[16 + 8 * r : 24 + 8 * r]
            sums[r] = jnp.where(block == b, both, sums[r])
    low = half_lanes((8, W))
    for j in range(4):
        one, two = sums[0][:, j * W : j * W + W], sums[1][:, j * W : j * W + W]
        update[pl.ds(2 * j, 8, stride=8), :] = jnp.where(low, one, swap_halves(two))
        update[pl.ds(2 * j + 1, 8, stride=8), :] = jnp.where(low, swap_halves(one), two)
    out[...] = smooth[...]
    for b in range(BLOCKS):
        n = node_block[b]
        out[n] = out[n] + update[8 * b : 8 * b + 8, :]


def shape(*dims, dtype=F32):
    return jax.ShapeDtypeStruct(dims, dtype)


def call(kernel, outs, ins, name, scratch=()):
    return pl.pallas_call(
        kernel,
        out_shape=outs,
        in_specs=ins,
        out_specs=(VMEM,) * len(outs),
        scratch_shapes=scratch,
        compiler_params=pltpu.CompilerParams(vmem_limit_bytes=24 * 1024 * 1024),
        name=name,
    )


def shards(
    noise, classes, table, obs_matrix, node_block, sample_block, sample_count, drill_data, obs_gain
):
    place = jnp.stack(
        [
            lax.axis_index("zh"),
            lax.axis_index("core"),
            lax.axis_index(("x", "y")),
            lax.axis_index(("x", "y")),
            lax.axis_index(("x", "zh", "y", "core")),
        ]
    ).astype(jnp.int32)

    even, odd, doubled = call(
        edge_y_kernel,
        (shape(X, 4, W), shape(X, 4, W), shape(X, Y, W)),
        [SMEM, VMEM, VMEM],
        "edge_y",
    )(place, noise, classes)
    odd = permute(odd, ("y", "core"), odd_pair)
    even = permute(even, ("y", "core"), even_pair)
    field, kinds, even, odd = call(
        edge_x_kernel,
        (shape(X, YP, W), shape(X, YP, W), shape(4, YP, W), shape(4, YP, W)),
        [SMEM] + [VMEM] * 4,
        "edge_x",
    )(place, noise, doubled, even, odd)
    odd = permute(odd, ("x", "zh"), odd_pair)
    even = permute(even, ("x", "zh"), even_pair)
    weights, first, second, third, middle, tables, matrix, rows = call(
        interior_kernel,
        (
            shape(27, X, YP, W),
            shape(3, X, YP, W),
            shape(3, 6, YP, W),
            shape(3, 4, YP, W),
            shape(8, 8, W),
            shape(27, 8, W),
            shape(BLOCKS, SAMPLES, NODES, dtype=jnp.bfloat16),
            shape(2, 2, SAMPLES),
        ),
        [VMEM] * 3 + [HBM] * 3,
        "interior",
        [pltpu.SemaphoreType.DMA((3,))],
    )(field, kinds, table, obs_matrix, drill_data, obs_gain)
    smooth, payload = call(
        finish_kernel,
        (shape(32, 8, W), shape(ROWS, SAMPLES)),
        [SMEM] * 4 + [VMEM] * 11,
        "finish",
        [
            pltpu.VMEM((6, YP, W), F32),
            pltpu.VMEM((4, YP, W), F32),
            pltpu.VMEM((27, 4, YP, W), F32),
            pltpu.VMEM((3, 6, YP, W), F32),
            pltpu.VMEM((3, 6, YP, W), F32),
            pltpu.VMEM((3, 6, YP, W), F32),
            pltpu.VMEM((64, W), F32),
        ],
    )(
        place, node_block, sample_count, sample_block, kinds, even, odd,
        weights, first, second, third, middle, tables, matrix, rows,
    )
    other = permute(payload, ("zh",), lambda z: (z ^ 1,))
    pair = jnp.stack([payload, other])
    here = lax.all_to_all(
        jnp.broadcast_to(pair[None], (16, 2, ROWS, SAMPLES)), ("x", "y"), 0, 0, tiled=True
    )
    there = permute(here, ("core",), lambda c: (c ^ 1,))
    (mine,) = call(collect_kernel, (shape(4, 16, SAMPLES),), [SMEM, SMEM, VMEM], "collect")(
        place, sample_block, here
    )
    out, misfit = call(
        update_kernel,
        (shape(32, 8, W), shape(2, 2, SAMPLES)),
        [SMEM] * 4 + [VMEM] * 5,
        "update",
        [pltpu.VMEM((4, 16, SAMPLES), F32), pltpu.VMEM((64, W), F32)],
    )(place, node_block, sample_block, sample_count, mine, there, smooth, matrix, rows)
    return out.reshape(X, Y, W), misfit


def solution(mesh):
    fine = Mesh(
        mesh.devices.reshape(4, 4, 2, 4, 2), ("real", "x", "zh", "y", "core")
    )
    sx, sy = ("x", "zh"), ("y", "core")
    both = sx + sy
    in_specs = (
        P(sx, sy, "real"),
        P(sx, sy, None),
        P(),
        P(both, None, None),
        P(both),
        P(both),
        P(both),
        P(both, None),
        P(both, None),
    )
    out_specs = (P(sx, sy, "real"), P(both, "real", None))
    return jax.shard_map(shards, mesh=fine, in_specs=in_specs, out_specs=out_specs, check_vma=False)
```

time: 79.4 us -> 63.5 us (0.80)
  Pallas kernels: 15.8 us -> 8.22 us
  local copies, waits for them, and re-layouts: 9.08 us -> 5.62 us
  blocking collectives: 22.3 us -> 19.3 us
  waiting for transfers between devices: 6.72 us -> 5.38 us
    pallas_call x4 -> x6, Pallas kernels: 15.8 us -> 8.22 us  [the longest x1 2.56 us: shards(): call(finish_kernel, (shape(32, 8, W), shape(ROWS, SAMPLES)), [SMEM] * 4 +...]
    all_to_all x1, blocking collectives: 22.3 us -> 19.3 us  [shards(): lax.all_to_all(jnp.broadcast_to(pair[None], (16, 2, ROWS, SAMPLES)), ('x'...]
    broadcast_in_dim x3 -> x0, local copies, waits for them, and re-layouts: 1.54 us -> none  [the longest x1 0.73 us: shards(): count = sample_count[:, None]]
    ppermute x6, waiting for transfers between devices: 6.72 us -> 5.38 us  [permute(): return lax.ppermute(value, axes if len(axes) > 1 else axes[0], pairs)]
    unnamed x30 -> x18, local copies, waits for them, and re-layouts: 6.69 us -> 5.46 us
  transfers between devices with their start and end apart: 6 -> 6, of which waited for: 4 -> 3; matrix products, arithmetic and copies ran while one was open for 3% -> 0% of each run, Pallas kernels for 0% -> 4%
where the time goes in v2:
time: 63.5 us; the launch traced here: 63.2 us
  starting transfers between devices  23.9 us (38%)
  blocking collectives  19.3 us (30%)
  Pallas kernels  8.22 us (13%)
  local copies, waits for them, and re-layouts  5.62 us (9%)
  waiting for transfers between devices  5.38 us (8%)
  between operations  0.79 us (1%)
    ppermute x6, starting transfers between devices, permute(): return lax.ppermute(value, axes if len(axes) > 1 else axes[0], pairs)  23.9 us
    all_to_all x1, blocking collectives, shards(): lax.all_to_all(jnp.broadcast_to(pair[None], (16, 2, ROWS, SAMPLES)), ('x'...  19.3 us
    unnamed x18, local copies, waits for them, and re-layouts  5.46 us
    ppermute x6, waiting for transfers between devices, permute(): return lax.ppermute(value, axes if len(axes) > 1 else axes[0], pairs)  5.38 us
    pallas_call x1, Pallas kernels, shards(): call(finish_kernel, (shape(32, 8, W), shape(ROWS, SAMPLES)), [SMEM] * 4 +...  2.56 us
    pallas_call x1, Pallas kernels, shards(): call(update_kernel, (shape(32, 8, W), shape(2, 2, SAMPLES)), [SMEM] * 4 +...  2.1 us
    pallas_call x1, Pallas kernels, shards(): call(interior_kernel, (shape(27, X, YP, W), shape(3, X, YP, W), shape(3,...  1.37 us
  transfers between devices with their start and end apart: 6, of which 3 were waited for; matrix products, arithmetic and copies ran while one was open for 0% of the time, Pallas kernels for 4%

profile of v2, /device:TPU:1, one launch (start us, length us, event | category | flops | bytes accessed | tf_op | source)
XLA Modules:
  0.0 63.2 jit_solution(10071570278528031872)
XLA Ops:
  0.6 0.0 copy-start.3
  0.6 0.0 copy-start.8
  0.7 0.0 copy-start.7
  0.7 0.1 stack.29.place
  0.8 0.0 copy-start.1
  0.8 0.9 %copy-done.1 = f32[8,32,128]{2,1,0:T(8,128)S(1)} copy-done((f32[8,32,128]{2,1,0:T(8,128)S(1)}, f32[8,32,128]{2,1,0:T(8,128)}, u32[]{:S(2)}) %copy-start.1) | copy-done | bytes 131096
  1.7 0.0 copy-start.2
  1.7 0.9 %copy-done.2 = s32[8,32,64]{2,1,0:T(8,128)S(1)} copy-done((s32[8,32,64]{2,1,0:T(8,128)S(1)}, s32[8,32,64]{2,1,0:T(8,128)}, u32[]{:S(2)}) %copy-start.2) | copy-done | bytes 65560
  2.6 0.7 %edge_y.1 = (f32[8,4,128]{2,1,0:T(4,128)S(1)}, f32[8,4,128]{2,1,0:T(4,128)S(1)}, f32[8,32,128]{2,1,0:T(8,128)S(1)}) custom-call(s32[5]{0:T(128)S(1)} %stack.29.place, f32[8,32,128]{2,1,0:T(8,128)S(1)} %copy-done.1, s32[8,32,64]{2,1,0:T(8,128)S(1)} %copy-done.2), custom_call_target="tpu_custom_call" | custom-call | tf_op jit(solution)/shard_map/edge_y/pallas_call | solution.py:473
  3.2 3.3 %collective-permute-start = (f32[8,4,128]{2,1,0:T(4,128)S(1)}, f32[8,4,128]{2,1,0:T(4,128)S(1)}, u32[]{:S(2)}, u32[]{:S(2)}) collective-permute-start(f32[8,4,128]{2,1,0:T(4,128)S(1)} %get-tuple-element.22), channel_id=1, source_target_pairs={{0,1},{1,0},{2,3},{3,2},{4,5},{5,4},{6,7},{7,6},{8,9},{9,8},{10,11... | collective-permute-start | bytes 49160 | tf_op jit(solution)/shard_map/ppermute | solution.py:40
  6.6 1.9 %collective-permute-start.1 = (f32[8,4,128]{2,1,0:T(4,128)S(1)}, f32[8,4,128]{2,1,0:T(4,128)S(1)}, u32[]{:S(2)}, u32[]{:S(2)}) collective-permute-start(f32[8,4,128]{2,1,0:T(4,128)S(1)} %get-tuple-element.23), channel_id=1, source_target_pairs={{1,2},{2,1},{3,4},{4,3},{5,6},{6,5},{9,10},{10,9},{11,12},{12,11},... | collective-permute-start | bytes 49160 | tf_op jit(solution)/shard_map/ppermute | solution.py:40
  8.5 0.0 collective-permute-done.even_in
  8.5 3.1 %collective-permute-done.1.odd_in = f32[8,4,128]{2,1,0:T(4,128)S(1)} collective-permute-done((f32[8,4,128]{2,1,0:T(4,128)S(1)}, f32[8,4,128]{2,1,0:T(4,128)S(1)}, u32[]{:S(2)}, u32[]{:S(2)}) %collective-permute-start.1) | collective-permute-done | bytes 16416 | tf_op jit(solution)/shard_map/ppermute | solution.py:40
  11.6 0.7 %edge_x.1 = (f32[8,40,128]{2,1,0:T(8,128)S(1)}, f32[8,40,128]{2,1,0:T(8,128)S(1)}, f32[4,40,128]{2,1,0:T(8,128)S(1)}, f32[4,40,128]{2,1,0:T(8,128)S(1)}) custom-call(s32[5]{0:T(128)S(1)} %stack.29.place, f32[8,32,128]{2,1,0:T(8,128)S(1)} %copy-done.1, f32[8,32,128]{2,1,0:T(8,128)S(1)} %get-tuple-element.21.doubled, ...), custom_call_target="tpu_custom_call" | custom-call | tf_op jit(solution)/shard_map/edge_x/pallas_call | solution.py:481
  12.3 5.3 %collective-permute-start.2 = (f32[4,40,128]{2,1,0:T(8,128)S(1)}, f32[4,40,128]{2,1,0:T(8,128)S(1)}, u32[]{:S(2)}, u32[]{:S(2)}) collective-permute-start(f32[4,40,128]{2,1,0:T(8,128)S(1)} %get-tuple-element.25), channel_id=1, source_target_pairs={{0,8},{8,0},{16,24},{24,16},{32,40},{40,32},{48,56},{56,48},{1,9},... | collective-permute-start | bytes 245768 | tf_op jit(solution)/shard_map/ppermute | solution.py:40
  17.5 0.7 %collective-permute-start.3 = (f32[4,40,128]{2,1,0:T(8,128)S(1)}, f32[4,40,128]{2,1,0:T(8,128)S(1)}, u32[]{:S(2)}, u32[]{:S(2)}) collective-permute-start(f32[4,40,128]{2,1,0:T(8,128)S(1)} %get-tuple-element.26), channel_id=1, source_target_pairs={{8,16},{16,8},{24,32},{32,24},{40,48},{48,40},{9,17},{17,9},{25,33... | collective-permute-start | bytes 245768 | tf_op jit(solution)/shard_map/ppermute | solution.py:40
  18.2 0.0 copy-start
  18.2 1.6 %copy-done = bf16[8,256,512]{2,1,0:T(8,128)(2,1)S(1)} copy-done((bf16[8,256,512]{2,1,0:T(8,128)(2,1)S(1)}, bf16[8,256,512]{2,1,0:T(8,128)(2,1)}, u32[]{:S(2)}) %copy-start) | copy-done | bytes 2097176
  19.8 0.0 copy-start.4
  19.8 0.7 %copy-done.4 = f32[8,27]{1,0:T(8,128)S(1)} copy-done((f32[8,27]{1,0:T(8,128)S(1)}, f32[8,27]{1,0:T(8,128)}, u32[]{:S(2)}) %copy-start.4) | copy-done | bytes 888
  20.5 0.0 copy-start.5
  20.5 0.7 %copy-done.5 = f32[2,256]{1,0:T(2,128)S(1)} copy-done((f32[2,256]{1,0:T(2,128)S(1)}, f32[2,256]{1,0:T(2,128)}, u32[]{:S(2)}) %copy-start.5) | copy-done | bytes 2072
  21.2 0.0 copy-start.6
  21.2 0.7 %copy-done.6 = f32[2,256]{1,0:T(2,128)S(1)} copy-done((f32[2,256]{1,0:T(2,128)S(1)}, f32[2,256]{1,0:T(2,128)}, u32[]{:S(2)}) %copy-start.6) | copy-done | bytes 2072
  21.8 1.4 %interior.1 = (f32[27,8,40,128]{3,2,1,0:T(8,128)S(1)}, f32[3,8,40,128]{3,2,1,0:T(8,128)S(1)}, f32[3,6,40,128]{3,2,1,0:T(8,128)S(1)}, f32[3,4,40,128]{3,2,1,0:T(8...) custom-call(f32[8,40,128]{2,1,0:T(8,128)S(1)} %get-tuple-element.27., ...), custom_call_target="tpu_custom_call" | custom-call | tf_op jit(solution)/shard_map/interior/pallas_call | solution.py:489
  23.2 0.0 collective-permute-done.2.even_in
  23.2 0.0 collective-permute-done.3.odd_in
  23.2 0.0 copy-done.3
  23.3 0.0 copy-done.8
  23.3 0.0 copy-done.7
  23.3 2.6 %finish.1 = (f32[32,8,128]{2,1,0:T(8,128)S(1)}, f32[24,256]{1,0:T(8,128)S(1)}) custom-call(s32[5]{0:T(128)S(1)} %stack.29.place, s32[8]{0:T(128)S(1)} %copy-done.7, s32[8]{0:T(128)S(1)} %copy-done.8, s32[8]{0:T(128)S(1)} %copy-done.3, f32[8,40,128]{2,1,0:T(8,128)S(1)} %get-tuple-element.24.kinds, f32[4,40,128]{2,1,0:T(8,128)S(1)} %collective-permute-done.2.even_in, ...), custom_call_target="tpu_custom_call" | custom-call | tf_op jit(solution)/shard_map/finish/pallas_call | solution.py:505
  25.8 7.6 %collective-permute-start.4 = (f32[24,256]{1,0:T(8,128)S(1)}, f32[24,256]{1,0:T(8,128)S(1)}, u32[]{:S(2)}, u32[]{:S(2)}) collective-permute-start(f32[24,256]{1,0:T(8,128)S(1)} %get-tuple-element.36), channel_id=1, source_target_pairs={{0,8},{8,0},{1,9},{9,1},{2,10},{10,2},{3,11},{11,3},{4,12},{12,4},... | collective-permute-start | bytes 73736 | tf_op jit(solution)/shard_map/ppermute | solution.py:40
  33.4 1.2 %collective-permute-done.4 = f32[24,256]{1,0:T(8,128)S(1)} collective-permute-done((f32[24,256]{1,0:T(8,128)S(1)}, f32[24,256]{1,0:T(8,128)S(1)}, u32[]{:S(2)}, u32[]{:S(2)}) %collective-permute-start.4) | collective-permute-done | bytes 24608 | tf_op jit(solution)/shard_map/ppermute | solution.py:40
  34.6 0.1 broadcast_in_dim.2
  34.7 19.3 %all_to_all.5.here = f32[16,2,24,256]{3,2,1,0:T(8,128)S(1)} all-to-all(f32[16,2,24,256]{3,2,1,0:T(8,128)S(1)} %broadcast_in_dim.2), channel_id=1, replica_groups=mesh['real'=4,'x'=4,'zh'=2,'y'=4,'core'=2] {'x','y'}, dimensions={0} | all-to-all | bytes 1572864 | tf_op jit(solution)/shard_map/all_to_all | solution.py:525
  54.0 5.2 %collective-permute-start.5 = (f32[16,2,24,256]{3,2,1,0:T(8,128)S(1)}, f32[16,2,24,256]{3,2,1,0:T(8,128)S(1)}, u32[]{:S(2)}, u32[]{:S(2)}) collective-permute-start(f32[16,2,24,256]{3,2,1,0:T(8,128)S(1)} %all_to_all.5.here), channel_id=1, source_target_pairs={{0,1},{1,0},{2,3},{3,2},{4,5},{5,4},{6,7},{7,6},{8,9},{9,8},{10,11... | collective-permute-start | bytes 2359304 | tf_op jit(solution)/shard_map/ppermute | solution.py:40
  59.2 0.9 %collect.1.mine = f32[4,16,256]{2,1,0:T(8,128)S(1)} custom-call(s32[5]{0:T(128)S(1)} %stack.29.place, s32[8]{0:T(128)S(1)} %copy-done.3, f32[16,2,24,256]{3,2,1,0:T(8,128)S(1)} %all_to_all.5.here), custom_call_target="tpu_custom_call" | custom-call | tf_op jit(solution)/shard_map/collect/pallas_call | solution.py:529
  60.0 1.0 %collective-permute-done.5.there = f32[16,2,24,256]{3,2,1,0:T(8,128)S(1)} collective-permute-done((f32[16,2,24,256]{3,2,1,0:T(8,128)S(1)}, f32[16,2,24,256]{3,2,1,0:T(8,128)S(1)}, u32[]{:S(2)}, u32[]{:S(2)}) %collective-permute-start.5) | collective-permute-done | bytes 786464 | tf_op jit(solution)/shard_map/ppermute | solution.py:40
  61.1 2.1 %update.1 = (f32[32,8,128]{2,1,0:T(8,128)}, f32[2,2,256]{2,1,0:T(2,128)}) custom-call(s32[5]{0:T(128)S(1)} %stack.29.place, s32[8]{0:T(128)S(1)} %copy-done.7, s32[8]{0:T(128)S(1)} %copy-done.3, s32[8]{0:T(128)S(1)} %copy-done.8, f32[4,16,256]{2,1,0:T(8,128)S(1)} %collect.1.mine, f32[16,2,24,256]{3,2,1,0:T(8,128)S(1)} %collective-permute-done.5.there, ...), custom_call_target="tpu_custom_call" | custom-call | tf_op jit(solution)/shard_map/update/pallas_call | solution.py:532
  (1 shorter events, 0.0 us)
Async XLA Ops:
  0.6 22.6 %copy-start.3 = (s32[8]{0:T(128)S(1)}, s32[8]{0:T(128)}, u32[]{:S(2)}) copy-start(s32[8]{0:T(128)} %owner.5) | copy-start | bytes 100
  0.6 22.6 %copy-start.8 = (s32[8]{0:T(128)S(1)}, s32[8]{0:T(128)}, u32[]{:S(2)}) copy-start(s32[8]{0:T(128)} %count.3) | copy-start | bytes 100
  0.7 22.6 %copy-start.7 = (s32[8]{0:T(128)S(1)}, s32[8]{0:T(128)}, u32[]{:S(2)}) copy-start(s32[8]{0:T(128)} %node_block.3) | copy-start | bytes 100
  0.8 0.9 %copy-start.1 = (f32[8,32,128]{2,1,0:T(8,128)S(1)}, f32[8,32,128]{2,1,0:T(8,128)}, u32[]{:S(2)}) copy-start(f32[8,32,128]{2,1,0:T(8,128)} %noise.3) | copy-start | bytes 393220
  1.7 0.9 %copy-start.2 = (s32[8,32,64]{2,1,0:T(8,128)S(1)}, s32[8,32,64]{2,1,0:T(8,128)}, u32[]{:S(2)}) copy-start(s32[8,32,64]{2,1,0:T(8,128)} %classes.1) | copy-start | bytes 196612
  3.2 5.3 %collective-permute-start = (f32[8,4,128]{2,1,0:T(4,128)S(1)}, f32[8,4,128]{2,1,0:T(4,128)S(1)}, u32[]{:S(2)}, u32[]{:S(2)}) collective-permute-start(f32[8,4,128]{2,1,0:T(4,128)S(1)} %get-tuple-element.22), channel_id=1, source_target_pairs={{0,1},{1,0},{2,3},{3,2},{4,5},{5,4},{6,7},{7,6},{8,9},{9,8},{10,11... | collective-permute-start | bytes 49160 | tf_op jit(solution)/shard_map/ppermute | solution.py:40
  6.6 5.0 %collective-permute-start.1 = (f32[8,4,128]{2,1,0:T(4,128)S(1)}, f32[8,4,128]{2,1,0:T(4,128)S(1)}, u32[]{:S(2)}, u32[]{:S(2)}) collective-permute-start(f32[8,4,128]{2,1,0:T(4,128)S(1)} %get-tuple-element.23), channel_id=1, source_target_pairs={{1,2},{2,1},{3,4},{4,3},{5,6},{6,5},{9,10},{10,9},{11,12},{12,11},... | collective-permute-start | bytes 49160 | tf_op jit(solution)/shard_map/ppermute | solution.py:40
  12.3 10.9 %collective-permute-start.2 = (f32[4,40,128]{2,1,0:T(8,128)S(1)}, f32[4,40,128]{2,1,0:T(8,128)S(1)}, u32[]{:S(2)}, u32[]{:S(2)}) collective-permute-start(f32[4,40,128]{2,1,0:T(8,128)S(1)} %get-tuple-element.25), channel_id=1, source_target_pairs={{0,8},{8,0},{16,24},{24,16},{32,40},{40,32},{48,56},{56,48},{1,9},... | collective-permute-start | bytes 245768 | tf_op jit(solution)/shard_map/ppermute | solution.py:40
  17.5 5.7 %collective-permute-start.3 = (f32[4,40,128]{2,1,0:T(8,128)S(1)}, f32[4,40,128]{2,1,0:T(8,128)S(1)}, u32[]{:S(2)}, u32[]{:S(2)}) collective-permute-start(f32[4,40,128]{2,1,0:T(8,128)S(1)} %get-tuple-element.26), channel_id=1, source_target_pairs={{8,16},{16,8},{24,32},{32,24},{40,48},{48,40},{9,17},{17,9},{25,33... | collective-permute-start | bytes 245768 | tf_op jit(solution)/shard_map/ppermute | solution.py:40
  18.2 1.6 %copy-start = (bf16[8,256,512]{2,1,0:T(8,128)(2,1)S(1)}, bf16[8,256,512]{2,1,0:T(8,128)(2,1)}, u32[]{:S(2)}) copy-start(bf16[8,256,512]{2,1,0:T(8,128)(2,1)} %matrix.1) | copy-start | bytes 6291460
  19.8 0.7 %copy-start.4 = (f32[8,27]{1,0:T(8,128)S(1)}, f32[8,27]{1,0:T(8,128)}, u32[]{:S(2)}) copy-start(f32[8,27]{1,0:T(8,128)} %table.1) | copy-start | bytes 2596
  20.5 0.7 %copy-start.5 = (f32[2,256]{1,0:T(2,128)S(1)}, f32[2,256]{1,0:T(2,128)}, u32[]{:S(2)}) copy-start(f32[2,256]{1,0:T(2,128)} %drill.1) | copy-start | bytes 6148
  21.2 0.7 %copy-start.6 = (f32[2,256]{1,0:T(2,128)S(1)}, f32[2,256]{1,0:T(2,128)}, u32[]{:S(2)}) copy-start(f32[2,256]{1,0:T(2,128)} %gain.1) | copy-start | bytes 6148
  25.8 8.8 %collective-permute-start.4 = (f32[24,256]{1,0:T(8,128)S(1)}, f32[24,256]{1,0:T(8,128)S(1)}, u32[]{:S(2)}, u32[]{:S(2)}) collective-permute-start(f32[24,256]{1,0:T(8,128)S(1)} %get-tuple-element.36), channel_id=1, source_target_pairs={{0,8},{8,0},{1,9},{9,1},{2,10},{10,2},{3,11},{11,3},{4,12},{12,4},... | collective-permute-start | bytes 73736 | tf_op jit(solution)/shard_map/ppermute | solution.py:40
  54.0 7.1 %collective-permute-start.5 = (f32[16,2,24,256]{3,2,1,0:T(8,128)S(1)}, f32[16,2,24,256]{3,2,1,0:T(8,128)S(1)}, u32[]{:S(2)}, u32[]{:S(2)}) collective-permute-start(f32[16,2,24,256]{3,2,1,0:T(8,128)S(1)} %all_to_all.5.here), channel_id=1, source_target_pairs={{0,1},{1,0},{2,3},{3,2},{4,5},{5,4},{6,7},{7,6},{8,9},{9,8},{10,11... | collective-permute-start | bytes 2359304 | tf_op jit(solution)/shard_map/ppermute | solution.py:40

commit v3 on v2

--- a/solution.py
+++ b/solution.py
@@ -68,18 +68,37 @@
     return jnp.where(low, row, other), jnp.where(low, other, row)
 
 
-def edge_y_kernel(place, noise, classes, even, odd, doubled):
+def edge_y_kernel(
+    place, noise_far, classes_far, owner_far,
+    even, odd, noise, doubled, names,
+    classes, owner, sems,
+):
+    copies = [
+        pltpu.make_async_copy(noise_far, noise, sems.at[0]),
+        pltpu.make_async_copy(classes_far, classes, sems.at[1]),
+        pltpu.make_async_copy(owner_far, owner, sems.at[2]),
+    ]
+    for copy in copies:
+        copy.start()
+    for copy in copies:
+        copy.wait()
     kinds = (classes[...] + 1).astype(F32)
     doubled[...] = jnp.concatenate([kinds, kinds], axis=-1)
     core = place[1]
+    lane = lax.broadcasted_iota(jnp.int32, (8, W), 1)
+    own = jnp.zeros((8, W), F32)
+    for b in range(BLOCKS):
+        own = jnp.where(lane == b, (owner[b] + 1).astype(F32), own)
+    names[...] = own
+    even[X] = own[0:4]
 
     def low(out):
-        out[:, 0:3, :] = noise[:, 0:3, :]
-        out[:, 3:4, :] = pack(doubled[:, 0:1, :], doubled[:, 1:2, :])
+        out[0:X, 0:3, :] = noise[:, 0:3, :]
+        out[0:X, 3:4, :] = pack(doubled[:, 0:1, :], doubled[:, 1:2, :])
 
     def high(out):
-        out[:, 0:3, :] = noise[:, Y - 3 : Y, :]
-        out[:, 3:4, :] = pack(doubled[:, Y - 2 : Y - 1, :], doubled[:, Y - 1 : Y, :])
+        out[0:X, 0:3, :] = noise[:, Y - 3 : Y, :]
+        out[0:X, 3:4, :] = pack(doubled[:, Y - 2 : Y - 1, :], doubled[:, Y - 1 : Y, :])
 
     @pl.when(core == 0)
     def _():
@@ -92,7 +111,9 @@
         high(odd)
 
 
-def edge_x_kernel(place, noise, doubled, even_in, odd_in, field, kinds, even, odd):
+def edge_x_kernel(
+    place, noise, doubled, names, even_in, odd_in, field, kinds, even, odd, lists
+):
     core, half = place[1], place[0]
     field[:, 0:8, :] = jnp.zeros((X, 8, W), F32)
     field[:, 32:40, :] = jnp.zeros((X, 8, W), F32)
@@ -101,13 +122,16 @@
     field[:, OFF : OFF + Y, :] = noise[...]
     kinds[:, OFF : OFF + Y, :] = doubled[...]
 
+    lists[0:4] = names[0:4]
+    lists[1:2] = even_in[X, 0:1, :]
+
     def sides(low, high):
-        field[:, 1:4, :] = low[:, 0:3, :]
-        first, second = unpack(low[:, 3:4, :])
+        field[:, 1:4, :] = low[0:X, 0:3, :]
+        first, second = unpack(low[0:X, 3:4, :])
         kinds[:, 2:3, :] = first
         kinds[:, 3:4, :] = second
-        field[:, 36:39, :] = high[:, 0:3, :]
-        first, second = unpack(high[:, 3:4, :])
+        field[:, 36:39, :] = high[0:X, 0:3, :]
+        first, second = unpack(high[0:X, 3:4, :])
         kinds[:, 36:37, :] = first
         kinds[:, 37:38, :] = second
 
@@ -136,6 +160,9 @@
     def _():
         low(even)
         high(odd)
+
+    even[3, 0:1, :] = lists[0:1]
+    even[3, YP - 1 : YP, :] = lists[1:2]
 
 
 def rows_by_column(block_rows):
@@ -193,16 +220,18 @@
 def interior_kernel(
     field, kinds, table, matrix, drill, gain,
     weights, first, second, third, smooth, tables, held_matrix, held_rows,
-    sems,
+    held_table, sems,
 ):
     copies = [
         pltpu.make_async_copy(matrix, held_matrix, sems.at[0]),
         pltpu.make_async_copy(drill, held_rows.at[0], sems.at[1]),
         pltpu.make_async_copy(gain, held_rows.at[1], sems.at[2]),
+        pltpu.make_async_copy(table, held_table, sems.at[3]),
     ]
-    for copy in copies:
+    for copy in reversed(copies):
         copy.start()
-    spread_table(table, tables)
+    copies[3].wait()
+    spread_table(held_table, tables)
     for x in range(X):
         def put(o, rows, value, x=x):
             weights[o, x, rows, :] = value
@@ -232,14 +261,14 @@
         )
         for g in range(4):
             smooth[4 * (x - 3) + g] = result[OFF + 8 * g : OFF + 8 * g + 8]
-    for copy in copies:
+    for copy in copies[:3]:
         copy.wait()
 
 
 def finish_kernel(
-    place, node_block, count, owner, kinds, even_in, odd_in,
+    place, node_block, count, owner, kinds, even_in, odd_in, near,
     weights, first, second, third, middle, tables, matrix, rows,
-    smooth, payload,
+    smooth, payload, lists,
     halo, halo_kinds, halo_weights, edge_first, edge_second, edge_third, chosen,
 ):
     half = place[0]
@@ -251,6 +280,13 @@
         halo_kinds[0], halo_kinds[1] = one, two
         one, two = unpack(high[3])
         halo_kinds[2], halo_kinds[3] = one, two
+        halo_kinds[:, 0:1, :] = jnp.zeros((4, 1, W), F32)
+        halo_kinds[:, YP - 1 : YP, :] = jnp.zeros((4, 1, W), F32)
+
+    lists[0:4] = near[0:4]
+    lists[4:8] = jnp.zeros((4, W), F32)
+    lists[2:3] = even_in[3, 0:1, :]
+    lists[3:4] = even_in[3, YP - 1 : YP, :]
 
     @pl.when(half == 0)
     def _():
@@ -355,72 +391,71 @@
     return lax.broadcasted_iota(jnp.int32, (BLOCKS, SAMPLES), 1) < limit
 
 
-def collect(source, owner, place, core, out):
-    half = place[0]
-    names = []
-    for z in range(2):
-        total = source[0, z, 16:24, W : 2 * W]
-        for n in range(1, 16):
-            total = total + source[n, z, 16:24, W : 2 * W]
-        names.append(total[0:1])
-    names = jnp.concatenate(names, axis=1)
-    target = lax.broadcasted_iota(jnp.int32, (16, 2 * W), 0)
-    lane = lax.broadcasted_iota(jnp.int32, (16, 2 * W), 1)
-    name = jnp.full((16, 2 * W), -1.0, F32)
-    spot = jnp.full((16, 2 * W), -1, jnp.int32)
-    for t in range(BLOCKS):
-        k = owner[t]
-        tiles = k // 2
-        sx, sy = tiles // 8, tiles % 8
-        where = ((sx % 2) ^ half) * W + ((sx // 2) * 4 + sy // 2) * 8 + 2 * (k % 2)
-        where = jnp.where(sy % 2 == core, where, -1024)
-        name = jnp.where(target == t, (k + 1).astype(F32), name)
-        spot = jnp.where(target == t, where, spot)
-    for t in range(2):
-        name = jnp.where(target == BLOCKS + t, (2 * place[4] + t + 1).astype(F32), name)
-    hit = (name == names).astype(jnp.bfloat16)
-    for r in range(2):
-        data = jnp.concatenate(
-            [source[n, z, 8 * r : 8 * r + 8, :] for z in range(2) for n in range(16)], axis=0
+def collect_kernel(place, lists, here, keep, send):
+    names = here[0, 16:24, W : 2 * W]
+    for n in range(1, 16):
+        names = names + here[n, 16:24, W : 2 * W]
+    names = jnp.broadcast_to(names[0:1], (8, W))
+    lane = lax.broadcasted_iota(jnp.int32, (8, W), 1)
+    row = lax.broadcasted_iota(jnp.int32, (8, W), 0)
+    hits, spots = [], []
+    for member in range(4):
+        tile = place[4] ^ (1 if member & 1 else 0) ^ (8 if member & 2 else 0)
+        held = jnp.broadcast_to(lists[member : member + 1], (8, W))
+        name = jnp.sum(jnp.where(lane == row, held, 0.0), axis=1, keepdims=True)
+        name = jnp.broadcast_to(name, (8, W))
+        hits.append(name == names)
+        hits.append((2 * tile + 1 + (row & 1)).astype(F32) == names)
+        block = name.astype(jnp.int32) - 1
+        holder = block >> 1
+        spot = ((holder >> 4) * 4 + ((holder >> 1) & 3)) * 8 + 2 * (block & 1)
+        mine = ((holder & 1) == place[1]) & (((holder >> 3) & 1) == place[0])
+        spots.append(jnp.where(mine, spot, -1024))
+    hit = jnp.concatenate([h.astype(F32) for h in hits], axis=0).astype(jnp.bfloat16)
+    spots = jnp.concatenate(spots, axis=0)
+    lane = lax.broadcasted_iota(jnp.int32, (32, W), 1)
+    choose = jnp.concatenate(
+        [(lane == spots + 4 * kind + h).astype(F32) for kind in range(2) for h in range(2)], axis=0
+    ).astype(jnp.bfloat16)
+
+    def gather(left, rows, lanes):
+        data = jnp.concatenate([here[n, rows, lanes] for n in range(16)], axis=0)
+        high, low = split(data)
+        return jnp.dot(left, high, preferred_element_type=F32) + jnp.dot(
+            left, low, preferred_element_type=F32
         )
-        high, low = split(data)
-        out[r] = jnp.dot(hit, high, preferred_element_type=F32) + jnp.dot(
-            hit, low, preferred_element_type=F32
-        )
-    data = jnp.concatenate([source[n, z, 16:24, 0:W] for z in range(2) for n in range(16)], axis=0)
-    high, low = split(data)
-    choose = jnp.concatenate(
-        [(lane == spot + 4 * kind + h).astype(jnp.bfloat16) for kind in range(2) for h in range(2)], axis=0
-    )
-    found = jnp.dot(choose, high, preferred_element_type=F32) + jnp.dot(
-        choose, low, preferred_element_type=F32
-    )
-    for kind in range(2):
-        for h in range(2):
-            row = 32 * kind + 16 * h
-            out[2 + kind, :, h * W : h * W + W] = found[row : row + 16]
-
-
-def collect_kernel(place, owner, here, out):
-    collect(here, owner, place, place[1], out)
+
+    totals = [gather(hit, slice(8 * r, 8 * r + 8), slice(0, 2 * W)) for r in range(2)]
+    found = gather(choose, slice(16, 24), slice(0, W))
+    row = lax.broadcasted_iota(jnp.int32, (8, SAMPLES), 0)
+    for member in range(4):
+        out = (send if member & 1 else keep).at[member // 2]
+        drill, gain = [
+            jnp.concatenate(
+                [found[64 * kind + 32 * h + 8 * member : 64 * kind + 32 * h + 8 * member + 8] for h in range(2)],
+                axis=1,
+            )
+            for kind in range(2)
+        ]
+        for r in range(2):
+            out[8 * r : 8 * r + 8, :] = drill - totals[r][16 * member : 16 * member + 8]
+        out[16:24, :] = gain
+        own = [totals[r][16 * member + 8 : 16 * member + 16] for r in range(2)]
+        out[24:32, :] = jnp.where(row < 2, own[0], own[1])
 
 
 def update_kernel(
-    place, node_block, owner, count, mine, there, smooth, matrix, rows,
+    node_block, count, keep, near, far, smooth, matrix, rows,
     out, misfit,
-    other, update,
+    update,
 ):
-    collect(there, owner, place, 1 - place[1], other)
+    sums = keep[0] + near[0] + far[...]
     for k in range(2):
         for r in range(2):
-            t = BLOCKS + k
-            misfit[k, r : r + 1, :] = rows[0, k : k + 1, :] - (mine[r, t : t + 1, :] + other[r, t : t + 1, :])
+            t = 24 + 2 * r + k
+            misfit[k, r : r + 1, :] = rows[0, k : k + 1, :] - sums[t : t + 1, :]
     live = is_live(count)
-    drill, gain = [mine[i, 0:BLOCKS, :] + other[i, 0:BLOCKS, :] for i in (2, 3)]
-    picked = [
-        jnp.where(live, gain * (drill - (mine[r, 0:BLOCKS, :] + other[r, 0:BLOCKS, :])), 0.0)
-        for r in range(2)
-    ]
+    picked = [jnp.where(live, sums[16:24] * sums[8 * r : 8 * r + 8], 0.0) for r in range(2)]
     pieces = [split(v) for v in picked]
     left = jnp.concatenate([pieces[0][0], pieces[1][0], pieces[0][1], pieces[1][1]], axis=0)
     block = lax.broadcasted_iota(jnp.int32, (BLOCKS, NODES), 0)
@@ -469,23 +504,32 @@
             lax.axis_index(("x", "zh", "y", "core")),
         ]
     ).astype(jnp.int32)
-
-    even, odd, doubled = call(
+    noise, classes, table, obs_matrix, owner, drill_data, obs_gain = [
+        pltpu.with_memory_space_constraint(a, pltpu.HBM)
+        for a in (noise, classes, table, obs_matrix, sample_block, drill_data, obs_gain)
+    ]
+
+    even, odd, near_noise, doubled, names = call(
         edge_y_kernel,
-        (shape(X, 4, W), shape(X, 4, W), shape(X, Y, W)),
-        [SMEM, VMEM, VMEM],
+        (shape(X + 1, 4, W), shape(X, 4, W), shape(X, Y, W), shape(X, Y, W), shape(8, W)),
+        [SMEM, HBM, HBM, HBM],
         "edge_y",
-    )(place, noise, classes)
+        [
+            pltpu.VMEM((X, Y, Z), jnp.int32),
+            pltpu.SMEM((BLOCKS,), jnp.int32),
+            pltpu.SemaphoreType.DMA((3,)),
+        ],
+    )(place, noise, classes, owner)
+    even = permute(even, ("y", "core"), even_pair)
     odd = permute(odd, ("y", "core"), odd_pair)
-    even = permute(even, ("y", "core"), even_pair)
-    field, kinds, even, odd = call(
+    field, kinds, even, odd, lists = call(
         edge_x_kernel,
-        (shape(X, YP, W), shape(X, YP, W), shape(4, YP, W), shape(4, YP, W)),
-        [SMEM] + [VMEM] * 4,
+        (shape(X, YP, W), shape(X, YP, W), shape(4, YP, W), shape(4, YP, W), shape(4, W)),
+        [SMEM] + [VMEM] * 5,
         "edge_x",
-    )(place, noise, doubled, even, odd)
+    )(place, near_noise, doubled, names, even, odd)
+    even = permute(even, ("x", "zh"), even_pair)
     odd = permute(odd, ("x", "zh"), odd_pair)
-    even = permute(even, ("x", "zh"), even_pair)
     weights, first, second, third, middle, tables, matrix, rows = call(
         interior_kernel,
         (
@@ -498,14 +542,14 @@
             shape(BLOCKS, SAMPLES, NODES, dtype=jnp.bfloat16),
             shape(2, 2, SAMPLES),
         ),
-        [VMEM] * 3 + [HBM] * 3,
+        [VMEM] * 2 + [HBM] * 4,
         "interior",
-        [pltpu.SemaphoreType.DMA((3,))],
+        [pltpu.VMEM((8, 27), F32), pltpu.SemaphoreType.DMA((4,))],
     )(field, kinds, table, obs_matrix, drill_data, obs_gain)
-    smooth, payload = call(
+    smooth, payload, lists = call(
         finish_kernel,
-        (shape(32, 8, W), shape(ROWS, SAMPLES)),
-        [SMEM] * 4 + [VMEM] * 11,
+        (shape(32, 8, W), shape(ROWS, SAMPLES), shape(8, W)),
+        [SMEM] * 4 + [VMEM] * 12,
         "finish",
         [
             pltpu.VMEM((6, YP, W), F32),
@@ -517,25 +561,24 @@
             pltpu.VMEM((64, W), F32),
         ],
     )(
-        place, node_block, sample_count, sample_block, kinds, even, odd,
+        place, node_block, sample_count, sample_block, kinds, even, odd, lists,
         weights, first, second, third, middle, tables, matrix, rows,
     )
-    other = permute(payload, ("zh",), lambda z: (z ^ 1,))
-    pair = jnp.stack([payload, other])
     here = lax.all_to_all(
-        jnp.broadcast_to(pair[None], (16, 2, ROWS, SAMPLES)), ("x", "y"), 0, 0, tiled=True
+        jnp.broadcast_to(payload[None], (16, ROWS, SAMPLES)), ("x", "y"), 0, 0, tiled=True
     )
-    there = permute(here, ("core",), lambda c: (c ^ 1,))
-    (mine,) = call(collect_kernel, (shape(4, 16, SAMPLES),), [SMEM, SMEM, VMEM], "collect")(
-        place, sample_block, here
-    )
+    keep, send = call(
+        collect_kernel, (shape(2, 32, SAMPLES), shape(2, 32, SAMPLES)), [SMEM, VMEM, VMEM], "collect"
+    )(place, lists, here)
+    near = permute(send, ("core",), lambda c: (c ^ 1,))
+    far = permute(keep[1] + near[1], ("zh",), lambda z: (z ^ 1,))
     out, misfit = call(
         update_kernel,
         (shape(32, 8, W), shape(2, 2, SAMPLES)),
-        [SMEM] * 4 + [VMEM] * 5,
+        [SMEM] * 2 + [VMEM] * 6,
         "update",
-        [pltpu.VMEM((4, 16, SAMPLES), F32), pltpu.VMEM((64, W), F32)],
-    )(place, node_block, sample_block, sample_count, mine, there, smooth, matrix, rows)
+        [pltpu.VMEM((64, W), F32)],
+    )(node_block, sample_count, keep, near, far, smooth, matrix, rows)
     return out.reshape(X, Y, W), misfit
 
 

time: 63.5 us -> 58.9 us (0.928)
  starting transfers between devices: 23.9 us -> 15.3 us
  waiting for transfers between devices: 5.38 us -> 10.9 us
  local copies, waits for them, and re-layouts: 5.62 us -> 0.14 us
  blocking collectives: 19.3 us -> 22.1 us
  Pallas kernels: 8.22 us -> 9.41 us
    ppermute x6, starting transfers between devices: 23.9 us -> 15.3 us  [permute(): return lax.ppermute(value, axes if len(axes) > 1 else axes[0], pairs)]
    ppermute x6, waiting for transfers between devices: 5.38 us -> 10.9 us  [permute(): return lax.ppermute(value, axes if len(axes) > 1 else axes[0], pairs)]
    unnamed x18 -> x6, local copies, waits for them, and re-layouts: 5.46 us -> 0.01 us
    all_to_all x1, blocking collectives: 19.3 us -> 22.1 us  [shards(): lax.all_to_all(jnp.broadcast_to(payload[None], (16, ROWS, SAMPLES)), ('x'...]
  transfers between devices with their start and end apart: 6 -> 6, of which waited for: 3 -> 4; matrix products, arithmetic and copies ran while one was open for 0% -> 0% of each run, Pallas kernels for 4% -> 3%
where the time goes in v3:
time: 58.9 us; the launch traced here: 58.6 us
  blocking collectives  22.1 us (38%)
  starting transfers between devices  15.3 us (26%)
  waiting for transfers between devices  10.9 us (19%)
  Pallas kernels  9.41 us (16%)
  between operations  0.74 us (1%)
    all_to_all x1, blocking collectives, shards(): lax.all_to_all(jnp.broadcast_to(payload[None], (16, ROWS, SAMPLES)), ('x'...  22.1 us
    ppermute x6, starting transfers between devices, permute(): return lax.ppermute(value, axes if len(axes) > 1 else axes[0], pairs)  15.3 us
    ppermute x6, waiting for transfers between devices, permute(): return lax.ppermute(value, axes if len(axes) > 1 else axes[0], pairs)  10.9 us
    pallas_call x1, Pallas kernels, shards(): call(finish_kernel, (shape(32, 8, W), shape(ROWS, SAMPLES), shape(8, W)),...  2.59 us
    pallas_call x1, Pallas kernels, shards(): call(interior_kernel, (shape(27, X, YP, W), shape(3, X, YP, W), shape(3,...  1.94 us
    pallas_call x1, Pallas kernels, shards(): call(update_kernel, (shape(32, 8, W), shape(2, 2, SAMPLES)), [SMEM] * 2 +...  1.76 us
    pallas_call x1, Pallas kernels, shards(): call(edge_y_kernel, (shape(X + 1, 4, W), shape(X, 4, W), shape(X, Y, W),...  1.66 us
  transfers between devices with their start and end apart: 6, of which 4 were waited for; matrix products, arithmetic and copies ran while one was open for 0% of the time, Pallas kernels for 3%

profile of v3, /device:TPU:1, one launch (start us, length us, event | category | flops | bytes accessed | tf_op | source)
XLA Modules:
  0.0 58.6 jit_solution(16893243732318852922)
XLA Ops:
  0.6 0.0 copy-start
  0.6 0.0 copy-start.2
  0.7 0.0 copy-start.1
  0.7 0.1 stack.20.place
  0.8 1.7 %edge_y.1 = (f32[9,4,128]{2,1,0:T(4,128)S(1)}, f32[8,4,128]{2,1,0:T(4,128)S(1)}, f32[8,32,128]{2,1,0:T(8,128)S(1)}, f32[8,32,128]{2,1,0:T(8,128)S(1)}, f32[8,128]{1,0:T(8,128)S(1)}) custom-call(s32[5]{0:T(128)S(1)} %stack.20.place, f32[8,32,128]{2,1,0:T(8,128)} %noise_far.1, s32[8,32,64]{2,1,0:T(8,128)} %classes_far.1, s32[8]{0:T(128)} %owner.1), custom_call_target="tpu_custom_call" | custom-call | tf_op jit(solution)/shard_map/edge_y/pallas_call | solution.py:512
  2.4 3.3 %collective-permute-start = (f32[9,4,128]{2,1,0:T(4,128)S(1)}, f32[9,4,128]{2,1,0:T(4,128)S(1)}, u32[]{:S(2)}, u32[]{:S(2)}) collective-permute-start(f32[9,4,128]{2,1,0:T(4,128)S(1)} %get-tuple-element.30), channel_id=1, source_target_pairs={{0,1},{1,0},{2,3},{3,2},{4,5},{5,4},{6,7},{7,6},{8,9},{9,8},{10,11... | collective-permute-start | bytes 55304 | tf_op jit(solution)/shard_map/ppermute | solution.py:40
  5.8 1.9 %collective-permute-start.1 = (f32[8,4,128]{2,1,0:T(4,128)S(1)}, f32[8,4,128]{2,1,0:T(4,128)S(1)}, u32[]{:S(2)}, u32[]{:S(2)}) collective-permute-start(f32[8,4,128]{2,1,0:T(4,128)S(1)} %get-tuple-element.31), channel_id=1, source_target_pairs={{1,2},{2,1},{3,4},{4,3},{5,6},{6,5},{9,10},{10,9},{11,12},{12,11},... | collective-permute-start | bytes 49160 | tf_op jit(solution)/shard_map/ppermute | solution.py:40
  7.7 3.1 %collective-permute-done.1.odd_in = f32[8,4,128]{2,1,0:T(4,128)S(1)} collective-permute-done((f32[8,4,128]{2,1,0:T(4,128)S(1)}, f32[8,4,128]{2,1,0:T(4,128)S(1)}, u32[]{:S(2)}, u32[]{:S(2)}) %collective-permute-start.1) | collective-permute-done | bytes 16416 | tf_op jit(solution)/shard_map/ppermute | solution.py:40
  10.8 0.0 collective-permute-done.even_in
  10.8 0.7 %edge_x.1 = (f32[8,40,128]{2,1,0:T(8,128)S(1)}, f32[8,40,128]{2,1,0:T(8,128)S(1)}, f32[4,40,128]{2,1,0:T(8,128)S(1)}, f32[4,40,128]{2,1,0:T(8,128)S(1)}, f32[4,128]{1,0:T(4,128)S(1)}) custom-call(s32[5]{0:T(128)S(1)} %stack.20.place, f32[8,32,128]{2,1,0:T(8,128)S(1)} %get-tuple-element.27.noise, f32[8,32,128]{2,1,0:T(8,128)S(1)} %get-tuple-element.28.doubled, ...), custom_call_target="tpu_custom_call" | custom-call | tf_op jit(solution)/shard_map/edge_x/pallas_call | solution.py:525
  11.5 5.3 %collective-permute-start.2 = (f32[4,40,128]{2,1,0:T(8,128)S(1)}, f32[4,40,128]{2,1,0:T(8,128)S(1)}, u32[]{:S(2)}, u32[]{:S(2)}) collective-permute-start(f32[4,40,128]{2,1,0:T(8,128)S(1)} %get-tuple-element.33), channel_id=1, source_target_pairs={{0,8},{8,0},{16,24},{24,16},{32,40},{40,32},{48,56},{56,48},{1,9},... | collective-permute-start | bytes 245768 | tf_op jit(solution)/shard_map/ppermute | solution.py:40
  16.7 0.7 %collective-permute-start.3 = (f32[4,40,128]{2,1,0:T(8,128)S(1)}, f32[4,40,128]{2,1,0:T(8,128)S(1)}, u32[]{:S(2)}, u32[]{:S(2)}) collective-permute-start(f32[4,40,128]{2,1,0:T(8,128)S(1)} %get-tuple-element.34), channel_id=1, source_target_pairs={{8,16},{16,8},{24,32},{32,24},{40,48},{48,40},{9,17},{17,9},{25,33... | collective-permute-start | bytes 245768 | tf_op jit(solution)/shard_map/ppermute | solution.py:40
  17.4 1.9 %interior.1 = (f32[27,8,40,128]{3,2,1,0:T(8,128)S(1)}, f32[3,8,40,128]{3,2,1,0:T(8,128)S(1)}, f32[3,6,40,128]{3,2,1,0:T(8,128)S(1)}, f32[3,4,40,128]{3,2,1,0:T(8...) custom-call(f32[8,40,128]{2,1,0:T(8,128)S(1)} %get-tuple-element.36., ...), custom_call_target="tpu_custom_call" | custom-call | tf_op jit(solution)/shard_map/interior/pallas_call | solution.py:533
  19.3 0.3 collective-permute-done.2.even_in
  19.6 0.0 collective-permute-done.3.odd_in
  19.6 0.0 copy-done
  19.6 0.0 copy-done.2
  19.7 0.0 copy-done.1
  19.7 2.6 %finish.1 = (f32[32,8,128]{2,1,0:T(8,128)S(1)}, f32[24,256]{1,0:T(8,128)S(1)}, f32[8,128]{1,0:T(8,128)S(1)}) custom-call(s32[5]{0:T(128)S(1)} %stack.20.place, s32[8]{0:T(128)S(1)} %copy-done.1, s32[8]{0:T(128)S(1)} %copy-done.2, s32[8]{0:T(128)S(1)} %copy-done, f32[8,40,128]{2,1,0:T(8,128)S(1)} %get-tuple-element.32.kinds, ...), custom_call_target="tpu_custom_call" | custom-call | tf_op jit(solution)/shard_map/finish/pallas_call | solution.py:549
  22.3 22.1 %all_to_all.5.here = f32[16,24,256]{2,1,0:T(8,128)S(1)} all-to-all(f32[16,24,256]{2,1,0:T(8,128)S(1)} %broadcast_in_dim.2), channel_id=1, replica_groups=mesh['real'=4,'x'=4,'zh'=2,'y'=4,'core'=2] {'x','y'}, dimensions={0} | all-to-all | bytes 786432 | tf_op jit(solution)/shard_map/all_to_all | solution.py:567
  44.4 0.8 %collect.1 = (f32[2,32,256]{2,1,0:T(8,128)S(1)}, f32[2,32,256]{2,1,0:T(8,128)S(1)}) custom-call(s32[5]{0:T(128)S(1)} %stack.20.place, f32[8,128]{1,0:T(8,128)S(1)} %get-tuple-element.45.lists, f32[16,24,256]{2,1,0:T(8,128)S(1)} %all_to_all.5.here), custom_call_target="tpu_custom_call" | custom-call | tf_op jit(solution)/shard_map/collect/pallas_call | solution.py:570
  45.2 4.1 %collective-permute-start.4 = (f32[2,32,256]{2,1,0:T(8,128)S(1)}, f32[2,32,256]{2,1,0:T(8,128)S(1)}, u32[]{:S(2)}, u32[]{:S(2)}) collective-permute-start(f32[2,32,256]{2,1,0:T(8,128)S(1)} %get-tuple-element.48), channel_id=1, source_target_pairs={{0,1},{1,0},{2,3},{3,2},{4,5},{5,4},{6,7},{7,6},{8,9},{9,8},{10,11... | collective-permute-start | bytes 196616 | tf_op jit(solution)/shard_map/ppermute | solution.py:40
  49.3 0.9 %collective-permute-done.4.near = f32[2,32,256]{2,1,0:T(8,128)S(1)} collective-permute-done((f32[2,32,256]{2,1,0:T(8,128)S(1)}, f32[2,32,256]{2,1,0:T(8,128)S(1)}, u32[]{:S(2)}, u32[]{:S(2)}) %collective-permute-start.4) | collective-permute-done | bytes 65568 | tf_op jit(solution)/shard_map/ppermute | solution.py:40
  50.2 0.1 collective-permute-start.5
  50.3 6.6 %collective-permute-done.5.far = f32[32,256]{1,0:T(8,128)S(1)} collective-permute-done((f32[32,256]{1,0:T(8,128)S(1)}, f32[32,256]{1,0:T(8,128)S(1)}, u32[]{:S(2)}, u32[]{:S(2)}) %collective-permute-start.5) | collective-permute-done | bytes 32800 | tf_op jit(solution)/shard_map/ppermute | solution.py:40
  56.9 1.8 %update.1 = (f32[32,8,128]{2,1,0:T(8,128)}, f32[2,2,256]{2,1,0:T(2,128)}) custom-call(s32[8]{0:T(128)S(1)} %copy-done.1, s32[8]{0:T(128)S(1)} %copy-done.2, f32[2,32,256]{2,1,0:T(8,128)S(1)} %get-tuple-element.47.keep, f32[2,32,256]{2,1,0:T(8,128)S(1)} %collective-permute-done.4.near, f32[32,256]{1,0:T(8,128)S(1)} %collective-permute-done.5.far, ...), custom_call_target="tpu_custom_call" | custom-call | tf_op jit(solution)/shard_map/update/pallas_call | solution.py:575
  (2 shorter events, 0.0 us)
Async XLA Ops:
  0.6 19.0 %copy-start = (s32[8]{0:T(128)S(1)}, s32[8]{0:T(128)}, u32[]{:S(2)}) copy-start(s32[8]{0:T(128)} %owner.1) | copy-start | bytes 100
  0.6 19.0 %copy-start.2 = (s32[8]{0:T(128)S(1)}, s32[8]{0:T(128)}, u32[]{:S(2)}) copy-start(s32[8]{0:T(128)} %count.3) | copy-start | bytes 100
  0.7 19.0 %copy-start.1 = (s32[8]{0:T(128)S(1)}, s32[8]{0:T(128)}, u32[]{:S(2)}) copy-start(s32[8]{0:T(128)} %node_block.3) | copy-start | bytes 100
  2.4 8.4 %collective-permute-start = (f32[9,4,128]{2,1,0:T(4,128)S(1)}, f32[9,4,128]{2,1,0:T(4,128)S(1)}, u32[]{:S(2)}, u32[]{:S(2)}) collective-permute-start(f32[9,4,128]{2,1,0:T(4,128)S(1)} %get-tuple-element.30), channel_id=1, source_target_pairs={{0,1},{1,0},{2,3},{3,2},{4,5},{5,4},{6,7},{7,6},{8,9},{9,8},{10,11... | collective-permute-start | bytes 55304 | tf_op jit(solution)/shard_map/ppermute | solution.py:40
  5.8 5.0 %collective-permute-start.1 = (f32[8,4,128]{2,1,0:T(4,128)S(1)}, f32[8,4,128]{2,1,0:T(4,128)S(1)}, u32[]{:S(2)}, u32[]{:S(2)}) collective-permute-start(f32[8,4,128]{2,1,0:T(4,128)S(1)} %get-tuple-element.31), channel_id=1, source_target_pairs={{1,2},{2,1},{3,4},{4,3},{5,6},{6,5},{9,10},{10,9},{11,12},{12,11},... | collective-permute-start | bytes 49160 | tf_op jit(solution)/shard_map/ppermute | solution.py:40
  11.5 8.2 %collective-permute-start.2 = (f32[4,40,128]{2,1,0:T(8,128)S(1)}, f32[4,40,128]{2,1,0:T(8,128)S(1)}, u32[]{:S(2)}, u32[]{:S(2)}) collective-permute-start(f32[4,40,128]{2,1,0:T(8,128)S(1)} %get-tuple-element.33), channel_id=1, source_target_pairs={{0,8},{8,0},{16,24},{24,16},{32,40},{40,32},{48,56},{56,48},{1,9},... | collective-permute-start | bytes 245768 | tf_op jit(solution)/shard_map/ppermute | solution.py:40
  16.7 2.9 %collective-permute-start.3 = (f32[4,40,128]{2,1,0:T(8,128)S(1)}, f32[4,40,128]{2,1,0:T(8,128)S(1)}, u32[]{:S(2)}, u32[]{:S(2)}) collective-permute-start(f32[4,40,128]{2,1,0:T(8,128)S(1)} %get-tuple-element.34), channel_id=1, source_target_pairs={{8,16},{16,8},{24,32},{32,24},{40,48},{48,40},{9,17},{17,9},{25,33... | collective-permute-start | bytes 245768 | tf_op jit(solution)/shard_map/ppermute | solution.py:40
  45.2 5.0 %collective-permute-start.4 = (f32[2,32,256]{2,1,0:T(8,128)S(1)}, f32[2,32,256]{2,1,0:T(8,128)S(1)}, u32[]{:S(2)}, u32[]{:S(2)}) collective-permute-start(f32[2,32,256]{2,1,0:T(8,128)S(1)} %get-tuple-element.48), channel_id=1, source_target_pairs={{0,1},{1,0},{2,3},{3,2},{4,5},{5,4},{6,7},{7,6},{8,9},{9,8},{10,11... | collective-permute-start | bytes 196616 | tf_op jit(solution)/shard_map/ppermute | solution.py:40
  50.2 6.7 %collective-permute-start.5 = (f32[32,256]{1,0:T(8,128)S(1)}, f32[32,256]{1,0:T(8,128)S(1)}, u32[]{:S(2)}, u32[]{:S(2)}) collective-permute-start(f32[32,256]{1,0:T(8,128)S(1)} %fusion), channel_id=1, source_target_pairs={{0,8},{8,0},{1,9},{9,1},{2,10},{10,2},{3,11},{11,3},{4,12},{12,4},... | collective-permute-start | bytes 98312 | tf_op jit(solution)/shard_map/ppermute | solution.py:40

commit v4 on v3

--- a/solution.py
+++ b/solution.py
@@ -112,28 +112,28 @@
 
 
 def edge_x_kernel(
-    place, noise, doubled, names, even_in, odd_in, field, kinds, even, odd, lists
+    place, noise, doubled, names, even_in, odd_in,
+    field, kinds, odd, even, lists,
+    true_field, true_kinds,
 ):
     core, half = place[1], place[0]
-    field[:, 0:8, :] = jnp.zeros((X, 8, W), F32)
-    field[:, 32:40, :] = jnp.zeros((X, 8, W), F32)
-    kinds[:, 0:8, :] = jnp.zeros((X, 8, W), F32)
-    kinds[:, 32:40, :] = jnp.zeros((X, 8, W), F32)
-    field[:, OFF : OFF + Y, :] = noise[...]
-    kinds[:, OFF : OFF + Y, :] = doubled[...]
-
+    for out in (true_field, true_kinds):
+        out[:, 0:8, :] = jnp.zeros((X, 8, W), F32)
+        out[:, 32:40, :] = jnp.zeros((X, 8, W), F32)
+    true_field[:, OFF : OFF + Y, :] = noise[...]
+    true_kinds[:, OFF : OFF + Y, :] = doubled[...]
     lists[0:4] = names[0:4]
     lists[1:2] = even_in[X, 0:1, :]
 
     def sides(low, high):
-        field[:, 1:4, :] = low[0:X, 0:3, :]
+        true_field[:, 1:4, :] = low[0:X, 0:3, :]
         first, second = unpack(low[0:X, 3:4, :])
-        kinds[:, 2:3, :] = first
-        kinds[:, 3:4, :] = second
-        field[:, 36:39, :] = high[0:X, 0:3, :]
+        true_kinds[:, 2:3, :] = first
+        true_kinds[:, 3:4, :] = second
+        true_field[:, 36:39, :] = high[0:X, 0:3, :]
         first, second = unpack(high[0:X, 3:4, :])
-        kinds[:, 36:37, :] = first
-        kinds[:, 37:38, :] = second
+        true_kinds[:, 36:37, :] = first
+        true_kinds[:, 37:38, :] = second
 
     @pl.when(core == 0)
     def _():
@@ -143,26 +143,21 @@
     def _():
         sides(even_in, odd_in)
 
-    def low(out):
-        out[0:3] = field[0:3]
-        out[3] = pack(kinds[0], kinds[1])
-
-    def high(out):
-        out[0:3] = field[X - 3 : X]
-        out[3] = pack(kinds[X - 2], kinds[X - 1])
-
-    @pl.when(half == 0)
-    def _():
-        high(even)
-        low(odd)
-
-    @pl.when(half == 1)
-    def _():
-        low(even)
-        high(odd)
-
+    for x in range(X):
+        true = mirrored(x, half)
+        field[x] = true_field[true]
+        kinds[x] = true_kinds[true]
+    for n in range(3):
+        even[n] = field[X - 1 - n]
+        odd[n] = field[n]
+    even[3] = pack(kinds[X - 1], kinds[X - 2])
+    odd[3] = pack(kinds[0], kinds[1])
     even[3, 0:1, :] = lists[0:1]
     even[3, YP - 1 : YP, :] = lists[1:2]
+
+
+def mirrored(x, half):
+    return x + half * (X - 1 - 2 * x)
 
 
 def rows_by_column(block_rows):
@@ -191,10 +186,11 @@
                     )
 
 
-def spread_table(table, out):
+def spread_table(table, half, out):
     held = table[...]
+    columns = [jnp.broadcast_to(held[:, o : o + 1], (8, W)) for o in range(27)]
     for o in range(27):
-        out[o] = jnp.broadcast_to(held[:, o : o + 1], (8, W))
+        out[o] = jnp.where(half == 0, columns[o], columns[o + 9 * (2 - 2 * (o // 9))])
 
 
 def lean(row):
@@ -218,7 +214,7 @@
 
 
 def interior_kernel(
-    field, kinds, table, matrix, drill, gain,
+    place, field, kinds, table, matrix, drill, gain,
     weights, first, second, third, smooth, tables, held_matrix, held_rows,
     held_table, sems,
 ):
@@ -231,7 +227,7 @@
     for copy in reversed(copies):
         copy.start()
     copies[3].wait()
-    spread_table(held_table, tables)
+    spread_table(held_table, place[0], tables)
     for x in range(X):
         def put(o, rows, value, x=x):
             weights[o, x, rows, :] = value
@@ -265,86 +261,107 @@
         copy.wait()
 
 
-def finish_kernel(
-    place, node_block, count, owner, kinds, even_in, odd_in, near,
-    weights, first, second, third, middle, tables, matrix, rows,
-    smooth, payload, lists,
-    halo, halo_kinds, halo_weights, edge_first, edge_second, edge_third, chosen,
-):
-    half = place[0]
-
-    def sides(low, high):
-        halo[0:3] = low[0:3]
-        halo[3:6] = high[0:3]
-        one, two = unpack(low[3])
-        halo_kinds[0], halo_kinds[1] = one, two
-        one, two = unpack(high[3])
-        halo_kinds[2], halo_kinds[3] = one, two
-        halo_kinds[:, 0:1, :] = jnp.zeros((4, 1, W), F32)
-        halo_kinds[:, YP - 1 : YP, :] = jnp.zeros((4, 1, W), F32)
-
-    lists[0:4] = near[0:4]
-    lists[4:8] = jnp.zeros((4, W), F32)
-    lists[2:3] = even_in[3, 0:1, :]
-    lists[3:4] = even_in[3, YP - 1 : YP, :]
-
-    @pl.when(half == 0)
-    def _():
-        sides(odd_in, even_in)
-
-    @pl.when(half == 1)
-    def _():
-        sides(even_in, odd_in)
-
-    smooth[12:20] = middle[...]
-    for i in range(4):
+def fill_halo(message, tables, halo_kinds, halo_weights, halo_first):
+    one, two = unpack(message[3])
+    halo_kinds[0], halo_kinds[1] = one, two
+    halo_kinds[:, 0:1, :] = jnp.zeros((2, 1, W), F32)
+    halo_kinds[:, YP - 1 : YP, :] = jnp.zeros((2, 1, W), F32)
+    for i in range(2):
         def put(o, part, value, i=i):
             halo_weights[o, i, part, :] = value
 
         weigh(halo_kinds[i], tables, put)
-    for i in range(6):
-        for c, value in enumerate(lean(halo[i])):
-            edge_first[c, i] = value
+    for i in range(3):
+        for c, value in enumerate(lean(message[i])):
+            halo_first[c, i] = value
+
+
+def side(
+    high, kinds, weights, first, second, third, halo_kinds, halo_weights, halo_first, edge_second, edge_third, put
+):
+    def beyond(x):
+        return x - X if high else -1 - x
 
     def weight(x):
         if 0 <= x < X:
             return (lambda o: weights[o, x]), jnp.minimum(kinds[x], 1.0)
-        i = x + 2 if x < 0 else x - 6
+        i = beyond(x)
         return (lambda o: halo_weights[o, i]), jnp.minimum(halo_kinds[i], 1.0)
 
     def at_first(x, c):
-        if 0 <= x < X:
-            return first[c, x]
-        return edge_first[c, x + 3 if x < 0 else x - 5]
+        return first[c, x] if 0 <= x < X else halo_first[c, beyond(x)]
 
     def at_second(x, c):
-        if 1 <= x < 7:
-            return second[c, x - 1]
-        return edge_second[c, x + 2 if x < 1 else x - 4]
+        return second[c, x - 1] if 1 <= x < 7 else edge_second[c, beyond(x) + 1]
 
     def at_third(x, c):
-        if 2 <= x < 6:
-            return third[c, x - 2]
-        return edge_third[c, x + 1 if x < 2 else x - 3]
+        return third[c, x - 2] if 2 <= x < 6 else edge_third[c, beyond(x) + 2]
 
     def step(at, x):
         of, inside = weight(x)
         return operate(of, lambda a, c: at(x + a - 1, c), inside)
 
-    for x in (-2, -1, 0, 7, 8, 9):
-        for c, value in enumerate(lean(step(at_first, x))):
-            edge_second[c, x + 2 if x < 1 else x - 4] = value
-    for x in (-1, 0, 1, 6, 7, 8):
-        value = 2.0 * step(at_second, x) - at_first(x, 1)
+    def row(n):
+        return X - 1 - n if high else n
+
+    for n in (-2, -1, 0):
+        for c, value in enumerate(lean(step(at_first, row(n)))):
+            edge_second[c, -n] = value
+    for n in (-1, 0, 1):
+        value = 2.0 * step(at_second, row(n)) - at_first(row(n), 1)
         for c, value in enumerate(lean(value)):
-            edge_third[c, x + 1 if x < 2 else x - 3] = value
-    for x in (0, 1, 2, 5, 6, 7):
+            edge_third[c, 1 - n] = value
+    for n in (0, 1, 2):
+        x = row(n)
         fourth = 2.0 * step(at_third, x) - at_second(x, 1)
         result = (
             CHEB[0] * at_first(x, 1) + CHEB[1] * at_second(x, 1) + CHEB[2] * at_third(x, 1) + CHEB[3] * fourth
         )
         for g in range(4):
-            smooth[4 * x + g] = result[OFF + 8 * g : OFF + 8 * g + 8]
+            put(x, g, result[OFF + 8 * g : OFF + 8 * g + 8])
+
+
+def lower_kernel(
+    kinds, edges, weights, first, second, third, tables,
+    lower,
+    halo_kinds, halo_weights, halo_first, edge_second, edge_third,
+):
+    fill_halo(edges, tables, halo_kinds, halo_weights, halo_first)
+
+    def put(x, g, value):
+        lower[4 * x + g] = value
+
+    side(
+        False, kinds, weights, first, second, third,
+        halo_kinds, halo_weights, halo_first, edge_second, edge_third, put,
+    )
+
+
+def finish_kernel(
+    place, node_block, count, owner, kinds, edges, near,
+    weights, first, second, third, middle, lower, tables, matrix, rows,
+    smooth, payload, lists,
+    halo_kinds, halo_weights, halo_first, edge_second, edge_third, chosen,
+):
+    half = place[0]
+    lists[0:4] = near[0:4]
+    lists[4:8] = jnp.zeros((4, W), F32)
+    lists[2:3] = edges[3, 0:1, :]
+    lists[3:4] = edges[3, YP - 1 : YP, :]
+    fill_halo(edges, tables, halo_kinds, halo_weights, halo_first)
+
+    def put(x, g, value):
+        smooth[4 * mirrored(x, half) + g] = value
+
+    side(
+        True, kinds, weights, first, second, third,
+        halo_kinds, halo_weights, halo_first, edge_second, edge_third, put,
+    )
+    for g in range(4):
+        for x in (0, 1, 2):
+            put(x, g, lower[4 * x + g])
+        for x in (3, 4):
+            put(x, g, middle[4 * (x - 3) + g])
 
     for b in range(BLOCKS):
         chosen[pl.ds(8 * b, 8), :] = smooth[node_block[b]]
@@ -522,14 +539,15 @@
     )(place, noise, classes, owner)
     even = permute(even, ("y", "core"), even_pair)
     odd = permute(odd, ("y", "core"), odd_pair)
-    field, kinds, even, odd, lists = call(
+    field, kinds, odd, even, lists = call(
         edge_x_kernel,
         (shape(X, YP, W), shape(X, YP, W), shape(4, YP, W), shape(4, YP, W), shape(4, W)),
         [SMEM] + [VMEM] * 5,
         "edge_x",
+        [pltpu.VMEM((X, YP, W), F32), pltpu.VMEM((X, YP, W), F32)],
     )(place, near_noise, doubled, names, even, odd)
+    odd = permute(odd, ("x", "zh"), odd_pair)
     even = permute(even, ("x", "zh"), even_pair)
-    odd = permute(odd, ("x", "zh"), odd_pair)
     weights, first, second, third, middle, tables, matrix, rows = call(
         interior_kernel,
         (
@@ -542,27 +560,29 @@
             shape(BLOCKS, SAMPLES, NODES, dtype=jnp.bfloat16),
             shape(2, 2, SAMPLES),
         ),
-        [VMEM] * 2 + [HBM] * 4,
+        [SMEM] + [VMEM] * 2 + [HBM] * 4,
         "interior",
         [pltpu.VMEM((8, 27), F32), pltpu.SemaphoreType.DMA((4,))],
-    )(field, kinds, table, obs_matrix, drill_data, obs_gain)
+    )(place, field, kinds, table, obs_matrix, drill_data, obs_gain)
+    halo_scratch = [
+        pltpu.VMEM((2, YP, W), F32),
+        pltpu.VMEM((27, 2, YP, W), F32),
+        pltpu.VMEM((3, 3, YP, W), F32),
+        pltpu.VMEM((3, 3, YP, W), F32),
+        pltpu.VMEM((3, 3, YP, W), F32),
+    ]
+    (lower,) = call(lower_kernel, (shape(12, 8, W),), [VMEM] * 7, "lower", halo_scratch)(
+        kinds, odd, weights, first, second, third, tables
+    )
     smooth, payload, lists = call(
         finish_kernel,
         (shape(32, 8, W), shape(ROWS, SAMPLES), shape(8, W)),
         [SMEM] * 4 + [VMEM] * 12,
         "finish",
-        [
-            pltpu.VMEM((6, YP, W), F32),
-            pltpu.VMEM((4, YP, W), F32),
-            pltpu.VMEM((27, 4, YP, W), F32),
-            pltpu.VMEM((3, 6, YP, W), F32),
-            pltpu.VMEM((3, 6, YP, W), F32),
-            pltpu.VMEM((3, 6, YP, W), F32),
-            pltpu.VMEM((64, W), F32),
-        ],
+        halo_scratch + [pltpu.VMEM((64, W), F32)],
     )(
-        place, node_block, sample_count, sample_block, kinds, even, odd, lists,
-        weights, first, second, third, middle, tables, matrix, rows,
+        place, node_block, sample_count, sample_block, kinds, even, lists,
+        weights, first, second, third, middle, lower, tables, matrix, rows,
     )
     here = lax.all_to_all(
         jnp.broadcast_to(payload[None], (16, ROWS, SAMPLES)), ("x", "y"), 0, 0, tiled=True

time: 58.9 us -> 57.5 us (0.976)
  starting transfers between devices: 15.3 us -> 19.8 us
  waiting for transfers between devices: 10.9 us -> 7.59 us
  blocking collectives: 22.1 us -> 19 us
    ppermute x6, starting transfers between devices: 15.3 us -> 19.8 us  [permute(): return lax.ppermute(value, axes if len(axes) > 1 else axes[0], pairs)]
    ppermute x6, waiting for transfers between devices: 10.9 us -> 7.59 us  [permute(): return lax.ppermute(value, axes if len(axes) > 1 else axes[0], pairs)]
    all_to_all x1, blocking collectives: 22.1 us -> 19 us  [shards(): lax.all_to_all(jnp.broadcast_to(payload[None], (16, ROWS, SAMPLES)), ('x'...]
    pallas_call x0 -> x1, Pallas kernels: none -> 0.72 us  [shards(): call(lower_kernel, (shape(12, 8, W),), [VMEM] * 7, 'lower', halo_scratch)]
    pallas_call x1, Pallas kernels: 2.59 us -> 1.9 us  [shards(): call(finish_kernel, (shape(32, 8, W), shape(ROWS, SAMPLES), shape(8, W)),...]
  transfers between devices with their start and end apart: 6 -> 6, of which waited for: 4 -> 3; matrix products, arithmetic and copies ran while one was open for 0% -> 0% of each run, Pallas kernels for 3% -> 5%
where the time goes in v4:
time: 57.5 us; the launch traced here: 57.3 us
  starting transfers between devices  19.8 us (34%)
  blocking collectives  19 us (33%)
  Pallas kernels  9.95 us (17%)
  waiting for transfers between devices  7.59 us (13%)
  between operations  0.77 us (1%)
    ppermute x6, starting transfers between devices, permute(): return lax.ppermute(value, axes if len(axes) > 1 else axes[0], pairs)  19.8 us
    all_to_all x1, blocking collectives, shards(): lax.all_to_all(jnp.broadcast_to(payload[None], (16, ROWS, SAMPLES)), ('x'...  19 us
    ppermute x6, waiting for transfers between devices, permute(): return lax.ppermute(value, axes if len(axes) > 1 else axes[0], pairs)  7.59 us
    pallas_call x1, Pallas kernels, shards(): call(interior_kernel, (shape(27, X, YP, W), shape(3, X, YP, W), shape(3,...  2.42 us
    pallas_call x1, Pallas kernels, shards(): call(finish_kernel, (shape(32, 8, W), shape(ROWS, SAMPLES), shape(8, W)),...  1.9 us
    pallas_call x1, Pallas kernels, shards(): call(update_kernel, (shape(32, 8, W), shape(2, 2, SAMPLES)), [SMEM] * 2 +...  1.76 us
    pallas_call x1, Pallas kernels, shards(): call(edge_y_kernel, (shape(X + 1, 4, W), shape(X, 4, W), shape(X, Y, W),...  1.66 us
  transfers between devices with their start and end apart: 6, of which 3 were waited for; matrix products, arithmetic and copies ran while one was open for 0% of the time, Pallas kernels for 5%

profile of v4, /device:TPU:1, one launch (start us, length us, event | category | flops | bytes accessed | tf_op | source)
XLA Modules:
  0.0 57.3 jit_solution(3915695587254877989)
XLA Ops:
  0.6 0.1 stack.20.place
  0.7 1.7 %edge_y.1 = (f32[9,4,128]{2,1,0:T(4,128)S(1)}, f32[8,4,128]{2,1,0:T(4,128)S(1)}, f32[8,32,128]{2,1,0:T(8,128)S(1)}, f32[8,32,128]{2,1,0:T(8,128)S(1)}, f32[8,128]{1,0:T(8,128)S(1)}) custom-call(s32[5]{0:T(128)S(1)} %stack.20.place, f32[8,32,128]{2,1,0:T(8,128)} %noise_far.1, s32[8,32,64]{2,1,0:T(8,128)} %classes_far.1, s32[8]{0:T(128)} %owner.1), custom_call_target="tpu_custom_call" | custom-call | tf_op jit(solution)/shard_map/edge_y/pallas_call | solution.py:529
  2.4 3.3 %collective-permute-start = (f32[9,4,128]{2,1,0:T(4,128)S(1)}, f32[9,4,128]{2,1,0:T(4,128)S(1)}, u32[]{:S(2)}, u32[]{:S(2)}) collective-permute-start(f32[9,4,128]{2,1,0:T(4,128)S(1)} %get-tuple-element.30), channel_id=1, source_target_pairs={{0,1},{1,0},{2,3},{3,2},{4,5},{5,4},{6,7},{7,6},{8,9},{9,8},{10,11... | collective-permute-start | bytes 55304 | tf_op jit(solution)/shard_map/ppermute | solution.py:40
  5.7 1.9 %collective-permute-start.1 = (f32[8,4,128]{2,1,0:T(4,128)S(1)}, f32[8,4,128]{2,1,0:T(4,128)S(1)}, u32[]{:S(2)}, u32[]{:S(2)}) collective-permute-start(f32[8,4,128]{2,1,0:T(4,128)S(1)} %get-tuple-element.31), channel_id=1, source_target_pairs={{1,2},{2,1},{3,4},{4,3},{5,6},{6,5},{9,10},{10,9},{11,12},{12,11},... | collective-permute-start | bytes 49160 | tf_op jit(solution)/shard_map/ppermute | solution.py:40
  7.6 3.1 %collective-permute-done.1.odd_in = f32[8,4,128]{2,1,0:T(4,128)S(1)} collective-permute-done((f32[8,4,128]{2,1,0:T(4,128)S(1)}, f32[8,4,128]{2,1,0:T(4,128)S(1)}, u32[]{:S(2)}, u32[]{:S(2)}) %collective-permute-start.1) | collective-permute-done | bytes 16416 | tf_op jit(solution)/shard_map/ppermute | solution.py:40
  10.8 0.0 collective-permute-done.even_in
  10.8 0.7 %edge_x.1 = (f32[8,40,128]{2,1,0:T(8,128)S(1)}, f32[8,40,128]{2,1,0:T(8,128)S(1)}, f32[4,40,128]{2,1,0:T(8,128)S(1)}, f32[4,40,128]{2,1,0:T(8,128)S(1)}, f32[4,128]{1,0:T(4,128)S(1)}) custom-call(s32[5]{0:T(128)S(1)} %stack.20.place, f32[8,32,128]{2,1,0:T(8,128)S(1)} %get-tuple-element.27.noise, f32[8,32,128]{2,1,0:T(8,128)S(1)} %get-tuple-element.28.doubled, ...), custom_call_target="tpu_custom_call" | custom-call | tf_op jit(solution)/shard_map/edge_x/pallas_call | solution.py:542
  11.5 0.7 %collective-permute-start.3 = (f32[4,40,128]{2,1,0:T(8,128)S(1)}, f32[4,40,128]{2,1,0:T(8,128)S(1)}, u32[]{:S(2)}, u32[]{:S(2)}) collective-permute-start(f32[4,40,128]{2,1,0:T(8,128)S(1)} %get-tuple-element.41), channel_id=1, source_target_pairs={{8,16},{16,8},{24,32},{32,24},{40,48},{48,40},{9,17},{17,9},{25,33... | collective-permute-start | bytes 245768 | tf_op jit(solution)/shard_map/ppermute | solution.py:40
  12.1 6.5 %collective-permute-start.2 = (f32[4,40,128]{2,1,0:T(8,128)S(1)}, f32[4,40,128]{2,1,0:T(8,128)S(1)}, u32[]{:S(2)}, u32[]{:S(2)}) collective-permute-start(f32[4,40,128]{2,1,0:T(8,128)S(1)} %get-tuple-element.33), channel_id=1, source_target_pairs={{0,8},{8,0},{16,24},{24,16},{32,40},{40,32},{48,56},{56,48},{1,9},... | collective-permute-start | bytes 245768 | tf_op jit(solution)/shard_map/ppermute | solution.py:40
  18.7 2.4 %interior.1 = (f32[27,8,40,128]{3,2,1,0:T(8,128)S(1)}, f32[3,8,40,128]{3,2,1,0:T(8,128)S(1)}, f32[3,6,40,128]{3,2,1,0:T(8,128)S(1)}, f32[3,4,40,128]{3,2,1,0:T(8...) custom-call(s32[5]{0:T(128)S(1)} %stack.20.place, ...), custom_call_target="tpu_custom_call" | custom-call | tf_op jit(solution)/shard_map/interior/pallas_call | solution.py:551
  21.1 0.0 collective-permute-done.3.edges
  21.1 0.0 copy-start
  21.1 0.0 copy-start.1
  21.1 0.0 copy-start.2
  21.1 0.7 %lower.1 = f32[12,8,128]{2,1,0:T(8,128)S(1)} custom-call(f32[8,40,128]{2,1,0:T(8,128)S(1)} %get-tuple-element.32.kinds, f32[4,40,128]{2,1,0:T(8,128)S(1)} %collective-permute-done.3.edges, f32[27,8,40,128]{3,2,1,0:T(8,128)S(1)} %get-tuple-element.36.weights, f32[3,8,40,128]{3,2,1,0:T(8,128)S(1)} %get-tuple-element.37.first, ...), custom_call_target="tpu_custom_call" | custom-call | tf_op jit(solution)/shard_map/lower/pallas_call | solution.py:574
  21.9 0.0 collective-permute-done.2.edges
  21.9 0.0 copy-done
  21.9 0.0 copy-done.1
  21.9 0.0 copy-done.2
  21.9 1.9 %finish.1 = (f32[32,8,128]{2,1,0:T(8,128)S(1)}, f32[24,256]{1,0:T(8,128)S(1)}, f32[8,128]{1,0:T(8,128)S(1)}) custom-call(s32[5]{0:T(128)S(1)} %stack.20.place, s32[8]{0:T(128)S(1)} %copy-done.1, s32[8]{0:T(128)S(1)} %copy-done.2, s32[8]{0:T(128)S(1)} %copy-done, f32[8,40,128]{2,1,0:T(8,128)S(1)} %get-tuple-element.32.kinds, ...), custom_call_target="tpu_custom_call" | custom-call | tf_op jit(solution)/shard_map/finish/pallas_call | solution.py:577
  23.8 19.0 %all_to_all.5.here = f32[16,24,256]{2,1,0:T(8,128)S(1)} all-to-all(f32[16,24,256]{2,1,0:T(8,128)S(1)} %broadcast_in_dim.2), channel_id=1, replica_groups=mesh['real'=4,'x'=4,'zh'=2,'y'=4,'core'=2] {'x','y'}, dimensions={0} | all-to-all | bytes 786432 | tf_op jit(solution)/shard_map/all_to_all | solution.py:587
  42.9 0.8 %collect.1 = (f32[2,32,256]{2,1,0:T(8,128)S(1)}, f32[2,32,256]{2,1,0:T(8,128)S(1)}) custom-call(s32[5]{0:T(128)S(1)} %stack.20.place, f32[8,128]{1,0:T(8,128)S(1)} %get-tuple-element.45.lists, f32[16,24,256]{2,1,0:T(8,128)S(1)} %all_to_all.5.here), custom_call_target="tpu_custom_call" | custom-call | tf_op jit(solution)/shard_map/collect/pallas_call | solution.py:590
  43.7 4.2 %collective-permute-start.4 = (f32[2,32,256]{2,1,0:T(8,128)S(1)}, f32[2,32,256]{2,1,0:T(8,128)S(1)}, u32[]{:S(2)}, u32[]{:S(2)}) collective-permute-start(f32[2,32,256]{2,1,0:T(8,128)S(1)} %get-tuple-element.48), channel_id=1, source_target_pairs={{0,1},{1,0},{2,3},{3,2},{4,5},{5,4},{6,7},{7,6},{8,9},{9,8},{10,11... | collective-permute-start | bytes 196616 | tf_op jit(solution)/shard_map/ppermute | solution.py:40
  47.9 0.9 %collective-permute-done.4.near = f32[2,32,256]{2,1,0:T(8,128)S(1)} collective-permute-done((f32[2,32,256]{2,1,0:T(8,128)S(1)}, f32[2,32,256]{2,1,0:T(8,128)S(1)}, u32[]{:S(2)}, u32[]{:S(2)}) %collective-permute-start.4) | collective-permute-done | bytes 65568 | tf_op jit(solution)/shard_map/ppermute | solution.py:40
  48.9 3.1 %collective-permute-start.5 = (f32[32,256]{1,0:T(8,128)S(1)}, f32[32,256]{1,0:T(8,128)S(1)}, u32[]{:S(2)}, u32[]{:S(2)}) collective-permute-start(f32[32,256]{1,0:T(8,128)S(1)} %fusion), channel_id=1, source_target_pairs={{0,8},{8,0},{1,9},{9,1},{2,10},{10,2},{3,11},{11,3},{4,12},{12,4},... | collective-permute-start | bytes 98312 | tf_op jit(solution)/shard_map/ppermute | solution.py:40
  52.0 3.5 %collective-permute-done.5.far = f32[32,256]{1,0:T(8,128)S(1)} collective-permute-done((f32[32,256]{1,0:T(8,128)S(1)}, f32[32,256]{1,0:T(8,128)S(1)}, u32[]{:S(2)}, u32[]{:S(2)}) %collective-permute-start.5) | collective-permute-done | bytes 32800 | tf_op jit(solution)/shard_map/ppermute | solution.py:40
  55.5 1.8 %update.1 = (f32[32,8,128]{2,1,0:T(8,128)}, f32[2,2,256]{2,1,0:T(2,128)}) custom-call(s32[8]{0:T(128)S(1)} %copy-done.1, s32[8]{0:T(128)S(1)} %copy-done.2, f32[2,32,256]{2,1,0:T(8,128)S(1)} %get-tuple-element.47.keep, f32[2,32,256]{2,1,0:T(8,128)S(1)} %collective-permute-done.4.near, f32[32,256]{1,0:T(8,128)S(1)} %collective-permute-done.5.far, ...), custom_call_target="tpu_custom_call" | custom-call | tf_op jit(solution)/shard_map/update/pallas_call | solution.py:595
  (2 shorter events, 0.0 us)
Async XLA Ops:
  2.4 8.4 %collective-permute-start = (f32[9,4,128]{2,1,0:T(4,128)S(1)}, f32[9,4,128]{2,1,0:T(4,128)S(1)}, u32[]{:S(2)}, u32[]{:S(2)}) collective-permute-start(f32[9,4,128]{2,1,0:T(4,128)S(1)} %get-tuple-element.30), channel_id=1, source_target_pairs={{0,1},{1,0},{2,3},{3,2},{4,5},{5,4},{6,7},{7,6},{8,9},{9,8},{10,11... | collective-permute-start | bytes 55304 | tf_op jit(solution)/shard_map/ppermute | solution.py:40
  5.7 5.0 %collective-permute-start.1 = (f32[8,4,128]{2,1,0:T(4,128)S(1)}, f32[8,4,128]{2,1,0:T(4,128)S(1)}, u32[]{:S(2)}, u32[]{:S(2)}) collective-permute-start(f32[8,4,128]{2,1,0:T(4,128)S(1)} %get-tuple-element.31), channel_id=1, source_target_pairs={{1,2},{2,1},{3,4},{4,3},{5,6},{6,5},{9,10},{10,9},{11,12},{12,11},... | collective-permute-start | bytes 49160 | tf_op jit(solution)/shard_map/ppermute | solution.py:40
  11.5 9.6 %collective-permute-start.3 = (f32[4,40,128]{2,1,0:T(8,128)S(1)}, f32[4,40,128]{2,1,0:T(8,128)S(1)}, u32[]{:S(2)}, u32[]{:S(2)}) collective-permute-start(f32[4,40,128]{2,1,0:T(8,128)S(1)} %get-tuple-element.41), channel_id=1, source_target_pairs={{8,16},{16,8},{24,32},{32,24},{40,48},{48,40},{9,17},{17,9},{25,33... | collective-permute-start | bytes 245768 | tf_op jit(solution)/shard_map/ppermute | solution.py:40
  12.1 9.7 %collective-permute-start.2 = (f32[4,40,128]{2,1,0:T(8,128)S(1)}, f32[4,40,128]{2,1,0:T(8,128)S(1)}, u32[]{:S(2)}, u32[]{:S(2)}) collective-permute-start(f32[4,40,128]{2,1,0:T(8,128)S(1)} %get-tuple-element.33), channel_id=1, source_target_pairs={{0,8},{8,0},{16,24},{24,16},{32,40},{40,32},{48,56},{56,48},{1,9},... | collective-permute-start | bytes 245768 | tf_op jit(solution)/shard_map/ppermute | solution.py:40
  21.1 0.8 %copy-start = (s32[8]{0:T(128)S(1)}, s32[8]{0:T(128)}, u32[]{:S(2)}) copy-start(s32[8]{0:T(128)} %owner.1) | copy-start | bytes 100
  21.1 0.8 %copy-start.1 = (s32[8]{0:T(128)S(1)}, s32[8]{0:T(128)}, u32[]{:S(2)}) copy-start(s32[8]{0:T(128)} %node_block.3) | copy-start | bytes 100
  21.1 0.8 %copy-start.2 = (s32[8]{0:T(128)S(1)}, s32[8]{0:T(128)}, u32[]{:S(2)}) copy-start(s32[8]{0:T(128)} %count.3) | copy-start | bytes 100
  43.7 5.1 %collective-permute-start.4 = (f32[2,32,256]{2,1,0:T(8,128)S(1)}, f32[2,32,256]{2,1,0:T(8,128)S(1)}, u32[]{:S(2)}, u32[]{:S(2)}) collective-permute-start(f32[2,32,256]{2,1,0:T(8,128)S(1)} %get-tuple-element.48), channel_id=1, source_target_pairs={{0,1},{1,0},{2,3},{3,2},{4,5},{5,4},{6,7},{7,6},{8,9},{9,8},{10,11... | collective-permute-start | bytes 196616 | tf_op jit(solution)/shard_map/ppermute | solution.py:40
  48.9 6.7 %collective-permute-start.5 = (f32[32,256]{1,0:T(8,128)S(1)}, f32[32,256]{1,0:T(8,128)S(1)}, u32[]{:S(2)}, u32[]{:S(2)}) collective-permute-start(f32[32,256]{1,0:T(8,128)S(1)} %fusion), channel_id=1, source_target_pairs={{0,8},{8,0},{1,9},{9,1},{2,10},{10,2},{3,11},{11,3},{4,12},{12,4},... | collective-permute-start | bytes 98312 | tf_op jit(solution)/shard_map/ppermute | solution.py:40

commit v5 on v4

--- a/solution.py
+++ b/solution.py
@@ -18,7 +18,6 @@
 ROWS = 24
 F32 = jnp.float32
 VMEM = pl.BlockSpec(memory_space=pltpu.VMEM)
-SMEM = pl.BlockSpec(memory_space=pltpu.SMEM)
 HBM = pl.BlockSpec(memory_space=pltpu.HBM)
 SIZES = {"x": 4, "zh": 2, "y": 4, "core": 2}
 
@@ -45,9 +44,7 @@
 
 
 def odd_pair(a, b):
-    if b == 1:
-        return (a + 1, 0) if a < 3 else None
-    return (a - 1, 1) if a > 0 else None
+    return ((a + 1) % 4, 0) if b == 1 else ((a + 3) % 4, 1)
 
 
 def half_lanes(shape):
@@ -68,72 +65,98 @@
     return jnp.where(low, row, other), jnp.where(low, other, row)
 
 
+def whereabouts():
+    x, zh, y, core = [lax.axis_index(axis) for axis in ("x", "zh", "y", "core")]
+    return zh, core, 4 * x + y, ((x * 2 + zh) * 4 + y) * 2 + core
+
+
+def has_odd_pair(outer, inner):
+    return lax.axis_index(outer) != 3 * lax.axis_index(inner)
+
+
 def edge_y_kernel(
-    place, noise_far, classes_far, owner_far,
-    even, odd, noise, doubled, names,
-    classes, owner, sems,
-):
-    copies = [
-        pltpu.make_async_copy(noise_far, noise, sems.at[0]),
-        pltpu.make_async_copy(classes_far, classes, sems.at[1]),
-        pltpu.make_async_copy(owner_far, owner, sems.at[2]),
+    noise_far, classes_far, owner_far,
+    odd, even, noise, classes, names,
+    noise_edges, class_edges, owner, sems,
+):
+    first = [
+        pltpu.make_async_copy(noise_far.at[:, 0:8, :], noise_edges.at[0], sems.at[0]),
+        pltpu.make_async_copy(noise_far.at[:, Y - 8 : Y, :], noise_edges.at[1], sems.at[1]),
+        pltpu.make_async_copy(classes_far.at[:, 0:8, :], class_edges.at[0], sems.at[2]),
+        pltpu.make_async_copy(classes_far.at[:, Y - 8 : Y, :], class_edges.at[1], sems.at[3]),
+        pltpu.make_async_copy(owner_far, owner, sems.at[4]),
     ]
-    for copy in copies:
+    rest = [
+        pltpu.make_async_copy(noise_far, noise, sems.at[5]),
+        pltpu.make_async_copy(classes_far, classes, sems.at[6]),
+    ]
+    for copy in first + rest:
         copy.start()
-    for copy in copies:
+    for copy in first:
         copy.wait()
-    kinds = (classes[...] + 1).astype(F32)
-    doubled[...] = jnp.concatenate([kinds, kinds], axis=-1)
-    core = place[1]
+    core = whereabouts()[1]
     lane = lax.broadcasted_iota(jnp.int32, (8, W), 1)
     own = jnp.zeros((8, W), F32)
     for b in range(BLOCKS):
         own = jnp.where(lane == b, (owner[b] + 1).astype(F32), own)
     names[...] = own
+    odd[X] = own[0:4]
     even[X] = own[0:4]
 
-    def low(out):
-        out[0:X, 0:3, :] = noise[:, 0:3, :]
-        out[0:X, 3:4, :] = pack(doubled[:, 0:1, :], doubled[:, 1:2, :])
-
-    def high(out):
-        out[0:X, 0:3, :] = noise[:, Y - 3 : Y, :]
-        out[0:X, 3:4, :] = pack(doubled[:, Y - 2 : Y - 1, :], doubled[:, Y - 1 : Y, :])
+    def message(out, end, start, one, two):
+        out[0:X, 0:3, :] = noise_edges[end, :, start : start + 3, :]
+        kinds = (class_edges[end] + 1).astype(F32)
+        out[0:X, 3:4, :] = jnp.concatenate([kinds[:, one : one + 1], kinds[:, two : two + 1]], axis=-1)
 
     @pl.when(core == 0)
     def _():
-        high(even)
-        low(odd)
+        message(even, 1, 5, 6, 7)
+        message(odd, 0, 0, 0, 1)
 
     @pl.when(core == 1)
     def _():
-        low(even)
-        high(odd)
-
-
-def edge_x_kernel(
-    place, noise, doubled, names, even_in, odd_in,
-    field, kinds, odd, even, lists,
-    true_field, true_kinds,
-):
-    core, half = place[1], place[0]
-    for out in (true_field, true_kinds):
+        message(even, 0, 0, 0, 1)
+        message(odd, 1, 5, 6, 7)
+
+    for copy in rest:
+        copy.wait()
+
+
+def prepare_kernel(noise, classes, field, kinds):
+    half = whereabouts()[0]
+    for out in (field, kinds):
         out[:, 0:8, :] = jnp.zeros((X, 8, W), F32)
         out[:, 32:40, :] = jnp.zeros((X, 8, W), F32)
-    true_field[:, OFF : OFF + Y, :] = noise[...]
-    true_kinds[:, OFF : OFF + Y, :] = doubled[...]
+    for x in range(X):
+        true = mirrored(x, half)
+        field[x, OFF : OFF + Y, :] = noise[true]
+        kind = (classes[true] + 1).astype(F32)
+        kinds[x, OFF : OFF + Y, :] = jnp.concatenate([kind, kind], axis=-1)
+
+
+def edge_x_kernel(
+    field_in, kinds_in, names, even_in, odd_in,
+    field, kinds, odd, even, lists,
+):
+    half, core = whereabouts()[0:2]
+    field[...] = field_in[...]
+    kinds[...] = kinds_in[...]
     lists[0:4] = names[0:4]
     lists[1:2] = even_in[X, 0:1, :]
 
+    inside = has_odd_pair("y", "core")
+
     def sides(low, high):
-        true_field[:, 1:4, :] = low[0:X, 0:3, :]
-        first, second = unpack(low[0:X, 3:4, :])
-        true_kinds[:, 2:3, :] = first
-        true_kinds[:, 3:4, :] = second
-        true_field[:, 36:39, :] = high[0:X, 0:3, :]
-        first, second = unpack(high[0:X, 3:4, :])
-        true_kinds[:, 36:37, :] = first
-        true_kinds[:, 37:38, :] = second
+        for x in range(X):
+            true = mirrored(x, half)
+            for message, start, one in ((low, 1, 2), (high, 36, 36)):
+                held = message[true]
+                if message is odd_in:
+                    held = jnp.where(inside, held, 0.0)
+                field[x, start : start + 3, :] = held[0:3]
+                first, second = unpack(held[3:4])
+                kinds[x, one : one + 1, :] = first
+                kinds[x, one + 1 : one + 2, :] = second
 
     @pl.when(core == 0)
     def _():
@@ -143,15 +166,11 @@
     def _():
         sides(even_in, odd_in)
 
-    for x in range(X):
-        true = mirrored(x, half)
-        field[x] = true_field[true]
-        kinds[x] = true_kinds[true]
     for n in range(3):
+        odd[n] = field[n]
         even[n] = field[X - 1 - n]
-        odd[n] = field[n]
+    odd[3] = pack(kinds[0], kinds[1])
     even[3] = pack(kinds[X - 1], kinds[X - 2])
-    odd[3] = pack(kinds[0], kinds[1])
     even[3, 0:1, :] = lists[0:1]
     even[3, YP - 1 : YP, :] = lists[1:2]
 
@@ -214,20 +233,24 @@
 
 
 def interior_kernel(
-    place, field, kinds, table, matrix, drill, gain,
-    weights, first, second, third, smooth, tables, held_matrix, held_rows,
-    held_table, sems,
+    field, kinds, table, matrix, drill, gain, node_block, count, owner,
+    weights, first, second, third, smooth, tables, held_matrix, held_rows, other, live, blocks,
+    held_table, scalars, sems,
 ):
     copies = [
         pltpu.make_async_copy(matrix, held_matrix, sems.at[0]),
         pltpu.make_async_copy(drill, held_rows.at[0], sems.at[1]),
         pltpu.make_async_copy(gain, held_rows.at[1], sems.at[2]),
+        pltpu.make_async_copy(node_block, scalars.at[0], sems.at[4]),
+        pltpu.make_async_copy(count, scalars.at[1], sems.at[5]),
+        pltpu.make_async_copy(owner, scalars.at[2], sems.at[6]),
         pltpu.make_async_copy(table, held_table, sems.at[3]),
     ]
     for copy in reversed(copies):
         copy.start()
-    copies[3].wait()
-    spread_table(held_table, place[0], tables)
+    copies[-1].wait()
+    half, _, plane, _ = whereabouts()
+    spread_table(held_table, half, tables)
     for x in range(X):
         def put(o, rows, value, x=x):
             weights[o, x, rows, :] = value
@@ -257,12 +280,31 @@
         )
         for g in range(4):
             smooth[4 * (x - 3) + g] = result[OFF + 8 * g : OFF + 8 * g + 8]
-    for copy in copies[:3]:
+    for copy in copies[:-1]:
         copy.wait()
-
-
-def fill_halo(message, tables, halo_kinds, halo_weights, halo_first):
-    one, two = unpack(message[3])
+    other[...] = jnp.zeros((8, SAMPLES), F32)
+    for k in range(2):
+        for h in range(2):
+            for kind in range(2):
+                row = 4 * kind + 2 * k + h
+                other[row : row + 1, 0:W] = held_rows[kind, k : k + 1, h * W : h * W + W]
+    lane = lax.broadcasted_iota(jnp.int32, (8, W), 1)
+    names = jnp.zeros((8, W), F32)
+    places = jnp.zeros((8, W), jnp.int32)
+    limit = jnp.zeros((BLOCKS, SAMPLES), jnp.int32)
+    block = lax.broadcasted_iota(jnp.int32, (BLOCKS, SAMPLES), 0)
+    for b in range(BLOCKS):
+        names = jnp.where(lane == 8 * plane + b, (scalars[2, b] + 1).astype(F32), names)
+        places = jnp.where(lane == b, scalars[0, b], places)
+        limit = jnp.where(block == b, scalars[1, b], limit)
+    other[0:1, W : 2 * W] = names[0:1]
+    blocks[...] = places
+    sample = lax.broadcasted_iota(jnp.int32, (BLOCKS, SAMPLES), 1)
+    live[...] = (sample < limit).astype(F32)
+
+
+def fill_halo(message, inside, tables, halo_kinds, halo_weights, halo_first):
+    one, two = unpack(jnp.where(inside, message[3], 0.0))
     halo_kinds[0], halo_kinds[1] = one, two
     halo_kinds[:, 0:1, :] = jnp.zeros((2, 1, W), F32)
     halo_kinds[:, YP - 1 : YP, :] = jnp.zeros((2, 1, W), F32)
@@ -272,7 +314,7 @@
 
         weigh(halo_kinds[i], tables, put)
     for i in range(3):
-        for c, value in enumerate(lean(message[i])):
+        for c, value in enumerate(lean(jnp.where(inside, message[i], 0.0))):
             halo_first[c, i] = value
 
 
@@ -326,7 +368,7 @@
     lower,
     halo_kinds, halo_weights, halo_first, edge_second, edge_third,
 ):
-    fill_halo(edges, tables, halo_kinds, halo_weights, halo_first)
+    fill_halo(edges, has_odd_pair("x", "zh"), tables, halo_kinds, halo_weights, halo_first)
 
     def put(x, g, value):
         lower[4 * x + g] = value
@@ -338,17 +380,18 @@
 
 
 def finish_kernel(
-    place, node_block, count, owner, kinds, edges, near,
-    weights, first, second, third, middle, lower, tables, matrix, rows,
+    kinds, edges, near, weights, first, second, third, middle, lower, tables, matrix, other, live, blocks,
     smooth, payload, lists,
-    halo_kinds, halo_weights, halo_first, edge_second, edge_third, chosen,
-):
-    half = place[0]
+    halo_kinds, halo_weights, halo_first, edge_second, edge_third, chosen, node_block, sem,
+):
+    copy = pltpu.make_async_copy(blocks.at[0:1], node_block, sem)
+    copy.start()
+    half = whereabouts()[0]
     lists[0:4] = near[0:4]
     lists[4:8] = jnp.zeros((4, W), F32)
     lists[2:3] = edges[3, 0:1, :]
     lists[3:4] = edges[3, YP - 1 : YP, :]
-    fill_halo(edges, tables, halo_kinds, halo_weights, halo_first)
+    fill_halo(edges, True, tables, halo_kinds, halo_weights, halo_first)
 
     def put(x, g, value):
         smooth[4 * mirrored(x, half) + g] = value
@@ -363,8 +406,9 @@
         for x in (3, 4):
             put(x, g, middle[4 * (x - 3) + g])
 
+    copy.wait()
     for b in range(BLOCKS):
-        chosen[pl.ds(8 * b, 8), :] = smooth[node_block[b]]
+        chosen[pl.ds(8 * b, 8), :] = smooth[node_block[0, b]]
     columns = rows_by_column(chosen)
     low = half_lanes((8, W))
     parts = ([], [])
@@ -384,31 +428,12 @@
         for r in range(2):
             both = product[8 * r : 8 * r + 8] + product[16 + 8 * r : 24 + 8 * r]
             sums[r] = jnp.where(block == b, both, sums[r])
-    live = is_live(count)
     for r in range(2):
-        payload[8 * r : 8 * r + 8, :] = jnp.where(live, sums[r], 0.0)
-    payload[16:24, :] = jnp.zeros((8, SAMPLES), F32)
-    for k in range(2):
-        for h in range(2):
-            for kind in range(2):
-                row = 16 + 4 * kind + 2 * k + h
-                payload[row : row + 1, 0:W] = rows[kind, k : k + 1, h * W : h * W + W]
-    lane = lax.broadcasted_iota(jnp.int32, (8, W), 1)
-    names = jnp.zeros((8, W), F32)
-    for b in range(BLOCKS):
-        names = jnp.where(lane == 8 * place[2] + b, (owner[b] + 1).astype(F32), names)
-    payload[16:17, W : 2 * W] = names[0:1]
-
-
-def is_live(count):
-    block = lax.broadcasted_iota(jnp.int32, (BLOCKS, SAMPLES), 0)
-    limit = jnp.zeros((BLOCKS, SAMPLES), jnp.int32)
-    for b in range(BLOCKS):
-        limit = jnp.where(block == b, count[b], limit)
-    return lax.broadcasted_iota(jnp.int32, (BLOCKS, SAMPLES), 1) < limit
-
-
-def collect_kernel(place, lists, here, keep, send):
+        payload[8 * r : 8 * r + 8, :] = jnp.where(live[...] > 0.0, sums[r], 0.0)
+    payload[16:24, :] = other[...]
+
+
+def collect_kernel(lists, here, keep, send):
     names = here[0, 16:24, W : 2 * W]
     for n in range(1, 16):
         names = names + here[n, 16:24, W : 2 * W]
@@ -416,8 +441,9 @@
     lane = lax.broadcasted_iota(jnp.int32, (8, W), 1)
     row = lax.broadcasted_iota(jnp.int32, (8, W), 0)
     hits, spots = [], []
+    half, core, _, me = whereabouts()
     for member in range(4):
-        tile = place[4] ^ (1 if member & 1 else 0) ^ (8 if member & 2 else 0)
+        tile = me ^ (1 if member & 1 else 0) ^ (8 if member & 2 else 0)
         held = jnp.broadcast_to(lists[member : member + 1], (8, W))
         name = jnp.sum(jnp.where(lane == row, held, 0.0), axis=1, keepdims=True)
         name = jnp.broadcast_to(name, (8, W))
@@ -426,7 +452,7 @@
         block = name.astype(jnp.int32) - 1
         holder = block >> 1
         spot = ((holder >> 4) * 4 + ((holder >> 1) & 3)) * 8 + 2 * (block & 1)
-        mine = ((holder & 1) == place[1]) & (((holder >> 3) & 1) == place[0])
+        mine = ((holder & 1) == core) & (((holder >> 3) & 1) == half)
         spots.append(jnp.where(mine, spot, -1024))
     hit = jnp.concatenate([h.astype(F32) for h in hits], axis=0).astype(jnp.bfloat16)
     spots = jnp.concatenate(spots, axis=0)
@@ -462,17 +488,18 @@
 
 
 def update_kernel(
-    node_block, count, keep, near, far, smooth, matrix, rows,
+    keep, near, far, smooth, matrix, rows, live, blocks,
     out, misfit,
-    update,
-):
+    update, node_block, sem,
+):
+    copy = pltpu.make_async_copy(blocks.at[0:1], node_block, sem)
+    copy.start()
     sums = keep[0] + near[0] + far[...]
     for k in range(2):
         for r in range(2):
             t = 24 + 2 * r + k
             misfit[k, r : r + 1, :] = rows[0, k : k + 1, :] - sums[t : t + 1, :]
-    live = is_live(count)
-    picked = [jnp.where(live, sums[16:24] * sums[8 * r : 8 * r + 8], 0.0) for r in range(2)]
+    picked = [jnp.where(live[...] > 0.0, sums[16:24] * sums[8 * r : 8 * r + 8], 0.0) for r in range(2)]
     pieces = [split(v) for v in picked]
     left = jnp.concatenate([pieces[0][0], pieces[1][0], pieces[0][1], pieces[1][1]], axis=0)
     block = lax.broadcasted_iota(jnp.int32, (BLOCKS, NODES), 0)
@@ -488,8 +515,9 @@
         update[pl.ds(2 * j, 8, stride=8), :] = jnp.where(low, one, swap_halves(two))
         update[pl.ds(2 * j + 1, 8, stride=8), :] = jnp.where(low, swap_halves(one), two)
     out[...] = smooth[...]
+    copy.wait()
     for b in range(BLOCKS):
-        n = node_block[b]
+        n = node_block[0, b]
         out[n] = out[n] + update[8 * b : 8 * b + 8, :]
 
 
@@ -512,43 +540,38 @@
 def shards(
     noise, classes, table, obs_matrix, node_block, sample_block, sample_count, drill_data, obs_gain
 ):
-    place = jnp.stack(
-        [
-            lax.axis_index("zh"),
-            lax.axis_index("core"),
-            lax.axis_index(("x", "y")),
-            lax.axis_index(("x", "y")),
-            lax.axis_index(("x", "zh", "y", "core")),
-        ]
-    ).astype(jnp.int32)
-    noise, classes, table, obs_matrix, owner, drill_data, obs_gain = [
+    noise, classes, table, matrix, blocks, owner, count, drill, gain = [
         pltpu.with_memory_space_constraint(a, pltpu.HBM)
-        for a in (noise, classes, table, obs_matrix, sample_block, drill_data, obs_gain)
+        for a in (
+            noise, classes, table, obs_matrix, node_block, sample_block, sample_count, drill_data, obs_gain
+        )
     ]
-
-    even, odd, near_noise, doubled, names = call(
+    odd, even, near_noise, near_classes, names = call(
         edge_y_kernel,
-        (shape(X + 1, 4, W), shape(X, 4, W), shape(X, Y, W), shape(X, Y, W), shape(8, W)),
-        [SMEM, HBM, HBM, HBM],
+        (shape(X + 1, 4, W), shape(X + 1, 4, W), shape(X, Y, W), shape(X, Y, Z, dtype=jnp.int32), shape(8, W)),
+        [HBM] * 3,
         "edge_y",
         [
-            pltpu.VMEM((X, Y, Z), jnp.int32),
+            pltpu.VMEM((2, X, 8, W), F32),
+            pltpu.VMEM((2, X, 8, Z), jnp.int32),
             pltpu.SMEM((BLOCKS,), jnp.int32),
-            pltpu.SemaphoreType.DMA((3,)),
+            pltpu.SemaphoreType.DMA((7,)),
         ],
-    )(place, noise, classes, owner)
+    )(noise, classes, owner)
+    odd = permute(odd, ("y", "core"), odd_pair)
     even = permute(even, ("y", "core"), even_pair)
-    odd = permute(odd, ("y", "core"), odd_pair)
+    field, kinds = call(
+        prepare_kernel, (shape(X, YP, W), shape(X, YP, W)), [VMEM] * 2, "prepare"
+    )(near_noise, near_classes)
     field, kinds, odd, even, lists = call(
         edge_x_kernel,
         (shape(X, YP, W), shape(X, YP, W), shape(4, YP, W), shape(4, YP, W), shape(4, W)),
-        [SMEM] + [VMEM] * 5,
+        [VMEM] * 5,
         "edge_x",
-        [pltpu.VMEM((X, YP, W), F32), pltpu.VMEM((X, YP, W), F32)],
-    )(place, near_noise, doubled, names, even, odd)
+    )(field, kinds, names, even, odd)
     odd = permute(odd, ("x", "zh"), odd_pair)
     even = permute(even, ("x", "zh"), even_pair)
-    weights, first, second, third, middle, tables, matrix, rows = call(
+    weights, first, second, third, middle, tables, matrix, rows, other, live, blocks = call(
         interior_kernel,
         (
             shape(27, X, YP, W),
@@ -559,11 +582,14 @@
             shape(27, 8, W),
             shape(BLOCKS, SAMPLES, NODES, dtype=jnp.bfloat16),
             shape(2, 2, SAMPLES),
+            shape(8, SAMPLES),
+            shape(BLOCKS, SAMPLES),
+            shape(8, W, dtype=jnp.int32),
         ),
-        [SMEM] + [VMEM] * 2 + [HBM] * 4,
+        [VMEM] * 2 + [HBM] * 7,
         "interior",
-        [pltpu.VMEM((8, 27), F32), pltpu.SemaphoreType.DMA((4,))],
-    )(place, field, kinds, table, obs_matrix, drill_data, obs_gain)
+        [pltpu.VMEM((8, 27), F32), pltpu.SMEM((3, BLOCKS), jnp.int32), pltpu.SemaphoreType.DMA((7,))],
+    )(field, kinds, table, matrix, drill, gain, blocks, count, owner)
     halo_scratch = [
         pltpu.VMEM((2, YP, W), F32),
         pltpu.VMEM((27, 2, YP, W), F32),
@@ -574,31 +600,32 @@
     (lower,) = call(lower_kernel, (shape(12, 8, W),), [VMEM] * 7, "lower", halo_scratch)(
         kinds, odd, weights, first, second, third, tables
     )
+    index_scratch = [pltpu.SMEM((1, W), jnp.int32), pltpu.SemaphoreType.DMA]
     smooth, payload, lists = call(
         finish_kernel,
         (shape(32, 8, W), shape(ROWS, SAMPLES), shape(8, W)),
-        [SMEM] * 4 + [VMEM] * 12,
+        [VMEM] * 14,
         "finish",
-        halo_scratch + [pltpu.VMEM((64, W), F32)],
+        halo_scratch + [pltpu.VMEM((64, W), F32)] + index_scratch,
     )(
-        place, node_block, sample_count, sample_block, kinds, even, lists,
-        weights, first, second, third, middle, lower, tables, matrix, rows,
+        kinds, even, lists, weights, first, second, third, middle, lower, tables, matrix,
+        other, live, blocks,
     )
     here = lax.all_to_all(
         jnp.broadcast_to(payload[None], (16, ROWS, SAMPLES)), ("x", "y"), 0, 0, tiled=True
     )
     keep, send = call(
-        collect_kernel, (shape(2, 32, SAMPLES), shape(2, 32, SAMPLES)), [SMEM, VMEM, VMEM], "collect"
-    )(place, lists, here)
+        collect_kernel, (shape(2, 32, SAMPLES), shape(2, 32, SAMPLES)), [VMEM] * 2, "collect"
+    )(lists, here)
     near = permute(send, ("core",), lambda c: (c ^ 1,))
     far = permute(keep[1] + near[1], ("zh",), lambda z: (z ^ 1,))
     out, misfit = call(
         update_kernel,
         (shape(32, 8, W), shape(2, 2, SAMPLES)),
-        [SMEM] * 2 + [VMEM] * 6,
+        [VMEM] * 8,
         "update",
-        [pltpu.VMEM((64, W), F32)],
-    )(node_block, sample_count, keep, near, far, smooth, matrix, rows)
+        [pltpu.VMEM((64, W), F32)] + index_scratch,
+    )(keep, near, far, smooth, matrix, rows, live, blocks)
     return out.reshape(X, Y, W), misfit
 
 

time: 57.5 us -> 52.8 us (0.918)
  waiting for transfers between devices: 7.59 us -> 13.6 us
  starting transfers between devices: 19.8 us -> 14.9 us
  blocking collectives: 19 us -> 15.8 us
  Pallas kernels: 9.95 us -> 7.55 us
    ppermute x6, waiting for transfers between devices: 7.59 us -> 13.6 us  [permute(): return lax.ppermute(value, axes if len(axes) > 1 else axes[0], pairs)]
    ppermute x6, starting transfers between devices: 19.8 us -> 14.9 us  [permute(): return lax.ppermute(value, axes if len(axes) > 1 else axes[0], pairs)]
    all_to_all x1, blocking collectives: 19 us -> 15.8 us  [shards(): lax.all_to_all(jnp.broadcast_to(payload[None], (16, ROWS, SAMPLES)), ('x'...]
    pallas_call x3 -> x4, Pallas kernels: 4.22 us -> 2.96 us  [the longest x1 1.48 us: shards(): call(update_kernel, (shape(32, 8, W), shape(2, 2, SAMPLES)), [VMEM] * 8,...]
  transfers between devices with their start and end apart: 6 -> 6, of which waited for: 3 -> 6; matrix products, arithmetic and copies ran while one was open for 0% -> 0% of each run, Pallas kernels for 5% -> 5%
where the time goes in v5:
time: 52.8 us; the launch traced here: 52.7 us
  blocking collectives  15.8 us (30%)
  starting transfers between devices  14.9 us (28%)
  waiting for transfers between devices  13.6 us (26%)
  Pallas kernels  7.55 us (14%)
  between operations  0.7 us (1%)
    all_to_all x1, blocking collectives, shards(): lax.all_to_all(jnp.broadcast_to(payload[None], (16, ROWS, SAMPLES)), ('x'...  15.8 us
    ppermute x6, starting transfers between devices, permute(): return lax.ppermute(value, axes if len(axes) > 1 else axes[0], pairs)  14.9 us
    ppermute x6, waiting for transfers between devices, permute(): return lax.ppermute(value, axes if len(axes) > 1 else axes[0], pairs)  13.6 us
    pallas_call x1, Pallas kernels, shards(): call(interior_kernel, (shape(27, X, YP, W), shape(3, X, YP, W), shape(3,...  2.01 us
    pallas_call x1, Pallas kernels, shards(): call(finish_kernel, (shape(32, 8, W), shape(ROWS, SAMPLES), shape(8, W)),...  1.74 us
    pallas_call x1, Pallas kernels, shards(): call(update_kernel, (shape(32, 8, W), shape(2, 2, SAMPLES)), [VMEM] * 8,...  1.48 us
    pallas_call x1, Pallas kernels, shards(): call(edge_y_kernel, (shape(X + 1, 4, W), shape(X + 1, 4, W), shape(X, Y,...  1.11 us
  transfers between devices with their start and end apart: 6, of which 6 were waited for; matrix products, arithmetic and copies ran while one was open for 0% of the time, Pallas kernels for 5%

profile of v5, /device:TPU:1, one launch (start us, length us, event | category | flops | bytes accessed | tf_op | source)
XLA Modules:
  0.0 52.7 jit_solution(18354275274317567260)
XLA Ops:
  0.6 1.1 %edge_y.1 = (f32[9,4,128]{2,1,0:T(4,128)S(1)}, f32[9,4,128]{2,1,0:T(4,128)S(1)}, f32[8,32,128]{2,1,0:T(8,128)S(1)}, s32[8,32,64]{2,1,0:T(8,128)S(1)}, f32[8,128]{1,0:T(8,128)S(1)}) custom-call(f32[8,32,128]{2,1,0:T(8,128)} %noise_far.1, s32[8,32,64]{2,1,0:T(8,128)} %classes_far.1, s32[8]{0:T(128)} %owner.1), custom_call_target="tpu_custom_call" | custom-call | tf_op jit(solution)/shard_map/edge_y/pallas_call | solution.py:549
  1.7 3.3 %collective-permute-start = (f32[9,4,128]{2,1,0:T(4,128)S(1)}, f32[9,4,128]{2,1,0:T(4,128)S(1)}, u32[]{:S(2)}, u32[]{:S(2)}) collective-permute-start(f32[9,4,128]{2,1,0:T(4,128)S(1)} %get-tuple-element.37), channel_id=1, source_target_pairs={{0,1},{1,0},{2,3},{3,2},{4,5},{5,4},{6,7},{7,6},{8,9},{9,8},{10,11... | collective-permute-start | bytes 55304 | tf_op jit(solution)/shard_map/ppermute | solution.py:39
  5.1 0.0 collective-permute-start.1
  5.1 0.1 prepare.1
  5.2 0.7 %collective-permute-done.even_in = f32[9,4,128]{2,1,0:T(4,128)S(1)} collective-permute-done((f32[9,4,128]{2,1,0:T(4,128)S(1)}, f32[9,4,128]{2,1,0:T(4,128)S(1)}, u32[]{:S(2)}, u32[]{:S(2)}) %collective-permute-start) | collective-permute-done | bytes 18464 | tf_op jit(solution)/shard_map/ppermute | solution.py:39
  5.9 2.3 %collective-permute-done.1.odd_in = f32[9,4,128]{2,1,0:T(4,128)S(1)} collective-permute-done((f32[9,4,128]{2,1,0:T(4,128)S(1)}, f32[9,4,128]{2,1,0:T(4,128)S(1)}, u32[]{:S(2)}, u32[]{:S(2)}) %collective-permute-start.1) | collective-permute-done | bytes 18464 | tf_op jit(solution)/shard_map/ppermute | solution.py:39
  8.3 0.1 edge_x.1
  8.4 7.5 %collective-permute-start.3 = (f32[4,40,128]{2,1,0:T(8,128)S(1)}, f32[4,40,128]{2,1,0:T(8,128)S(1)}, u32[]{:S(2)}, u32[]{:S(2)}) collective-permute-start(f32[4,40,128]{2,1,0:T(8,128)S(1)} %get-tuple-element.48), channel_id=1, source_target_pairs={{0,56},{8,16},{16,8},{24,32},{32,24},{40,48},{48,40},{56,0},{1,57}... | collective-permute-start | bytes 245768 | tf_op jit(solution)/shard_map/ppermute | solution.py:39
  15.8 0.0 collective-permute-start.2
  15.9 2.0 %interior.1 = (f32[27,8,40,128]{3,2,1,0:T(8,128)S(1)}, f32[3,8,40,128]{3,2,1,0:T(8,128)S(1)}, f32[3,6,40,128]{3,2,1,0:T(8,128)S(1)}, f32[3,4,40,128]{3,2,1,0:T(8...) custom-call(f32[8,40,128]{2,1,0:T(8,128)S(1)} %get-tuple-element.42., ...), custom_call_target="tpu_custom_call" | custom-call | tf_op jit(solution)/shard_map/interior/pallas_call | solution.py:574
  17.9 0.3 collective-permute-done.3.edges
  18.2 0.7 %lower.1 = f32[12,8,128]{2,1,0:T(8,128)S(1)} custom-call(f32[8,40,128]{2,1,0:T(8,128)S(1)} %get-tuple-element.39.kinds, f32[4,40,128]{2,1,0:T(8,128)S(1)} %collective-permute-done.3.edges, f32[27,8,40,128]{3,2,1,0:T(8,128)S(1)} %get-tuple-element.43.weights, f32[3,8,40,128]{3,2,1,0:T(8,128)S(1)} %get-tuple-element.44.first, ...), custom_call_target="tpu_custom_call" | custom-call | tf_op jit(solution)/shard_map/lower/pallas_call | solution.py:600
  18.9 5.1 %collective-permute-done.2.edges = f32[4,40,128]{2,1,0:T(8,128)S(1)} collective-permute-done((f32[4,40,128]{2,1,0:T(8,128)S(1)}, f32[4,40,128]{2,1,0:T(8,128)S(1)}, u32[]{:S(2)}, u32[]{:S(2)}) %collective-permute-start.2) | collective-permute-done | bytes 81952 | tf_op jit(solution)/shard_map/ppermute | solution.py:39
  24.1 1.7 %finish.1 = (f32[32,8,128]{2,1,0:T(8,128)S(1)}, f32[24,256]{1,0:T(8,128)S(1)}, f32[8,128]{1,0:T(8,128)S(1)}) custom-call(f32[8,40,128]{2,1,0:T(8,128)S(1)} %get-tuple-element.39.kinds, f32[4,40,128]{2,1,0:T(8,128)S(1)} %collective-permute-done.2.edges, f32[4,128]{1,0:T(4,128)S(1)} %get-tuple-element.41.near, ...), custom_call_target="tpu_custom_call" | custom-call | tf_op jit(solution)/shard_map/finish/pallas_call | solution.py:604
  25.8 15.8 %all_to_all.5.here = f32[16,24,256]{2,1,0:T(8,128)S(1)} all-to-all(f32[16,24,256]{2,1,0:T(8,128)S(1)} %broadcast_in_dim.2), channel_id=1, replica_groups=mesh['real'=4,'x'=4,'zh'=2,'y'=4,'core'=2] {'x','y'}, dimensions={0} | all-to-all | bytes 786432 | tf_op jit(solution)/shard_map/all_to_all | solution.py:614
  41.7 0.3 collect.1
  41.9 1.7 %collective-permute-start.4 = (f32[2,32,256]{2,1,0:T(8,128)S(1)}, f32[2,32,256]{2,1,0:T(8,128)S(1)}, u32[]{:S(2)}, u32[]{:S(2)}) collective-permute-start(f32[2,32,256]{2,1,0:T(8,128)S(1)} %get-tuple-element.57), channel_id=1, source_target_pairs={{0,1},{1,0},{2,3},{3,2},{4,5},{5,4},{6,7},{7,6},{8,9},{9,8},{10,11... | collective-permute-start | bytes 196616 | tf_op jit(solution)/shard_map/ppermute | solution.py:39
  43.6 0.9 %collective-permute-done.4.near = f32[2,32,256]{2,1,0:T(8,128)S(1)} collective-permute-done((f32[2,32,256]{2,1,0:T(8,128)S(1)}, f32[2,32,256]{2,1,0:T(8,128)S(1)}, u32[]{:S(2)}, u32[]{:S(2)}) %collective-permute-start.4) | collective-permute-done | bytes 65568 | tf_op jit(solution)/shard_map/ppermute | solution.py:39
  44.5 2.5 %collective-permute-start.5 = (f32[32,256]{1,0:T(8,128)S(1)}, f32[32,256]{1,0:T(8,128)S(1)}, u32[]{:S(2)}, u32[]{:S(2)}) collective-permute-start(f32[32,256]{1,0:T(8,128)S(1)} %fusion), channel_id=1, source_target_pairs={{0,8},{8,0},{1,9},{9,1},{2,10},{10,2},{3,11},{11,3},{4,12},{12,4},... | collective-permute-start | bytes 98312 | tf_op jit(solution)/shard_map/ppermute | solution.py:39
  47.0 4.2 %collective-permute-done.5.far = f32[32,256]{1,0:T(8,128)S(1)} collective-permute-done((f32[32,256]{1,0:T(8,128)S(1)}, f32[32,256]{1,0:T(8,128)S(1)}, u32[]{:S(2)}, u32[]{:S(2)}) %collective-permute-start.5) | collective-permute-done | bytes 32800 | tf_op jit(solution)/shard_map/ppermute | solution.py:39
  51.2 1.5 %update.1 = (f32[32,8,128]{2,1,0:T(8,128)}, f32[2,2,256]{2,1,0:T(2,128)}) custom-call(f32[2,32,256]{2,1,0:T(8,128)S(1)} %get-tuple-element.56.keep, f32[2,32,256]{2,1,0:T(8,128)S(1)} %collective-permute-done.4.near, f32[32,256]{1,0:T(8,128)S(1)} %collective-permute-done.5.far, f32[32,8,128]{2,1,0:T(8,128)S(1)} %get-tuple-element.58.smooth, ...), custom_call_target="tpu_custom_call" | custom-call | tf_op jit(solution)/shard_map/update/pallas_call | solution.py:622
  (2 shorter events, 0.0 us)
Async XLA Ops:
  1.7 4.2 %collective-permute-start = (f32[9,4,128]{2,1,0:T(4,128)S(1)}, f32[9,4,128]{2,1,0:T(4,128)S(1)}, u32[]{:S(2)}, u32[]{:S(2)}) collective-permute-start(f32[9,4,128]{2,1,0:T(4,128)S(1)} %get-tuple-element.37), channel_id=1, source_target_pairs={{0,1},{1,0},{2,3},{3,2},{4,5},{5,4},{6,7},{7,6},{8,9},{9,8},{10,11... | collective-permute-start | bytes 55304 | tf_op jit(solution)/shard_map/ppermute | solution.py:39
  5.1 3.2 %collective-permute-start.1 = (f32[9,4,128]{2,1,0:T(4,128)S(1)}, f32[9,4,128]{2,1,0:T(4,128)S(1)}, u32[]{:S(2)}, u32[]{:S(2)}) collective-permute-start(f32[9,4,128]{2,1,0:T(4,128)S(1)} %get-tuple-element.38), channel_id=1, source_target_pairs={{0,7},{1,2},{2,1},{3,4},{4,3},{5,6},{6,5},{7,0},{8,15},{9,10},{10,... | collective-permute-start | bytes 55304 | tf_op jit(solution)/shard_map/ppermute | solution.py:39
  8.4 9.8 %collective-permute-start.3 = (f32[4,40,128]{2,1,0:T(8,128)S(1)}, f32[4,40,128]{2,1,0:T(8,128)S(1)}, u32[]{:S(2)}, u32[]{:S(2)}) collective-permute-start(f32[4,40,128]{2,1,0:T(8,128)S(1)} %get-tuple-element.48), channel_id=1, source_target_pairs={{0,56},{8,16},{16,8},{24,32},{32,24},{40,48},{48,40},{56,0},{1,57}... | collective-permute-start | bytes 245768 | tf_op jit(solution)/shard_map/ppermute | solution.py:39
  15.8 8.2 %collective-permute-start.2 = (f32[4,40,128]{2,1,0:T(8,128)S(1)}, f32[4,40,128]{2,1,0:T(8,128)S(1)}, u32[]{:S(2)}, u32[]{:S(2)}) collective-permute-start(f32[4,40,128]{2,1,0:T(8,128)S(1)} %get-tuple-element.40), channel_id=1, source_target_pairs={{0,8},{8,0},{16,24},{24,16},{32,40},{40,32},{48,56},{56,48},{1,9},... | collective-permute-start | bytes 245768 | tf_op jit(solution)/shard_map/ppermute | solution.py:39
  41.9 2.6 %collective-permute-start.4 = (f32[2,32,256]{2,1,0:T(8,128)S(1)}, f32[2,32,256]{2,1,0:T(8,128)S(1)}, u32[]{:S(2)}, u32[]{:S(2)}) collective-permute-start(f32[2,32,256]{2,1,0:T(8,128)S(1)} %get-tuple-element.57), channel_id=1, source_target_pairs={{0,1},{1,0},{2,3},{3,2},{4,5},{5,4},{6,7},{7,6},{8,9},{9,8},{10,11... | collective-permute-start | bytes 196616 | tf_op jit(solution)/shard_map/ppermute | solution.py:39
  44.5 6.7 %collective-permute-start.5 = (f32[32,256]{1,0:T(8,128)S(1)}, f32[32,256]{1,0:T(8,128)S(1)}, u32[]{:S(2)}, u32[]{:S(2)}) collective-permute-start(f32[32,256]{1,0:T(8,128)S(1)} %fusion), channel_id=1, source_target_pairs={{0,8},{8,0},{1,9},{9,1},{2,10},{10,2},{3,11},{11,3},{4,12},{12,4},... | collective-permute-start | bytes 98312 | tf_op jit(solution)/shard_map/ppermute | solution.py:39

commit v6 on v5

--- a/solution.py
+++ b/solution.py
@@ -16,6 +16,7 @@
 SAMPLES = 256
 NODES = 512
 ROWS = 24
+MESSAGE = 136
 F32 = jnp.float32
 VMEM = pl.BlockSpec(memory_space=pltpu.VMEM)
 HBM = pl.BlockSpec(memory_space=pltpu.HBM)
@@ -44,7 +45,19 @@
 
 
 def odd_pair(a, b):
-    return ((a + 1) % 4, 0) if b == 1 else ((a + 3) % 4, 1)
+    if b == 1:
+        return (a + 1, 0) if a < 3 else None
+    return (a - 1, 1) if a > 0 else None
+
+
+def odd_along_x(x, zh, core):
+    other = odd_pair(x, zh)
+    return other + (core,) if other else (x, zh, core ^ 1)
+
+
+def odd_along_y(x, y, core):
+    other = odd_pair(y, core)
+    return (x,) + other if other else (x ^ 1, y, core)
 
 
 def half_lanes(shape):
@@ -122,7 +135,9 @@
         copy.wait()
 
 
-def prepare_kernel(noise, classes, field, kinds):
+def prepare_kernel(noise, classes, table, field, kinds, tables, held_table, sem):
+    copy = pltpu.make_async_copy(table, held_table, sem)
+    copy.start()
     half = whereabouts()[0]
     for out in (field, kinds):
         out[:, 0:8, :] = jnp.zeros((X, 8, W), F32)
@@ -132,11 +147,14 @@
         field[x, OFF : OFF + Y, :] = noise[true]
         kind = (classes[true] + 1).astype(F32)
         kinds[x, OFF : OFF + Y, :] = jnp.concatenate([kind, kind], axis=-1)
+    copy.wait()
+    spread_table(held_table, half, tables)
 
 
 def edge_x_kernel(
-    field_in, kinds_in, names, even_in, odd_in,
+    field_in, kinds_in, names, even_in, odd_in, tables,
     field, kinds, odd, even, lists,
+    weights, moved,
 ):
     half, core = whereabouts()[0:2]
     field[...] = field_in[...]
@@ -166,13 +184,26 @@
     def _():
         sides(even_in, odd_in)
 
-    for n in range(3):
-        odd[n] = field[n]
-        even[n] = field[X - 1 - n]
-    odd[3] = pack(kinds[0], kinds[1])
-    even[3] = pack(kinds[X - 1], kinds[X - 2])
-    even[3, 0:1, :] = lists[0:1]
-    even[3, YP - 1 : YP, :] = lists[1:2]
+    for out, row, step in ((odd, 0, 1), (even, X - 1, -1)):
+        def put(o, part, value):
+            weights[o, part, :] = value
+
+        weigh(kinds[row + step], tables, put)
+        for n in range(3):
+            for c, value in enumerate(lean(field[row + n * step])):
+                moved[c, n] = value
+        second = operate(
+            lambda o: weights[o],
+            lambda a, c: moved[c, a if step == 1 else 2 - a],
+            jnp.minimum(kinds[row + step], 1.0),
+        )
+        out[0:38, :] = field[row][1:39]
+        out[38:76, :] = field[row + step][1:39]
+        out[76:112, :] = second[2:38]
+        kind = kinds[row]
+        out[112:130, :] = pack(kind[2:20], kind[20:38])
+        out[130:132, :] = lists[0:2]
+        out[132:MESSAGE, :] = jnp.zeros((MESSAGE - 132, W), F32)
 
 
 def mirrored(x, half):
@@ -233,24 +264,21 @@
 
 
 def interior_kernel(
-    field, kinds, table, matrix, drill, gain, node_block, count, owner,
-    weights, first, second, third, smooth, tables, held_matrix, held_rows, other, live, blocks,
-    held_table, scalars, sems,
+    field, kinds, tables, matrix, drill, gain, node_block, count, owner,
+    weights, first, second, third, smooth, held_matrix, held_rows, other, live, blocks,
+    scalars, sems,
 ):
     copies = [
         pltpu.make_async_copy(matrix, held_matrix, sems.at[0]),
         pltpu.make_async_copy(drill, held_rows.at[0], sems.at[1]),
         pltpu.make_async_copy(gain, held_rows.at[1], sems.at[2]),
-        pltpu.make_async_copy(node_block, scalars.at[0], sems.at[4]),
-        pltpu.make_async_copy(count, scalars.at[1], sems.at[5]),
-        pltpu.make_async_copy(owner, scalars.at[2], sems.at[6]),
-        pltpu.make_async_copy(table, held_table, sems.at[3]),
+        pltpu.make_async_copy(node_block, scalars.at[0], sems.at[3]),
+        pltpu.make_async_copy(count, scalars.at[1], sems.at[4]),
+        pltpu.make_async_copy(owner, scalars.at[2], sems.at[5]),
     ]
     for copy in reversed(copies):
         copy.start()
-    copies[-1].wait()
-    half, _, plane, _ = whereabouts()
-    spread_table(held_table, half, tables)
+    plane = whereabouts()[2]
     for x in range(X):
         def put(o, rows, value, x=x):
             weights[o, x, rows, :] = value
@@ -280,7 +308,7 @@
         )
         for g in range(4):
             smooth[4 * (x - 3) + g] = result[OFF + 8 * g : OFF + 8 * g + 8]
-    for copy in copies[:-1]:
+    for copy in copies:
         copy.wait()
     other[...] = jnp.zeros((8, SAMPLES), F32)
     for k in range(2):
@@ -303,19 +331,21 @@
     live[...] = (sample < limit).astype(F32)
 
 
-def fill_halo(message, inside, tables, halo_kinds, halo_weights, halo_first):
-    one, two = unpack(jnp.where(inside, message[3], 0.0))
-    halo_kinds[0], halo_kinds[1] = one, two
-    halo_kinds[:, 0:1, :] = jnp.zeros((2, 1, W), F32)
-    halo_kinds[:, YP - 1 : YP, :] = jnp.zeros((2, 1, W), F32)
+def fill_halo(message, inside, tables, halo_kinds, halo_weights, halo_first, edge_second):
+    held = jnp.where(inside, message[...], 0.0)
+    one, two = [jnp.zeros((n, W), F32) for n in (1, 2)]
+    low, high = unpack(held[112:130])
+    halo_kinds[...] = jnp.concatenate([two, low, high, two], axis=0)
+
+    def put(o, part, value):
+        halo_weights[o, part, :] = value
+
+    weigh(halo_kinds[...], tables, put)
     for i in range(2):
-        def put(o, part, value, i=i):
-            halo_weights[o, i, part, :] = value
-
-        weigh(halo_kinds[i], tables, put)
-    for i in range(3):
-        for c, value in enumerate(lean(jnp.where(inside, message[i], 0.0))):
+        for c, value in enumerate(lean(jnp.concatenate([one, held[38 * i : 38 * i + 38], one], axis=0))):
             halo_first[c, i] = value
+    for c, value in enumerate(lean(jnp.concatenate([two, held[76:112], two], axis=0))):
+        edge_second[c, 2] = value
 
 
 def side(
@@ -327,8 +357,7 @@
     def weight(x):
         if 0 <= x < X:
             return (lambda o: weights[o, x]), jnp.minimum(kinds[x], 1.0)
-        i = beyond(x)
-        return (lambda o: halo_weights[o, i]), jnp.minimum(halo_kinds[i], 1.0)
+        return (lambda o: halo_weights[o]), jnp.minimum(halo_kinds[...], 1.0)
 
     def at_first(x, c):
         return first[c, x] if 0 <= x < X else halo_first[c, beyond(x)]
@@ -346,7 +375,7 @@
     def row(n):
         return X - 1 - n if high else n
 
-    for n in (-2, -1, 0):
+    for n in (-1, 0):
         for c, value in enumerate(lean(step(at_first, row(n)))):
             edge_second[c, -n] = value
     for n in (-1, 0, 1):
@@ -368,7 +397,7 @@
     lower,
     halo_kinds, halo_weights, halo_first, edge_second, edge_third,
 ):
-    fill_halo(edges, has_odd_pair("x", "zh"), tables, halo_kinds, halo_weights, halo_first)
+    fill_halo(edges, has_odd_pair("x", "zh"), tables, halo_kinds, halo_weights, halo_first, edge_second)
 
     def put(x, g, value):
         lower[4 * x + g] = value
@@ -389,9 +418,8 @@
     half = whereabouts()[0]
     lists[0:4] = near[0:4]
     lists[4:8] = jnp.zeros((4, W), F32)
-    lists[2:3] = edges[3, 0:1, :]
-    lists[3:4] = edges[3, YP - 1 : YP, :]
-    fill_halo(edges, True, tables, halo_kinds, halo_weights, halo_first)
+    lists[2:4] = edges[130:132]
+    fill_halo(edges, True, tables, halo_kinds, halo_weights, halo_first, edge_second)
 
     def put(x, g, value):
         smooth[4 * mirrored(x, half) + g] = value
@@ -558,20 +586,25 @@
             pltpu.SemaphoreType.DMA((7,)),
         ],
     )(noise, classes, owner)
-    odd = permute(odd, ("y", "core"), odd_pair)
+    odd = permute(odd, ("x", "y", "core"), odd_along_y)
     even = permute(even, ("y", "core"), even_pair)
-    field, kinds = call(
-        prepare_kernel, (shape(X, YP, W), shape(X, YP, W)), [VMEM] * 2, "prepare"
-    )(near_noise, near_classes)
+    field, kinds, tables = call(
+        prepare_kernel,
+        (shape(X, YP, W), shape(X, YP, W), shape(27, 8, W)),
+        [VMEM] * 2 + [HBM],
+        "prepare",
+        [pltpu.VMEM((8, 27), F32), pltpu.SemaphoreType.DMA],
+    )(near_noise, near_classes, table)
     field, kinds, odd, even, lists = call(
         edge_x_kernel,
-        (shape(X, YP, W), shape(X, YP, W), shape(4, YP, W), shape(4, YP, W), shape(4, W)),
-        [VMEM] * 5,
+        (shape(X, YP, W), shape(X, YP, W), shape(MESSAGE, W), shape(MESSAGE, W), shape(4, W)),
+        [VMEM] * 6,
         "edge_x",
-    )(field, kinds, names, even, odd)
-    odd = permute(odd, ("x", "zh"), odd_pair)
+        [pltpu.VMEM((27, YP, W), F32), pltpu.VMEM((3, 3, YP, W), F32)],
+    )(field, kinds, names, even, odd, tables)
+    odd = permute(odd, ("x", "zh", "core"), odd_along_x)
     even = permute(even, ("x", "zh"), even_pair)
-    weights, first, second, third, middle, tables, matrix, rows, other, live, blocks = call(
+    weights, first, second, third, middle, matrix, rows, other, live, blocks = call(
         interior_kernel,
         (
             shape(27, X, YP, W),
@@ -579,21 +612,20 @@
             shape(3, 6, YP, W),
             shape(3, 4, YP, W),
             shape(8, 8, W),
-            shape(27, 8, W),
             shape(BLOCKS, SAMPLES, NODES, dtype=jnp.bfloat16),
             shape(2, 2, SAMPLES),
             shape(8, SAMPLES),
             shape(BLOCKS, SAMPLES),
             shape(8, W, dtype=jnp.int32),
         ),
-        [VMEM] * 2 + [HBM] * 7,
+        [VMEM] * 3 + [HBM] * 6,
         "interior",
-        [pltpu.VMEM((8, 27), F32), pltpu.SMEM((3, BLOCKS), jnp.int32), pltpu.SemaphoreType.DMA((7,))],
-    )(field, kinds, table, matrix, drill, gain, blocks, count, owner)
+        [pltpu.SMEM((3, BLOCKS), jnp.int32), pltpu.SemaphoreType.DMA((6,))],
+    )(field, kinds, tables, matrix, drill, gain, blocks, count, owner)
     halo_scratch = [
-        pltpu.VMEM((2, YP, W), F32),
-        pltpu.VMEM((27, 2, YP, W), F32),
-        pltpu.VMEM((3, 3, YP, W), F32),
+        pltpu.VMEM((YP, W), F32),
+        pltpu.VMEM((27, YP, W), F32),
+        pltpu.VMEM((3, 2, YP, W), F32),
         pltpu.VMEM((3, 3, YP, W), F32),
         pltpu.VMEM((3, 3, YP, W), F32),
     ]

time: 52.8 us -> 51.2 us (0.970)
  waiting for transfers between devices: 13.6 us -> 8.17 us
  blocking collectives: 15.8 us -> 17.8 us
  Pallas kernels: 7.55 us -> 8.96 us
    ppermute x6, waiting for transfers between devices: 13.6 us -> 8.17 us  [permute(): return lax.ppermute(value, axes if len(axes) > 1 else axes[0], pairs)]
    all_to_all x1, blocking collectives: 15.8 us -> 17.8 us  [shards(): lax.all_to_all(jnp.broadcast_to(payload[None], (16, ROWS, SAMPLES)), ('x'...]
    pallas_call x2, Pallas kernels: 0.23 us -> 1.14 us  [the longest x1 0.83 us: shards(): call(prepare_kernel, (shape(X, YP, W), shape(X, YP, W), shape(27, 8, W)),...]
    pallas_call x1, Pallas kernels: 2.01 us -> 2.71 us  [shards(): call(interior_kernel, (shape(27, X, YP, W), shape(3, X, YP, W), shape(3,...]
  transfers between devices with their start and end apart: 6 -> 6, of which waited for: 6 -> 4; matrix products, arithmetic and copies ran while one was open for 0% -> 0% of each run, Pallas kernels for 5% -> 8%
where the time goes in v6:
time: 51.2 us; the launch traced here: 51 us
  blocking collectives  17.8 us (35%)
  starting transfers between devices  15.3 us (30%)
  Pallas kernels  8.96 us (18%)
  waiting for transfers between devices  8.17 us (16%)
  between operations  0.71 us (1%)
    all_to_all x1, blocking collectives, shards(): lax.all_to_all(jnp.broadcast_to(payload[None], (16, ROWS, SAMPLES)), ('x'...  17.8 us
    ppermute x6, starting transfers between devices, permute(): return lax.ppermute(value, axes if len(axes) > 1 else axes[0], pairs)  15.3 us
    ppermute x6, waiting for transfers between devices, permute(): return lax.ppermute(value, axes if len(axes) > 1 else axes[0], pairs)  8.17 us
    pallas_call x1, Pallas kernels, shards(): call(interior_kernel, (shape(27, X, YP, W), shape(3, X, YP, W), shape(3,...  2.71 us
    pallas_call x1, Pallas kernels, shards(): call(finish_kernel, (shape(32, 8, W), shape(ROWS, SAMPLES), shape(8, W)),...  1.65 us
    pallas_call x1, Pallas kernels, shards(): call(update_kernel, (shape(32, 8, W), shape(2, 2, SAMPLES)), [VMEM] * 8,...  1.47 us
    pallas_call x1, Pallas kernels, shards(): call(edge_y_kernel, (shape(X + 1, 4, W), shape(X + 1, 4, W), shape(X, Y,...  1.11 us
  transfers between devices with their start and end apart: 6, of which 4 were waited for; matrix products, arithmetic and copies ran while one was open for 0% of the time, Pallas kernels for 8%

profile of v6, /device:TPU:1, one launch (start us, length us, event | category | flops | bytes accessed | tf_op | source)
XLA Modules:
  0.0 51.0 jit_solution(331160082406116112)
XLA Ops:
  0.6 1.1 %edge_y.1 = (f32[9,4,128]{2,1,0:T(4,128)S(1)}, f32[9,4,128]{2,1,0:T(4,128)S(1)}, f32[8,32,128]{2,1,0:T(8,128)S(1)}, s32[8,32,64]{2,1,0:T(8,128)S(1)}, f32[8,128]{1,0:T(8,128)S(1)}) custom-call(f32[8,32,128]{2,1,0:T(8,128)} %noise_far.1, s32[8,32,64]{2,1,0:T(8,128)} %classes_far.1, s32[8]{0:T(128)} %owner.1), custom_call_target="tpu_custom_call" | custom-call | tf_op jit(solution)/shard_map/edge_y/pallas_call | solution.py:577
  1.7 3.3 %collective-permute-start = (f32[9,4,128]{2,1,0:T(4,128)S(1)}, f32[9,4,128]{2,1,0:T(4,128)S(1)}, u32[]{:S(2)}, u32[]{:S(2)}) collective-permute-start(f32[9,4,128]{2,1,0:T(4,128)S(1)} %get-tuple-element.37), channel_id=1, source_target_pairs={{0,1},{1,0},{2,3},{3,2},{4,5},{5,4},{6,7},{7,6},{8,9},{9,8},{10,11... | collective-permute-start | bytes 55304 | tf_op jit(solution)/shard_map/ppermute | solution.py:40
  5.1 0.0 collective-permute-start.1
  5.1 0.8 %prepare.1 = (f32[8,40,128]{2,1,0:T(8,128)S(1)}, f32[8,40,128]{2,1,0:T(8,128)S(1)}, f32[27,8,128]{2,1,0:T(8,128)S(1)}) custom-call(f32[8,32,128]{2,1,0:T(8,128)S(1)} %get-tuple-element.32.noise, s32[8,32,64]{2,1,0:T(8,128)S(1)} %get-tuple-element.33.classes, f32[8,27]{1,0:T(8,128)} %table.1), custom_call_target="tpu_custom_call" | custom-call | tf_op jit(solution)/shard_map/prepare/pallas_call | solution.py:591
  5.9 0.0 collective-permute-done.even_in
  5.9 2.6 %collective-permute-done.1.odd_in = f32[9,4,128]{2,1,0:T(4,128)S(1)} collective-permute-done((f32[9,4,128]{2,1,0:T(4,128)S(1)}, f32[9,4,128]{2,1,0:T(4,128)S(1)}, u32[]{:S(2)}, u32[]{:S(2)}) %collective-permute-start.1) | collective-permute-done | bytes 18464 | tf_op jit(solution)/shard_map/ppermute | solution.py:40
  8.5 0.3 edge_x.1
  8.9 0.5 collective-permute-start.3
  9.3 4.9 %collective-permute-start.2 = (f32[136,128]{1,0:T(8,128)S(1)}, f32[136,128]{1,0:T(8,128)S(1)}, u32[]{:S(2)}, u32[]{:S(2)}) collective-permute-start(f32[136,128]{1,0:T(8,128)S(1)} %get-tuple-element.41), channel_id=1, source_target_pairs={{0,8},{8,0},{16,24},{24,16},{32,40},{40,32},{48,56},{56,48},{1,9},... | collective-permute-start | bytes 208904 | tf_op jit(solution)/shard_map/ppermute | solution.py:40
  14.2 2.7 %interior.1 = (f32[27,8,40,128]{3,2,1,0:T(8,128)S(1)}, f32[3,8,40,128]{3,2,1,0:T(8,128)S(1)}, f32[3,6,40,128]{3,2,1,0:T(8,128)S(1)}, f32[3,4,40,128]{3,2,1,0:T(8...) custom-call(f32[8,40,128]{2,1,0:T(8,128)S(1)} %get-tuple-element.43., ...), custom_call_target="tpu_custom_call" | custom-call | tf_op jit(solution)/shard_map/interior/pallas_call | solution.py:607
  16.9 0.0 collective-permute-done.3.edges
  16.9 0.6 %lower.1 = f32[12,8,128]{2,1,0:T(8,128)S(1)} custom-call(f32[8,40,128]{2,1,0:T(8,128)S(1)} %get-tuple-element.40.kinds, f32[136,128]{1,0:T(8,128)S(1)} %collective-permute-done.3.edges, f32[27,8,40,128]{3,2,1,0:T(8,128)S(1)} %get-tuple-element.44.weights, f32[3,8,40,128]{3,2,1,0:T(8,128)S(1)} %get-tuple-element.45.first, ...), custom_call_target="tpu_custom_call" | custom-call | tf_op jit(solution)/shard_map/lower/pallas_call | solution.py:632
  17.6 0.3 collective-permute-done.2.edges
  17.8 1.6 %finish.1 = (f32[32,8,128]{2,1,0:T(8,128)S(1)}, f32[24,256]{1,0:T(8,128)S(1)}, f32[8,128]{1,0:T(8,128)S(1)}) custom-call(f32[8,40,128]{2,1,0:T(8,128)S(1)} %get-tuple-element.40.kinds, f32[136,128]{1,0:T(8,128)S(1)} %collective-permute-done.2.edges, f32[4,128]{1,0:T(4,128)S(1)} %get-tuple-element.42.near, f32[27,8,40,128]{3,2,1,0:T(8,128)S(1)} %get-tuple-element.44.weights, ...), custom_call_target="tpu_custom_call" | custom-call | tf_op jit(solution)/shard_map/finish/pallas_call | solution.py:636
  19.5 17.8 %all_to_all.5.here = f32[16,24,256]{2,1,0:T(8,128)S(1)} all-to-all(f32[16,24,256]{2,1,0:T(8,128)S(1)} %broadcast_in_dim.2), channel_id=1, replica_groups=mesh['real'=4,'x'=4,'zh'=2,'y'=4,'core'=2] {'x','y'}, dimensions={0} | all-to-all | bytes 786432 | tf_op jit(solution)/shard_map/all_to_all | solution.py:646
  37.4 0.3 collect.1
  37.6 4.3 %collective-permute-start.4 = (f32[2,32,256]{2,1,0:T(8,128)S(1)}, f32[2,32,256]{2,1,0:T(8,128)S(1)}, u32[]{:S(2)}, u32[]{:S(2)}) collective-permute-start(f32[2,32,256]{2,1,0:T(8,128)S(1)} %get-tuple-element.57), channel_id=1, source_target_pairs={{0,1},{1,0},{2,3},{3,2},{4,5},{5,4},{6,7},{7,6},{8,9},{9,8},{10,11... | collective-permute-start | bytes 196616 | tf_op jit(solution)/shard_map/ppermute | solution.py:40
  41.9 0.9 %collective-permute-done.4.near = f32[2,32,256]{2,1,0:T(8,128)S(1)} collective-permute-done((f32[2,32,256]{2,1,0:T(8,128)S(1)}, f32[2,32,256]{2,1,0:T(8,128)S(1)}, u32[]{:S(2)}, u32[]{:S(2)}) %collective-permute-start.4) | collective-permute-done | bytes 65568 | tf_op jit(solution)/shard_map/ppermute | solution.py:40
  42.8 2.4 %collective-permute-start.5 = (f32[32,256]{1,0:T(8,128)S(1)}, f32[32,256]{1,0:T(8,128)S(1)}, u32[]{:S(2)}, u32[]{:S(2)}) collective-permute-start(f32[32,256]{1,0:T(8,128)S(1)} %fusion), channel_id=1, source_target_pairs={{0,8},{8,0},{1,9},{9,1},{2,10},{10,2},{3,11},{11,3},{4,12},{12,4},... | collective-permute-start | bytes 98312 | tf_op jit(solution)/shard_map/ppermute | solution.py:40
  45.2 4.4 %collective-permute-done.5.far = f32[32,256]{1,0:T(8,128)S(1)} collective-permute-done((f32[32,256]{1,0:T(8,128)S(1)}, f32[32,256]{1,0:T(8,128)S(1)}, u32[]{:S(2)}, u32[]{:S(2)}) %collective-permute-start.5) | collective-permute-done | bytes 32800 | tf_op jit(solution)/shard_map/ppermute | solution.py:40
  49.6 1.5 %update.1 = (f32[32,8,128]{2,1,0:T(8,128)}, f32[2,2,256]{2,1,0:T(2,128)}) custom-call(f32[2,32,256]{2,1,0:T(8,128)S(1)} %get-tuple-element.56.keep, f32[2,32,256]{2,1,0:T(8,128)S(1)} %collective-permute-done.4.near, f32[32,256]{1,0:T(8,128)S(1)} %collective-permute-done.5.far, f32[32,8,128]{2,1,0:T(8,128)S(1)} %get-tuple-element.58.smooth, ...), custom_call_target="tpu_custom_call" | custom-call | tf_op jit(solution)/shard_map/update/pallas_call | solution.py:654
  (2 shorter events, 0.0 us)
Async XLA Ops:
  1.7 4.2 %collective-permute-start = (f32[9,4,128]{2,1,0:T(4,128)S(1)}, f32[9,4,128]{2,1,0:T(4,128)S(1)}, u32[]{:S(2)}, u32[]{:S(2)}) collective-permute-start(f32[9,4,128]{2,1,0:T(4,128)S(1)} %get-tuple-element.37), channel_id=1, source_target_pairs={{0,1},{1,0},{2,3},{3,2},{4,5},{5,4},{6,7},{7,6},{8,9},{9,8},{10,11... | collective-permute-start | bytes 55304 | tf_op jit(solution)/shard_map/ppermute | solution.py:40
  5.1 3.5 %collective-permute-start.1 = (f32[9,4,128]{2,1,0:T(4,128)S(1)}, f32[9,4,128]{2,1,0:T(4,128)S(1)}, u32[]{:S(2)}, u32[]{:S(2)}) collective-permute-start(f32[9,4,128]{2,1,0:T(4,128)S(1)} %get-tuple-element.38), channel_id=1, source_target_pairs={{0,16},{1,2},{2,1},{3,4},{4,3},{5,6},{6,5},{7,23},{16,0},{17,18},{... | collective-permute-start | bytes 55304 | tf_op jit(solution)/shard_map/ppermute | solution.py:40
  8.9 8.1 %collective-permute-start.3 = (f32[136,128]{1,0:T(8,128)S(1)}, f32[136,128]{1,0:T(8,128)S(1)}, u32[]{:S(2)}, u32[]{:S(2)}) collective-permute-start(f32[136,128]{1,0:T(8,128)S(1)} %get-tuple-element.49), channel_id=1, source_target_pairs={{0,1},{1,0},{8,16},{9,17},{16,8},{17,9},{24,32},{25,33},{32,24},{3... | collective-permute-start | bytes 208904 | tf_op jit(solution)/shard_map/ppermute | solution.py:40
  9.3 8.5 %collective-permute-start.2 = (f32[136,128]{1,0:T(8,128)S(1)}, f32[136,128]{1,0:T(8,128)S(1)}, u32[]{:S(2)}, u32[]{:S(2)}) collective-permute-start(f32[136,128]{1,0:T(8,128)S(1)} %get-tuple-element.41), channel_id=1, source_target_pairs={{0,8},{8,0},{16,24},{24,16},{32,40},{40,32},{48,56},{56,48},{1,9},... | collective-permute-start | bytes 208904 | tf_op jit(solution)/shard_map/ppermute | solution.py:40
  37.6 5.2 %collective-permute-start.4 = (f32[2,32,256]{2,1,0:T(8,128)S(1)}, f32[2,32,256]{2,1,0:T(8,128)S(1)}, u32[]{:S(2)}, u32[]{:S(2)}) collective-permute-start(f32[2,32,256]{2,1,0:T(8,128)S(1)} %get-tuple-element.57), channel_id=1, source_target_pairs={{0,1},{1,0},{2,3},{3,2},{4,5},{5,4},{6,7},{7,6},{8,9},{9,8},{10,11... | collective-permute-start | bytes 196616 | tf_op jit(solution)/shard_map/ppermute | solution.py:40
  42.8 6.8 %collective-permute-start.5 = (f32[32,256]{1,0:T(8,128)S(1)}, f32[32,256]{1,0:T(8,128)S(1)}, u32[]{:S(2)}, u32[]{:S(2)}) collective-permute-start(f32[32,256]{1,0:T(8,128)S(1)} %fusion), channel_id=1, source_target_pairs={{0,8},{8,0},{1,9},{9,1},{2,10},{10,2},{3,11},{11,3},{4,12},{12,4},... | collective-permute-start | bytes 98312 | tf_op jit(solution)/shard_map/ppermute | solution.py:40

commit v7 on v6

--- a/solution.py
+++ b/solution.py
@@ -89,23 +89,19 @@
 
 def edge_y_kernel(
     noise_far, classes_far, owner_far,
-    odd, even, noise, classes, names,
+    odd, even, names,
     noise_edges, class_edges, owner, sems,
 ):
-    first = [
+    copies = [
         pltpu.make_async_copy(noise_far.at[:, 0:8, :], noise_edges.at[0], sems.at[0]),
         pltpu.make_async_copy(noise_far.at[:, Y - 8 : Y, :], noise_edges.at[1], sems.at[1]),
         pltpu.make_async_copy(classes_far.at[:, 0:8, :], class_edges.at[0], sems.at[2]),
         pltpu.make_async_copy(classes_far.at[:, Y - 8 : Y, :], class_edges.at[1], sems.at[3]),
         pltpu.make_async_copy(owner_far, owner, sems.at[4]),
     ]
-    rest = [
-        pltpu.make_async_copy(noise_far, noise, sems.at[5]),
-        pltpu.make_async_copy(classes_far, classes, sems.at[6]),
-    ]
-    for copy in first + rest:
+    for copy in copies:
         copy.start()
-    for copy in first:
+    for copy in copies:
         copy.wait()
     core = whereabouts()[1]
     lane = lax.broadcasted_iota(jnp.int32, (8, W), 1)
@@ -131,13 +127,19 @@
         message(even, 0, 0, 0, 1)
         message(odd, 1, 5, 6, 7)
 
-    for copy in rest:
+
+def prepare_kernel(
+    noise_far, classes_far, table, field, kinds, tables, noise, classes, held_table, sems
+):
+    copies = [
+        pltpu.make_async_copy(noise_far, noise, sems.at[0]),
+        pltpu.make_async_copy(classes_far, classes, sems.at[1]),
+        pltpu.make_async_copy(table, held_table, sems.at[2]),
+    ]
+    for copy in copies:
+        copy.start()
+    for copy in copies:
         copy.wait()
-
-
-def prepare_kernel(noise, classes, table, field, kinds, tables, held_table, sem):
-    copy = pltpu.make_async_copy(table, held_table, sem)
-    copy.start()
     half = whereabouts()[0]
     for out in (field, kinds):
         out[:, 0:8, :] = jnp.zeros((X, 8, W), F32)
@@ -147,12 +149,11 @@
         field[x, OFF : OFF + Y, :] = noise[true]
         kind = (classes[true] + 1).astype(F32)
         kinds[x, OFF : OFF + Y, :] = jnp.concatenate([kind, kind], axis=-1)
-    copy.wait()
     spread_table(held_table, half, tables)
 
 
 def edge_x_kernel(
-    field_in, kinds_in, names, even_in, odd_in, tables,
+    odd_in, even_in, field_in, kinds_in, names, tables,
     field, kinds, odd, even, lists,
     weights, moved,
 ):
@@ -574,16 +575,16 @@
             noise, classes, table, obs_matrix, node_block, sample_block, sample_count, drill_data, obs_gain
         )
     ]
-    odd, even, near_noise, near_classes, names = call(
+    odd, even, names = call(
         edge_y_kernel,
-        (shape(X + 1, 4, W), shape(X + 1, 4, W), shape(X, Y, W), shape(X, Y, Z, dtype=jnp.int32), shape(8, W)),
+        (shape(X + 1, 4, W), shape(X + 1, 4, W), shape(8, W)),
         [HBM] * 3,
         "edge_y",
         [
             pltpu.VMEM((2, X, 8, W), F32),
             pltpu.VMEM((2, X, 8, Z), jnp.int32),
             pltpu.SMEM((BLOCKS,), jnp.int32),
-            pltpu.SemaphoreType.DMA((7,)),
+            pltpu.SemaphoreType.DMA((5,)),
         ],
     )(noise, classes, owner)
     odd = permute(odd, ("x", "y", "core"), odd_along_y)
@@ -591,17 +592,22 @@
     field, kinds, tables = call(
         prepare_kernel,
         (shape(X, YP, W), shape(X, YP, W), shape(27, 8, W)),
-        [VMEM] * 2 + [HBM],
+        [HBM] * 3,
         "prepare",
-        [pltpu.VMEM((8, 27), F32), pltpu.SemaphoreType.DMA],
-    )(near_noise, near_classes, table)
+        [
+            pltpu.VMEM((X, Y, W), F32),
+            pltpu.VMEM((X, Y, Z), jnp.int32),
+            pltpu.VMEM((8, 27), F32),
+            pltpu.SemaphoreType.DMA((3,)),
+        ],
+    )(noise, classes, table)
     field, kinds, odd, even, lists = call(
         edge_x_kernel,
         (shape(X, YP, W), shape(X, YP, W), shape(MESSAGE, W), shape(MESSAGE, W), shape(4, W)),
         [VMEM] * 6,
         "edge_x",
         [pltpu.VMEM((27, YP, W), F32), pltpu.VMEM((3, 3, YP, W), F32)],
-    )(field, kinds, names, even, odd, tables)
+    )(odd, even, field, kinds, names, tables)
     odd = permute(odd, ("x", "zh", "core"), odd_along_x)
     even = permute(even, ("x", "zh"), even_pair)
     weights, first, second, third, middle, matrix, rows, other, live, blocks = call(

time: 51.2 us -> 51 us (level)
  waiting for transfers between devices: 8.17 us -> 6.26 us
  starting transfers between devices: 15.3 us -> 16.8 us
    ppermute x6, waiting for transfers between devices: 8.17 us -> 6.26 us  [permute(): return lax.ppermute(value, axes if len(axes) > 1 else axes[0], pairs)]
    ppermute x6, starting transfers between devices: 15.3 us -> 16.8 us  [permute(): return lax.ppermute(value, axes if len(axes) > 1 else axes[0], pairs)]
  transfers between devices with their start and end apart: 6 -> 6, of which waited for: 4 -> 3; matrix products, arithmetic and copies ran while one was open for 0% -> 0% of each run, Pallas kernels for 8% -> 9%
where the time goes in v7:
time: 51 us; the launch traced here: 50.8 us
  blocking collectives  17.8 us (35%)
  starting transfers between devices  16.8 us (33%)
  Pallas kernels  9.13 us (18%)
  waiting for transfers between devices  6.26 us (12%)
  between operations  0.72 us (1%)
    all_to_all x1, blocking collectives, shards(): lax.all_to_all(jnp.broadcast_to(payload[None], (16, ROWS, SAMPLES)), ('x'...  17.8 us
    ppermute x6, starting transfers between devices, permute(): return lax.ppermute(value, axes if len(axes) > 1 else axes[0], pairs)  16.8 us
    ppermute x6, waiting for transfers between devices, permute(): return lax.ppermute(value, axes if len(axes) > 1 else axes[0], pairs)  6.26 us
    pallas_call x1, Pallas kernels, shards(): call(interior_kernel, (shape(27, X, YP, W), shape(3, X, YP, W), shape(3,...  2.71 us
    pallas_call x1, Pallas kernels, shards(): call(finish_kernel, (shape(32, 8, W), shape(ROWS, SAMPLES), shape(8, W)),...  1.64 us
    pallas_call x1, Pallas kernels, shards(): call(update_kernel, (shape(32, 8, W), shape(2, 2, SAMPLES)), [VMEM] * 8,...  1.47 us
    pallas_call x1, Pallas kernels, shards(): call(prepare_kernel, (shape(X, YP, W), shape(X, YP, W), shape(27, 8, W)),...  1.15 us
  transfers between devices with their start and end apart: 6, of which 3 were waited for; matrix products, arithmetic and copies ran while one was open for 0% of the time, Pallas kernels for 9%

profile of v7, /device:TPU:1, one launch (start us, length us, event | category | flops | bytes accessed | tf_op | source)
XLA Modules:
  0.0 50.8 jit_solution(16936882801460890187)
XLA Ops:
  0.6 1.0 %edge_y.1 = (f32[9,4,128]{2,1,0:T(4,128)S(1)}, f32[9,4,128]{2,1,0:T(4,128)S(1)}, f32[8,128]{1,0:T(8,128)S(1)}) custom-call(f32[8,32,128]{2,1,0:T(8,128)} %noise_far.3, s32[8,32,64]{2,1,0:T(8,128)} %classes_far.3, s32[8]{0:T(128)} %owner.1), custom_call_target="tpu_custom_call" | custom-call | tf_op jit(solution)/shard_map/edge_y/pallas_call | solution.py:578
  1.6 2.8 %collective-permute-start = (f32[9,4,128]{2,1,0:T(4,128)S(1)}, f32[9,4,128]{2,1,0:T(4,128)S(1)}, u32[]{:S(2)}, u32[]{:S(2)}) collective-permute-start(f32[9,4,128]{2,1,0:T(4,128)S(1)} %get-tuple-element.30), channel_id=1, source_target_pairs={{0,16},{1,2},{2,1},{3,4},{4,3},{5,6},{6,5},{7,23},{16,0},{17,18},{... | collective-permute-start | bytes 55304 | tf_op jit(solution)/shard_map/ppermute | solution.py:40
  4.4 0.7 %collective-permute-start.1 = (f32[9,4,128]{2,1,0:T(4,128)S(1)}, f32[9,4,128]{2,1,0:T(4,128)S(1)}, u32[]{:S(2)}, u32[]{:S(2)}) collective-permute-start(f32[9,4,128]{2,1,0:T(4,128)S(1)} %get-tuple-element.31), channel_id=1, source_target_pairs={{0,1},{1,0},{2,3},{3,2},{4,5},{5,4},{6,7},{7,6},{8,9},{9,8},{10,11... | collective-permute-start | bytes 55304 | tf_op jit(solution)/shard_map/ppermute | solution.py:40
  5.0 1.2 %prepare.1 = (f32[8,40,128]{2,1,0:T(8,128)S(1)}, f32[8,40,128]{2,1,0:T(8,128)S(1)}, f32[27,8,128]{2,1,0:T(8,128)S(1)}) custom-call(f32[8,32,128]{2,1,0:T(8,128)} %noise_far.3, s32[8,32,64]{2,1,0:T(8,128)} %classes_far.3, f32[8,27]{1,0:T(8,128)} %table.1), custom_call_target="tpu_custom_call" | custom-call | tf_op jit(solution)/shard_map/prepare/pallas_call | solution.py:592
  6.2 0.0 collective-permute-done.odd_in
  6.2 0.0 collective-permute-done.1.even_in
  6.2 0.3 edge_x.1
  6.5 2.6 %collective-permute-start.3 = (f32[136,128]{1,0:T(8,128)S(1)}, f32[136,128]{1,0:T(8,128)S(1)}, u32[]{:S(2)}, u32[]{:S(2)}) collective-permute-start(f32[136,128]{1,0:T(8,128)S(1)} %get-tuple-element.45), channel_id=1, source_target_pairs={{0,1},{1,0},{8,16},{9,17},{16,8},{17,9},{24,32},{25,33},{32,24},{3... | collective-permute-start | bytes 208904 | tf_op jit(solution)/shard_map/ppermute | solution.py:40
  9.1 4.3 %collective-permute-start.2 = (f32[136,128]{1,0:T(8,128)S(1)}, f32[136,128]{1,0:T(8,128)S(1)}, u32[]{:S(2)}, u32[]{:S(2)}) collective-permute-start(f32[136,128]{1,0:T(8,128)S(1)} %get-tuple-element.37), channel_id=1, source_target_pairs={{0,8},{8,0},{16,24},{24,16},{32,40},{40,32},{48,56},{56,48},{1,9},... | collective-permute-start | bytes 208904 | tf_op jit(solution)/shard_map/ppermute | solution.py:40
  13.3 2.7 %interior.1 = (f32[27,8,40,128]{3,2,1,0:T(8,128)S(1)}, f32[3,8,40,128]{3,2,1,0:T(8,128)S(1)}, f32[3,6,40,128]{3,2,1,0:T(8,128)S(1)}, f32[3,4,40,128]{3,2,1,0:T(8...) custom-call(f32[8,40,128]{2,1,0:T(8,128)S(1)} %get-tuple-element.39., ...), custom_call_target="tpu_custom_call" | custom-call | tf_op jit(solution)/shard_map/interior/pallas_call | solution.py:613
  16.1 0.0 collective-permute-done.3.edges
  16.1 0.6 %lower.1 = f32[12,8,128]{2,1,0:T(8,128)S(1)} custom-call(f32[8,40,128]{2,1,0:T(8,128)S(1)} %get-tuple-element.36.kinds, f32[136,128]{1,0:T(8,128)S(1)} %collective-permute-done.3.edges, f32[27,8,40,128]{3,2,1,0:T(8,128)S(1)} %get-tuple-element.40.weights, f32[3,8,40,128]{3,2,1,0:T(8,128)S(1)} %get-tuple-element.41.first, ...), custom_call_target="tpu_custom_call" | custom-call | tf_op jit(solution)/shard_map/lower/pallas_call | solution.py:638
  16.7 0.5 collective-permute-done.2.edges
  17.2 1.6 %finish.1 = (f32[32,8,128]{2,1,0:T(8,128)S(1)}, f32[24,256]{1,0:T(8,128)S(1)}, f32[8,128]{1,0:T(8,128)S(1)}) custom-call(f32[8,40,128]{2,1,0:T(8,128)S(1)} %get-tuple-element.36.kinds, f32[136,128]{1,0:T(8,128)S(1)} %collective-permute-done.2.edges, f32[4,128]{1,0:T(4,128)S(1)} %get-tuple-element.38.near, f32[27,8,40,128]{3,2,1,0:T(8,128)S(1)} %get-tuple-element.40.weights, ...), custom_call_target="tpu_custom_call" | custom-call | tf_op jit(solution)/shard_map/finish/pallas_call | solution.py:642
  18.9 17.8 %all_to_all.5.here = f32[16,24,256]{2,1,0:T(8,128)S(1)} all-to-all(f32[16,24,256]{2,1,0:T(8,128)S(1)} %broadcast_in_dim.2), channel_id=1, replica_groups=mesh['real'=4,'x'=4,'zh'=2,'y'=4,'core'=2] {'x','y'}, dimensions={0} | all-to-all | bytes 786432 | tf_op jit(solution)/shard_map/all_to_all | solution.py:652
  36.7 0.3 collect.1
  36.9 4.7 %collective-permute-start.4 = (f32[2,32,256]{2,1,0:T(8,128)S(1)}, f32[2,32,256]{2,1,0:T(8,128)S(1)}, u32[]{:S(2)}, u32[]{:S(2)}) collective-permute-start(f32[2,32,256]{2,1,0:T(8,128)S(1)} %get-tuple-element.53), channel_id=1, source_target_pairs={{0,1},{1,0},{2,3},{3,2},{4,5},{5,4},{6,7},{7,6},{8,9},{9,8},{10,11... | collective-permute-start | bytes 196616 | tf_op jit(solution)/shard_map/ppermute | solution.py:40
  41.6 0.9 %collective-permute-done.4.near = f32[2,32,256]{2,1,0:T(8,128)S(1)} collective-permute-done((f32[2,32,256]{2,1,0:T(8,128)S(1)}, f32[2,32,256]{2,1,0:T(8,128)S(1)}, u32[]{:S(2)}, u32[]{:S(2)}) %collective-permute-start.4) | collective-permute-done | bytes 65568 | tf_op jit(solution)/shard_map/ppermute | solution.py:40
  42.5 1.9 %collective-permute-start.5 = (f32[32,256]{1,0:T(8,128)S(1)}, f32[32,256]{1,0:T(8,128)S(1)}, u32[]{:S(2)}, u32[]{:S(2)}) collective-permute-start(f32[32,256]{1,0:T(8,128)S(1)} %fusion), channel_id=1, source_target_pairs={{0,8},{8,0},{1,9},{9,1},{2,10},{10,2},{3,11},{11,3},{4,12},{12,4},... | collective-permute-start | bytes 98312 | tf_op jit(solution)/shard_map/ppermute | solution.py:40
  44.4 4.8 %collective-permute-done.5.far = f32[32,256]{1,0:T(8,128)S(1)} collective-permute-done((f32[32,256]{1,0:T(8,128)S(1)}, f32[32,256]{1,0:T(8,128)S(1)}, u32[]{:S(2)}, u32[]{:S(2)}) %collective-permute-start.5) | collective-permute-done | bytes 32800 | tf_op jit(solution)/shard_map/ppermute | solution.py:40
  49.3 1.5 %update.1 = (f32[32,8,128]{2,1,0:T(8,128)}, f32[2,2,256]{2,1,0:T(2,128)}) custom-call(f32[2,32,256]{2,1,0:T(8,128)S(1)} %get-tuple-element.52.keep, f32[2,32,256]{2,1,0:T(8,128)S(1)} %collective-permute-done.4.near, f32[32,256]{1,0:T(8,128)S(1)} %collective-permute-done.5.far, f32[32,8,128]{2,1,0:T(8,128)S(1)} %get-tuple-element.54.smooth, ...), custom_call_target="tpu_custom_call" | custom-call | tf_op jit(solution)/shard_map/update/pallas_call | solution.py:660
  (2 shorter events, 0.0 us)
Async XLA Ops:
  1.6 4.6 %collective-permute-start = (f32[9,4,128]{2,1,0:T(4,128)S(1)}, f32[9,4,128]{2,1,0:T(4,128)S(1)}, u32[]{:S(2)}, u32[]{:S(2)}) collective-permute-start(f32[9,4,128]{2,1,0:T(4,128)S(1)} %get-tuple-element.30), channel_id=1, source_target_pairs={{0,16},{1,2},{2,1},{3,4},{4,3},{5,6},{6,5},{7,23},{16,0},{17,18},{... | collective-permute-start | bytes 55304 | tf_op jit(solution)/shard_map/ppermute | solution.py:40
  4.4 1.8 %collective-permute-start.1 = (f32[9,4,128]{2,1,0:T(4,128)S(1)}, f32[9,4,128]{2,1,0:T(4,128)S(1)}, u32[]{:S(2)}, u32[]{:S(2)}) collective-permute-start(f32[9,4,128]{2,1,0:T(4,128)S(1)} %get-tuple-element.31), channel_id=1, source_target_pairs={{0,1},{1,0},{2,3},{3,2},{4,5},{5,4},{6,7},{7,6},{8,9},{9,8},{10,11... | collective-permute-start | bytes 55304 | tf_op jit(solution)/shard_map/ppermute | solution.py:40
  6.5 9.5 %collective-permute-start.3 = (f32[136,128]{1,0:T(8,128)S(1)}, f32[136,128]{1,0:T(8,128)S(1)}, u32[]{:S(2)}, u32[]{:S(2)}) collective-permute-start(f32[136,128]{1,0:T(8,128)S(1)} %get-tuple-element.45), channel_id=1, source_target_pairs={{0,1},{1,0},{8,16},{9,17},{16,8},{17,9},{24,32},{25,33},{32,24},{3... | collective-permute-start | bytes 208904 | tf_op jit(solution)/shard_map/ppermute | solution.py:40
  9.1 8.1 %collective-permute-start.2 = (f32[136,128]{1,0:T(8,128)S(1)}, f32[136,128]{1,0:T(8,128)S(1)}, u32[]{:S(2)}, u32[]{:S(2)}) collective-permute-start(f32[136,128]{1,0:T(8,128)S(1)} %get-tuple-element.37), channel_id=1, source_target_pairs={{0,8},{8,0},{16,24},{24,16},{32,40},{40,32},{48,56},{56,48},{1,9},... | collective-permute-start | bytes 208904 | tf_op jit(solution)/shard_map/ppermute | solution.py:40
  36.9 5.6 %collective-permute-start.4 = (f32[2,32,256]{2,1,0:T(8,128)S(1)}, f32[2,32,256]{2,1,0:T(8,128)S(1)}, u32[]{:S(2)}, u32[]{:S(2)}) collective-permute-start(f32[2,32,256]{2,1,0:T(8,128)S(1)} %get-tuple-element.53), channel_id=1, source_target_pairs={{0,1},{1,0},{2,3},{3,2},{4,5},{5,4},{6,7},{7,6},{8,9},{9,8},{10,11... | collective-permute-start | bytes 196616 | tf_op jit(solution)/shard_map/ppermute | solution.py:40
  42.5 6.7 %collective-permute-start.5 = (f32[32,256]{1,0:T(8,128)S(1)}, f32[32,256]{1,0:T(8,128)S(1)}, u32[]{:S(2)}, u32[]{:S(2)}) collective-permute-start(f32[32,256]{1,0:T(8,128)S(1)} %fusion), channel_id=1, source_target_pairs={{0,8},{8,0},{1,9},{9,1},{2,10},{10,2},{3,11},{11,3},{4,12},{12,4},... | collective-permute-start | bytes 98312 | tf_op jit(solution)/shard_map/ppermute | solution.py:40

commit v8 on v7

--- a/solution.py
+++ b/solution.py
@@ -15,7 +15,7 @@
 BLOCKS = 8
 SAMPLES = 256
 NODES = 512
-ROWS = 24
+GROUPS = 11
 MESSAGE = 136
 F32 = jnp.float32
 VMEM = pl.BlockSpec(memory_space=pltpu.VMEM)
@@ -266,7 +266,7 @@
 
 def interior_kernel(
     field, kinds, tables, matrix, drill, gain, node_block, count, owner,
-    weights, first, second, third, smooth, held_matrix, held_rows, other, live, blocks,
+    weights, first, second, third, smooth, held_matrix, turned, held_rows, other, live, blocks,
     scalars, sems,
 ):
     copies = [
@@ -277,7 +277,7 @@
         pltpu.make_async_copy(count, scalars.at[1], sems.at[4]),
         pltpu.make_async_copy(owner, scalars.at[2], sems.at[5]),
     ]
-    for copy in reversed(copies):
+    for copy in copies:
         copy.start()
     plane = whereabouts()[2]
     for x in range(X):
@@ -311,6 +311,8 @@
             smooth[4 * (x - 3) + g] = result[OFF + 8 * g : OFF + 8 * g + 8]
     for copy in copies:
         copy.wait()
+    for b in range(BLOCKS):
+        turned[b] = held_matrix[b].T
     other[...] = jnp.zeros((8, SAMPLES), F32)
     for k in range(2):
         for h in range(2):
@@ -410,7 +412,7 @@
 
 
 def finish_kernel(
-    kinds, edges, near, weights, first, second, third, middle, lower, tables, matrix, other, live, blocks,
+    kinds, edges, near, weights, first, second, third, middle, lower, tables, turned, other, live, blocks,
     smooth, payload, lists,
     halo_kinds, halo_weights, halo_first, edge_second, edge_third, chosen, node_block, sem,
 ):
@@ -451,21 +453,25 @@
     block = lax.broadcasted_iota(jnp.int32, (BLOCKS, SAMPLES), 0)
     sums = [jnp.zeros((BLOCKS, SAMPLES), F32) for _ in range(2)]
     for b in range(BLOCKS):
-        product = lax.dot_general(
-            left, matrix[b], (((1,), (1,)), ((), ())), preferred_element_type=F32
-        )
+        product = jnp.dot(left, turned[b], preferred_element_type=F32)
         for r in range(2):
             both = product[8 * r : 8 * r + 8] + product[16 + 8 * r : 24 + 8 * r]
             sums[r] = jnp.where(block == b, both, sums[r])
+    tiles = []
     for r in range(2):
-        payload[8 * r : 8 * r + 8, :] = jnp.where(live[...] > 0.0, sums[r], 0.0)
-    payload[16:24, :] = other[...]
+        told = jnp.where(live[...] > 0.0, sums[r], 0.0)
+        tiles += [told[:, 0:W], told[:, W : 2 * W]]
+    tiles.append(other[:, 0:W])
+    for n, tile in enumerate(tiles):
+        payload[2 * n] = tile[0:4]
+        payload[2 * n + 1] = tile[4:8]
+    payload[10] = other[0:4, W : 2 * W]
 
 
 def collect_kernel(lists, here, keep, send):
-    names = here[0, 16:24, W : 2 * W]
+    names = here[0, 10]
     for n in range(1, 16):
-        names = names + here[n, 16:24, W : 2 * W]
+        names = names + here[n, 10]
     names = jnp.broadcast_to(names[0:1], (8, W))
     lane = lax.broadcasted_iota(jnp.int32, (8, W), 1)
     row = lax.broadcasted_iota(jnp.int32, (8, W), 0)
@@ -490,15 +496,19 @@
         [(lane == spots + 4 * kind + h).astype(F32) for kind in range(2) for h in range(2)], axis=0
     ).astype(jnp.bfloat16)
 
-    def gather(left, rows, lanes):
-        data = jnp.concatenate([here[n, rows, lanes] for n in range(16)], axis=0)
+    def column(tile):
+        return jnp.concatenate([here[n, 2 * tile + k] for n in range(16) for k in range(2)], axis=0)
+
+    def gather(left, data):
         high, low = split(data)
         return jnp.dot(left, high, preferred_element_type=F32) + jnp.dot(
             left, low, preferred_element_type=F32
         )
 
-    totals = [gather(hit, slice(8 * r, 8 * r + 8), slice(0, 2 * W)) for r in range(2)]
-    found = gather(choose, slice(16, 24), slice(0, W))
+    totals = [
+        gather(hit, jnp.concatenate([column(2 * r), column(2 * r + 1)], axis=1)) for r in range(2)
+    ]
+    found = gather(choose, column(4))
     row = lax.broadcasted_iota(jnp.int32, (8, SAMPLES), 0)
     for member in range(4):
         out = (send if member & 1 else keep).at[member // 2]
@@ -610,7 +620,7 @@
     )(odd, even, field, kinds, names, tables)
     odd = permute(odd, ("x", "zh", "core"), odd_along_x)
     even = permute(even, ("x", "zh"), even_pair)
-    weights, first, second, third, middle, matrix, rows, other, live, blocks = call(
+    weights, first, second, third, middle, matrix, turned, rows, other, live, blocks = call(
         interior_kernel,
         (
             shape(27, X, YP, W),
@@ -619,6 +629,7 @@
             shape(3, 4, YP, W),
             shape(8, 8, W),
             shape(BLOCKS, SAMPLES, NODES, dtype=jnp.bfloat16),
+            shape(BLOCKS, NODES, SAMPLES, dtype=jnp.bfloat16),
             shape(2, 2, SAMPLES),
             shape(8, SAMPLES),
             shape(BLOCKS, SAMPLES),
@@ -641,16 +652,16 @@
     index_scratch = [pltpu.SMEM((1, W), jnp.int32), pltpu.SemaphoreType.DMA]
     smooth, payload, lists = call(
         finish_kernel,
-        (shape(32, 8, W), shape(ROWS, SAMPLES), shape(8, W)),
+        (shape(32, 8, W), shape(GROUPS, 4, W), shape(8, W)),
         [VMEM] * 14,
         "finish",
         halo_scratch + [pltpu.VMEM((64, W), F32)] + index_scratch,
     )(
-        kinds, even, lists, weights, first, second, third, middle, lower, tables, matrix,
+        kinds, even, lists, weights, first, second, third, middle, lower, tables, turned,
         other, live, blocks,
     )
     here = lax.all_to_all(
-        jnp.broadcast_to(payload[None], (16, ROWS, SAMPLES)), ("x", "y"), 0, 0, tiled=True
+        jnp.broadcast_to(payload[None], (16, GROUPS, 4, W)), ("x", "y"), 0, 0, tiled=True
     )
     keep, send = call(
         collect_kernel, (shape(2, 32, SAMPLES), shape(2, 32, SAMPLES)), [VMEM] * 2, "collect"

time: 51 us -> 50.7 us (level)
  Pallas kernels: 9.13 us -> 8.5 us
  transfers between devices with their start and end apart: 6 -> 6, of which waited for: 3 -> 3; matrix products, arithmetic and copies ran while one was open for 0% -> 0% of each run, Pallas kernels for 9% -> 8%
where the time goes in v8:
time: 50.7 us; the launch traced here: 50.4 us
  blocking collectives  17.6 us (35%)
  starting transfers between devices  16.9 us (33%)
  Pallas kernels  8.5 us (17%)
  waiting for transfers between devices  6.69 us (13%)
  between operations  0.72 us (1%)
    all_to_all x1, blocking collectives, shards(): lax.all_to_all(jnp.broadcast_to(payload[None], (16, GROUPS, 4, W)), ('x',...  17.6 us
    ppermute x6, starting transfers between devices, permute(): return lax.ppermute(value, axes if len(axes) > 1 else axes[0], pairs)  16.9 us
    ppermute x6, waiting for transfers between devices, permute(): return lax.ppermute(value, axes if len(axes) > 1 else axes[0], pairs)  6.69 us
    pallas_call x1, Pallas kernels, shards(): call(interior_kernel, (shape(27, X, YP, W), shape(3, X, YP, W), shape(3,...  2.27 us
    pallas_call x1, Pallas kernels, shards(): call(update_kernel, (shape(32, 8, W), shape(2, 2, SAMPLES)), [VMEM] * 8,...  1.47 us
    pallas_call x1, Pallas kernels, shards(): call(finish_kernel, (shape(32, 8, W), shape(GROUPS, 4, W), shape(8, W)),...  1.43 us
    pallas_call x1, Pallas kernels, shards(): call(prepare_kernel, (shape(X, YP, W), shape(X, YP, W), shape(27, 8, W)),...  1.15 us
  transfers between devices with their start and end apart: 6, of which 3 were waited for; matrix products, arithmetic and copies ran while one was open for 0% of the time, Pallas kernels for 8%

profile of v8, /device:TPU:1, one launch (start us, length us, event | category | flops | bytes accessed | tf_op | source)
XLA Modules:
  0.0 50.4 jit_solution(2504473473830744101)
XLA Ops:
  0.6 1.0 %edge_y.1 = (f32[9,4,128]{2,1,0:T(4,128)S(1)}, f32[9,4,128]{2,1,0:T(4,128)S(1)}, f32[8,128]{1,0:T(8,128)S(1)}) custom-call(f32[8,32,128]{2,1,0:T(8,128)} %noise_far.3, s32[8,32,64]{2,1,0:T(8,128)} %classes_far.3, s32[8]{0:T(128)} %owner.1), custom_call_target="tpu_custom_call" | custom-call | tf_op jit(solution)/shard_map/edge_y/pallas_call | solution.py:588
  1.6 2.8 %collective-permute-start = (f32[9,4,128]{2,1,0:T(4,128)S(1)}, f32[9,4,128]{2,1,0:T(4,128)S(1)}, u32[]{:S(2)}, u32[]{:S(2)}) collective-permute-start(f32[9,4,128]{2,1,0:T(4,128)S(1)} %get-tuple-element.31), channel_id=1, source_target_pairs={{0,16},{1,2},{2,1},{3,4},{4,3},{5,6},{6,5},{7,23},{16,0},{17,18},{... | collective-permute-start | bytes 55304 | tf_op jit(solution)/shard_map/ppermute | solution.py:40
  4.4 0.7 %collective-permute-start.1 = (f32[9,4,128]{2,1,0:T(4,128)S(1)}, f32[9,4,128]{2,1,0:T(4,128)S(1)}, u32[]{:S(2)}, u32[]{:S(2)}) collective-permute-start(f32[9,4,128]{2,1,0:T(4,128)S(1)} %get-tuple-element.32), channel_id=1, source_target_pairs={{0,1},{1,0},{2,3},{3,2},{4,5},{5,4},{6,7},{7,6},{8,9},{9,8},{10,11... | collective-permute-start | bytes 55304 | tf_op jit(solution)/shard_map/ppermute | solution.py:40
  5.0 1.2 %prepare.1 = (f32[8,40,128]{2,1,0:T(8,128)S(1)}, f32[8,40,128]{2,1,0:T(8,128)S(1)}, f32[27,8,128]{2,1,0:T(8,128)S(1)}) custom-call(f32[8,32,128]{2,1,0:T(8,128)} %noise_far.3, s32[8,32,64]{2,1,0:T(8,128)} %classes_far.3, f32[8,27]{1,0:T(8,128)} %table.1), custom_call_target="tpu_custom_call" | custom-call | tf_op jit(solution)/shard_map/prepare/pallas_call | solution.py:602
  6.2 0.0 collective-permute-done.odd_in
  6.2 0.0 collective-permute-done.1.even_in
  6.2 0.3 edge_x.1
  6.5 2.6 %collective-permute-start.3 = (f32[136,128]{1,0:T(8,128)S(1)}, f32[136,128]{1,0:T(8,128)S(1)}, u32[]{:S(2)}, u32[]{:S(2)}) collective-permute-start(f32[136,128]{1,0:T(8,128)S(1)} %get-tuple-element.46), channel_id=1, source_target_pairs={{0,1},{1,0},{8,16},{9,17},{16,8},{17,9},{24,32},{25,33},{32,24},{3... | collective-permute-start | bytes 208904 | tf_op jit(solution)/shard_map/ppermute | solution.py:40
  9.1 4.3 %collective-permute-start.2 = (f32[136,128]{1,0:T(8,128)S(1)}, f32[136,128]{1,0:T(8,128)S(1)}, u32[]{:S(2)}, u32[]{:S(2)}) collective-permute-start(f32[136,128]{1,0:T(8,128)S(1)} %get-tuple-element.38), channel_id=1, source_target_pairs={{0,8},{8,0},{16,24},{24,16},{32,40},{40,32},{48,56},{56,48},{1,9},... | collective-permute-start | bytes 208904 | tf_op jit(solution)/shard_map/ppermute | solution.py:40
  13.3 2.3 %interior.1 = (f32[27,8,40,128]{3,2,1,0:T(8,128)S(1)}, f32[3,8,40,128]{3,2,1,0:T(8,128)S(1)}, f32[3,6,40,128]{3,2,1,0:T(8,128)S(1)}, f32[3,4,40,128]{3,2,1,0:T(8...) custom-call(f32[8,40,128]{2,1,0:T(8,128)S(1)} %get-tuple-element.40., ...), custom_call_target="tpu_custom_call" | custom-call | tf_op jit(solution)/shard_map/interior/pallas_call | solution.py:623
  15.6 0.0 collective-permute-done.3.edges
  15.6 0.6 %lower.1 = f32[12,8,128]{2,1,0:T(8,128)S(1)} custom-call(f32[8,40,128]{2,1,0:T(8,128)S(1)} %get-tuple-element.37.kinds, f32[136,128]{1,0:T(8,128)S(1)} %collective-permute-done.3.edges, f32[27,8,40,128]{3,2,1,0:T(8,128)S(1)} %get-tuple-element.41.weights, f32[3,8,40,128]{3,2,1,0:T(8,128)S(1)} %get-tuple-element.42.first, ...), custom_call_target="tpu_custom_call" | custom-call | tf_op jit(solution)/shard_map/lower/pallas_call | solution.py:649
  16.3 0.9 %collective-permute-done.2.edges = f32[136,128]{1,0:T(8,128)S(1)} collective-permute-done((f32[136,128]{1,0:T(8,128)S(1)}, f32[136,128]{1,0:T(8,128)S(1)}, u32[]{:S(2)}, u32[]{:S(2)}) %collective-permute-start.2) | collective-permute-done | bytes 69664 | tf_op jit(solution)/shard_map/ppermute | solution.py:40
  17.2 1.4 %finish.1 = (f32[32,8,128]{2,1,0:T(8,128)S(1)}, f32[11,4,128]{2,1,0:T(4,128)S(1)}, f32[8,128]{1,0:T(8,128)S(1)}) custom-call(f32[8,40,128]{2,1,0:T(8,128)S(1)} %get-tuple-element.37.kinds, f32[136,128]{1,0:T(8,128)S(1)} %collective-permute-done.2.edges, f32[4,128]{1,0:T(4,128)S(1)} %get-tuple-element.39.near, ...), custom_call_target="tpu_custom_call" | custom-call | tf_op jit(solution)/shard_map/finish/pallas_call | solution.py:653
  18.7 17.6 %all_to_all.5.here = f32[16,11,4,128]{3,2,1,0:T(4,128)S(1)} all-to-all(f32[16,11,4,128]{3,2,1,0:T(4,128)S(1)} %broadcast_in_dim.2), channel_id=1, replica_groups=mesh['real'=4,'x'=4,'zh'=2,'y'=4,'core'=2] {'x','y'}, dimensions={0} | all-to-all | bytes 720896 | tf_op jit(solution)/shard_map/all_to_all | solution.py:663
  36.3 0.3 collect.1
  36.6 4.7 %collective-permute-start.4 = (f32[2,32,256]{2,1,0:T(8,128)S(1)}, f32[2,32,256]{2,1,0:T(8,128)S(1)}, u32[]{:S(2)}, u32[]{:S(2)}) collective-permute-start(f32[2,32,256]{2,1,0:T(8,128)S(1)} %get-tuple-element.54), channel_id=1, source_target_pairs={{0,1},{1,0},{2,3},{3,2},{4,5},{5,4},{6,7},{7,6},{8,9},{9,8},{10,11... | collective-permute-start | bytes 196616 | tf_op jit(solution)/shard_map/ppermute | solution.py:40
  41.3 0.9 %collective-permute-done.4.near = f32[2,32,256]{2,1,0:T(8,128)S(1)} collective-permute-done((f32[2,32,256]{2,1,0:T(8,128)S(1)}, f32[2,32,256]{2,1,0:T(8,128)S(1)}, u32[]{:S(2)}, u32[]{:S(2)}) %collective-permute-start.4) | collective-permute-done | bytes 65568 | tf_op jit(solution)/shard_map/ppermute | solution.py:40
  42.2 1.9 %collective-permute-start.5 = (f32[32,256]{1,0:T(8,128)S(1)}, f32[32,256]{1,0:T(8,128)S(1)}, u32[]{:S(2)}, u32[]{:S(2)}) collective-permute-start(f32[32,256]{1,0:T(8,128)S(1)} %fusion), channel_id=1, source_target_pairs={{0,8},{8,0},{1,9},{9,1},{2,10},{10,2},{3,11},{11,3},{4,12},{12,4},... | collective-permute-start | bytes 98312 | tf_op jit(solution)/shard_map/ppermute | solution.py:40
  44.1 4.9 %collective-permute-done.5.far = f32[32,256]{1,0:T(8,128)S(1)} collective-permute-done((f32[32,256]{1,0:T(8,128)S(1)}, f32[32,256]{1,0:T(8,128)S(1)}, u32[]{:S(2)}, u32[]{:S(2)}) %collective-permute-start.5) | collective-permute-done | bytes 32800 | tf_op jit(solution)/shard_map/ppermute | solution.py:40
  48.9 1.5 %update.1 = (f32[32,8,128]{2,1,0:T(8,128)}, f32[2,2,256]{2,1,0:T(2,128)}) custom-call(f32[2,32,256]{2,1,0:T(8,128)S(1)} %get-tuple-element.53.keep, f32[2,32,256]{2,1,0:T(8,128)S(1)} %collective-permute-done.4.near, f32[32,256]{1,0:T(8,128)S(1)} %collective-permute-done.5.far, f32[32,8,128]{2,1,0:T(8,128)S(1)} %get-tuple-element.55.smooth, ...), custom_call_target="tpu_custom_call" | custom-call | tf_op jit(solution)/shard_map/update/pallas_call | solution.py:671
  (2 shorter events, 0.1 us)
Async XLA Ops:
  1.6 4.6 %collective-permute-start = (f32[9,4,128]{2,1,0:T(4,128)S(1)}, f32[9,4,128]{2,1,0:T(4,128)S(1)}, u32[]{:S(2)}, u32[]{:S(2)}) collective-permute-start(f32[9,4,128]{2,1,0:T(4,128)S(1)} %get-tuple-element.31), channel_id=1, source_target_pairs={{0,16},{1,2},{2,1},{3,4},{4,3},{5,6},{6,5},{7,23},{16,0},{17,18},{... | collective-permute-start | bytes 55304 | tf_op jit(solution)/shard_map/ppermute | solution.py:40
  4.4 1.8 %collective-permute-start.1 = (f32[9,4,128]{2,1,0:T(4,128)S(1)}, f32[9,4,128]{2,1,0:T(4,128)S(1)}, u32[]{:S(2)}, u32[]{:S(2)}) collective-permute-start(f32[9,4,128]{2,1,0:T(4,128)S(1)} %get-tuple-element.32), channel_id=1, source_target_pairs={{0,1},{1,0},{2,3},{3,2},{4,5},{5,4},{6,7},{7,6},{8,9},{9,8},{10,11... | collective-permute-start | bytes 55304 | tf_op jit(solution)/shard_map/ppermute | solution.py:40
  6.5 9.1 %collective-permute-start.3 = (f32[136,128]{1,0:T(8,128)S(1)}, f32[136,128]{1,0:T(8,128)S(1)}, u32[]{:S(2)}, u32[]{:S(2)}) collective-permute-start(f32[136,128]{1,0:T(8,128)S(1)} %get-tuple-element.46), channel_id=1, source_target_pairs={{0,1},{1,0},{8,16},{9,17},{16,8},{17,9},{24,32},{25,33},{32,24},{3... | collective-permute-start | bytes 208904 | tf_op jit(solution)/shard_map/ppermute | solution.py:40
  9.1 8.1 %collective-permute-start.2 = (f32[136,128]{1,0:T(8,128)S(1)}, f32[136,128]{1,0:T(8,128)S(1)}, u32[]{:S(2)}, u32[]{:S(2)}) collective-permute-start(f32[136,128]{1,0:T(8,128)S(1)} %get-tuple-element.38), channel_id=1, source_target_pairs={{0,8},{8,0},{16,24},{24,16},{32,40},{40,32},{48,56},{56,48},{1,9},... | collective-permute-start | bytes 208904 | tf_op jit(solution)/shard_map/ppermute | solution.py:40
  36.6 5.6 %collective-permute-start.4 = (f32[2,32,256]{2,1,0:T(8,128)S(1)}, f32[2,32,256]{2,1,0:T(8,128)S(1)}, u32[]{:S(2)}, u32[]{:S(2)}) collective-permute-start(f32[2,32,256]{2,1,0:T(8,128)S(1)} %get-tuple-element.54), channel_id=1, source_target_pairs={{0,1},{1,0},{2,3},{3,2},{4,5},{5,4},{6,7},{7,6},{8,9},{9,8},{10,11... | collective-permute-start | bytes 196616 | tf_op jit(solution)/shard_map/ppermute | solution.py:40
  42.2 6.8 %collective-permute-start.5 = (f32[32,256]{1,0:T(8,128)S(1)}, f32[32,256]{1,0:T(8,128)S(1)}, u32[]{:S(2)}, u32[]{:S(2)}) collective-permute-start(f32[32,256]{1,0:T(8,128)S(1)} %fusion), channel_id=1, source_target_pairs={{0,8},{8,0},{1,9},{9,1},{2,10},{10,2},{3,11},{11,3},{4,12},{12,4},... | collective-permute-start | bytes 98312 | tf_op jit(solution)/shard_map/ppermute | solution.py:40

commit v9 on v8

--- a/solution.py
+++ b/solution.py
@@ -509,21 +509,23 @@
         gather(hit, jnp.concatenate([column(2 * r), column(2 * r + 1)], axis=1)) for r in range(2)
     ]
     found = gather(choose, column(4))
-    row = lax.broadcasted_iota(jnp.int32, (8, SAMPLES), 0)
+    row = lax.broadcasted_iota(jnp.int32, (8, W), 0)
     for member in range(4):
         out = (send if member & 1 else keep).at[member // 2]
-        drill, gain = [
-            jnp.concatenate(
-                [found[64 * kind + 32 * h + 8 * member : 64 * kind + 32 * h + 8 * member + 8] for h in range(2)],
-                axis=1,
-            )
-            for kind in range(2)
-        ]
-        for r in range(2):
-            out[8 * r : 8 * r + 8, :] = drill - totals[r][16 * member : 16 * member + 8]
-        out[16:24, :] = gain
-        own = [totals[r][16 * member + 8 : 16 * member + 16] for r in range(2)]
-        out[24:32, :] = jnp.where(row < 2, own[0], own[1])
+        own = []
+        for h in range(2):
+            lanes = slice(h * W, h * W + W)
+            drill, gain = [
+                found[64 * kind + 32 * h + 8 * member : 64 * kind + 32 * h + 8 * member + 8]
+                for kind in range(2)
+            ]
+            for r in range(2):
+                out[16 * r + 8 * h : 16 * r + 8 * h + 8, :] = drill - totals[r][16 * member : 16 * member + 8, lanes]
+                own.append(totals[r][16 * member + 8 : 16 * member + 16, lanes])
+            out[32 + 8 * h : 40 + 8 * h, :] = gain
+        out[48:56, :] = jnp.where(
+            row < 4, jnp.where(row < 2, own[0], own[1]), jnp.where(row < 6, own[2], own[3])
+        )
 
 
 def update_kernel(
@@ -536,9 +538,19 @@
     sums = keep[0] + near[0] + far[...]
     for k in range(2):
         for r in range(2):
-            t = 24 + 2 * r + k
-            misfit[k, r : r + 1, :] = rows[0, k : k + 1, :] - sums[t : t + 1, :]
-    picked = [jnp.where(live[...] > 0.0, sums[16:24] * sums[8 * r : 8 * r + 8], 0.0) for r in range(2)]
+            for h in range(2):
+                t = 48 + 4 * h + 2 * r + k
+                lanes = slice(h * W, h * W + W)
+                misfit[k, r : r + 1, lanes] = rows[0, k : k + 1, lanes] - sums[t : t + 1, :]
+    gain = jnp.concatenate([sums[32:40], sums[40:48]], axis=1)
+    picked = [
+        jnp.where(
+            live[...] > 0.0,
+            gain * jnp.concatenate([sums[16 * r : 16 * r + 8], sums[16 * r + 8 : 16 * r + 16]], axis=1),
+            0.0,
+        )
+        for r in range(2)
+    ]
     pieces = [split(v) for v in picked]
     left = jnp.concatenate([pieces[0][0], pieces[1][0], pieces[0][1], pieces[1][1]], axis=0)
     block = lax.broadcasted_iota(jnp.int32, (BLOCKS, NODES), 0)
@@ -664,7 +676,7 @@
         jnp.broadcast_to(payload[None], (16, GROUPS, 4, W)), ("x", "y"), 0, 0, tiled=True
     )
     keep, send = call(
-        collect_kernel, (shape(2, 32, SAMPLES), shape(2, 32, SAMPLES)), [VMEM] * 2, "collect"
+        collect_kernel, (shape(2, 56, W), shape(2, 56, W)), [VMEM] * 2, "collect"
     )(lists, here)
     near = permute(send, ("core",), lambda c: (c ^ 1,))
     far = permute(keep[1] + near[1], ("zh",), lambda z: (z ^ 1,))

time: 50.7 us -> 50.5 us (level)
  no operation moved by 1% of the time
where the time goes in v9:
time: 50.5 us; the launch traced here: 50.3 us
  blocking collectives  17.6 us (35%)
  starting transfers between devices  16.9 us (33%)
  Pallas kernels  8.48 us (17%)
  waiting for transfers between devices  6.59 us (13%)
  between operations  0.72 us (1%)
    all_to_all x1, blocking collectives, shards(): lax.all_to_all(jnp.broadcast_to(payload[None], (16, GROUPS, 4, W)), ('x',...  17.6 us
    ppermute x6, starting transfers between devices, permute(): return lax.ppermute(value, axes if len(axes) > 1 else axes[0], pairs)  16.9 us
    ppermute x6, waiting for transfers between devices, permute(): return lax.ppermute(value, axes if len(axes) > 1 else axes[0], pairs)  6.59 us
    pallas_call x1, Pallas kernels, shards(): call(interior_kernel, (shape(27, X, YP, W), shape(3, X, YP, W), shape(3,...  2.27 us
    pallas_call x1, Pallas kernels, shards(): call(update_kernel, (shape(32, 8, W), shape(2, 2, SAMPLES)), [VMEM] * 8,...  1.45 us
    pallas_call x1, Pallas kernels, shards(): call(finish_kernel, (shape(32, 8, W), shape(GROUPS, 4, W), shape(8, W)),...  1.43 us
    pallas_call x1, Pallas kernels, shards(): call(prepare_kernel, (shape(X, YP, W), shape(X, YP, W), shape(27, 8, W)),...  1.15 us
  transfers between devices with their start and end apart: 6, of which 3 were waited for; matrix products, arithmetic and copies ran while one was open for 0% of the time, Pallas kernels for 8%

profile of v9, /device:TPU:1, one launch (start us, length us, event | category | flops | bytes accessed | tf_op | source)
XLA Modules:
  0.0 50.3 jit_solution(10609095667609278989)
XLA Ops:
  0.6 1.0 %edge_y.1 = (f32[9,4,128]{2,1,0:T(4,128)S(1)}, f32[9,4,128]{2,1,0:T(4,128)S(1)}, f32[8,128]{1,0:T(8,128)S(1)}) custom-call(f32[8,32,128]{2,1,0:T(8,128)} %noise_far.3, s32[8,32,64]{2,1,0:T(8,128)} %classes_far.3, s32[8]{0:T(128)} %owner.1), custom_call_target="tpu_custom_call" | custom-call | tf_op jit(solution)/shard_map/edge_y/pallas_call | solution.py:600
  1.6 2.8 %collective-permute-start = (f32[9,4,128]{2,1,0:T(4,128)S(1)}, f32[9,4,128]{2,1,0:T(4,128)S(1)}, u32[]{:S(2)}, u32[]{:S(2)}) collective-permute-start(f32[9,4,128]{2,1,0:T(4,128)S(1)} %get-tuple-element.31), channel_id=1, source_target_pairs={{0,16},{1,2},{2,1},{3,4},{4,3},{5,6},{6,5},{7,23},{16,0},{17,18},{... | collective-permute-start | bytes 55304 | tf_op jit(solution)/shard_map/ppermute | solution.py:40
  4.4 0.7 %collective-permute-start.1 = (f32[9,4,128]{2,1,0:T(4,128)S(1)}, f32[9,4,128]{2,1,0:T(4,128)S(1)}, u32[]{:S(2)}, u32[]{:S(2)}) collective-permute-start(f32[9,4,128]{2,1,0:T(4,128)S(1)} %get-tuple-element.32), channel_id=1, source_target_pairs={{0,1},{1,0},{2,3},{3,2},{4,5},{5,4},{6,7},{7,6},{8,9},{9,8},{10,11... | collective-permute-start | bytes 55304 | tf_op jit(solution)/shard_map/ppermute | solution.py:40
  5.0 1.2 %prepare.1 = (f32[8,40,128]{2,1,0:T(8,128)S(1)}, f32[8,40,128]{2,1,0:T(8,128)S(1)}, f32[27,8,128]{2,1,0:T(8,128)S(1)}) custom-call(f32[8,32,128]{2,1,0:T(8,128)} %noise_far.3, s32[8,32,64]{2,1,0:T(8,128)} %classes_far.3, f32[8,27]{1,0:T(8,128)} %table.1), custom_call_target="tpu_custom_call" | custom-call | tf_op jit(solution)/shard_map/prepare/pallas_call | solution.py:614
  6.2 0.0 collective-permute-done.odd_in
  6.2 0.0 collective-permute-done.1.even_in
  6.2 0.3 edge_x.1
  6.5 2.6 %collective-permute-start.3 = (f32[136,128]{1,0:T(8,128)S(1)}, f32[136,128]{1,0:T(8,128)S(1)}, u32[]{:S(2)}, u32[]{:S(2)}) collective-permute-start(f32[136,128]{1,0:T(8,128)S(1)} %get-tuple-element.46), channel_id=1, source_target_pairs={{0,1},{1,0},{8,16},{9,17},{16,8},{17,9},{24,32},{25,33},{32,24},{3... | collective-permute-start | bytes 208904 | tf_op jit(solution)/shard_map/ppermute | solution.py:40
  9.1 4.3 %collective-permute-start.2 = (f32[136,128]{1,0:T(8,128)S(1)}, f32[136,128]{1,0:T(8,128)S(1)}, u32[]{:S(2)}, u32[]{:S(2)}) collective-permute-start(f32[136,128]{1,0:T(8,128)S(1)} %get-tuple-element.38), channel_id=1, source_target_pairs={{0,8},{8,0},{16,24},{24,16},{32,40},{40,32},{48,56},{56,48},{1,9},... | collective-permute-start | bytes 208904 | tf_op jit(solution)/shard_map/ppermute | solution.py:40
  13.3 2.3 %interior.1 = (f32[27,8,40,128]{3,2,1,0:T(8,128)S(1)}, f32[3,8,40,128]{3,2,1,0:T(8,128)S(1)}, f32[3,6,40,128]{3,2,1,0:T(8,128)S(1)}, f32[3,4,40,128]{3,2,1,0:T(8...) custom-call(f32[8,40,128]{2,1,0:T(8,128)S(1)} %get-tuple-element.40., ...), custom_call_target="tpu_custom_call" | custom-call | tf_op jit(solution)/shard_map/interior/pallas_call | solution.py:635
  15.6 0.0 collective-permute-done.3.edges
  15.6 0.6 %lower.1 = f32[12,8,128]{2,1,0:T(8,128)S(1)} custom-call(f32[8,40,128]{2,1,0:T(8,128)S(1)} %get-tuple-element.37.kinds, f32[136,128]{1,0:T(8,128)S(1)} %collective-permute-done.3.edges, f32[27,8,40,128]{3,2,1,0:T(8,128)S(1)} %get-tuple-element.41.weights, f32[3,8,40,128]{3,2,1,0:T(8,128)S(1)} %get-tuple-element.42.first, ...), custom_call_target="tpu_custom_call" | custom-call | tf_op jit(solution)/shard_map/lower/pallas_call | solution.py:661
  16.3 0.9 %collective-permute-done.2.edges = f32[136,128]{1,0:T(8,128)S(1)} collective-permute-done((f32[136,128]{1,0:T(8,128)S(1)}, f32[136,128]{1,0:T(8,128)S(1)}, u32[]{:S(2)}, u32[]{:S(2)}) %collective-permute-start.2) | collective-permute-done | bytes 69664 | tf_op jit(solution)/shard_map/ppermute | solution.py:40
  17.2 1.4 %finish.1 = (f32[32,8,128]{2,1,0:T(8,128)S(1)}, f32[11,4,128]{2,1,0:T(4,128)S(1)}, f32[8,128]{1,0:T(8,128)S(1)}) custom-call(f32[8,40,128]{2,1,0:T(8,128)S(1)} %get-tuple-element.37.kinds, f32[136,128]{1,0:T(8,128)S(1)} %collective-permute-done.2.edges, f32[4,128]{1,0:T(4,128)S(1)} %get-tuple-element.39.near, ...), custom_call_target="tpu_custom_call" | custom-call | tf_op jit(solution)/shard_map/finish/pallas_call | solution.py:665
  18.7 17.6 %all_to_all.5.here = f32[16,11,4,128]{3,2,1,0:T(4,128)S(1)} all-to-all(f32[16,11,4,128]{3,2,1,0:T(4,128)S(1)} %broadcast_in_dim.2), channel_id=1, replica_groups=mesh['real'=4,'x'=4,'zh'=2,'y'=4,'core'=2] {'x','y'}, dimensions={0} | all-to-all | bytes 720896 | tf_op jit(solution)/shard_map/all_to_all | solution.py:675
  36.3 0.3 collect.1
  36.6 4.7 %collective-permute-start.4 = (f32[2,56,128]{2,1,0:T(8,128)S(1)}, f32[2,56,128]{2,1,0:T(8,128)S(1)}, u32[]{:S(2)}, u32[]{:S(2)}) collective-permute-start(f32[2,56,128]{2,1,0:T(8,128)S(1)} %get-tuple-element.54), channel_id=1, source_target_pairs={{0,1},{1,0},{2,3},{3,2},{4,5},{5,4},{6,7},{7,6},{8,9},{9,8},{10,11... | collective-permute-start | bytes 172040 | tf_op jit(solution)/shard_map/ppermute | solution.py:40
  41.3 0.9 %collective-permute-done.4.near = f32[2,56,128]{2,1,0:T(8,128)S(1)} collective-permute-done((f32[2,56,128]{2,1,0:T(8,128)S(1)}, f32[2,56,128]{2,1,0:T(8,128)S(1)}, u32[]{:S(2)}, u32[]{:S(2)}) %collective-permute-start.4) | collective-permute-done | bytes 57376 | tf_op jit(solution)/shard_map/ppermute | solution.py:40
  42.2 1.9 %collective-permute-start.5 = (f32[56,128]{1,0:T(8,128)S(1)}, f32[56,128]{1,0:T(8,128)S(1)}, u32[]{:S(2)}, u32[]{:S(2)}) collective-permute-start(f32[56,128]{1,0:T(8,128)S(1)} %fusion), channel_id=1, source_target_pairs={{0,8},{8,0},{1,9},{9,1},{2,10},{10,2},{3,11},{11,3},{4,12},{12,4},... | collective-permute-start | bytes 86024 | tf_op jit(solution)/shard_map/ppermute | solution.py:40
  44.1 4.8 %collective-permute-done.5.far = f32[56,128]{1,0:T(8,128)S(1)} collective-permute-done((f32[56,128]{1,0:T(8,128)S(1)}, f32[56,128]{1,0:T(8,128)S(1)}, u32[]{:S(2)}, u32[]{:S(2)}) %collective-permute-start.5) | collective-permute-done | bytes 28704 | tf_op jit(solution)/shard_map/ppermute | solution.py:40
  48.8 1.5 %update.1 = (f32[32,8,128]{2,1,0:T(8,128)}, f32[2,2,256]{2,1,0:T(2,128)}) custom-call(f32[2,56,128]{2,1,0:T(8,128)S(1)} %get-tuple-element.53.keep, f32[2,56,128]{2,1,0:T(8,128)S(1)} %collective-permute-done.4.near, f32[56,128]{1,0:T(8,128)S(1)} %collective-permute-done.5.far, f32[32,8,128]{2,1,0:T(8,128)S(1)} %get-tuple-element.55.smooth, ...), custom_call_target="tpu_custom_call" | custom-call | tf_op jit(solution)/shard_map/update/pallas_call | solution.py:683
  (2 shorter events, 0.1 us)
Async XLA Ops:
  1.6 4.6 %collective-permute-start = (f32[9,4,128]{2,1,0:T(4,128)S(1)}, f32[9,4,128]{2,1,0:T(4,128)S(1)}, u32[]{:S(2)}, u32[]{:S(2)}) collective-permute-start(f32[9,4,128]{2,1,0:T(4,128)S(1)} %get-tuple-element.31), channel_id=1, source_target_pairs={{0,16},{1,2},{2,1},{3,4},{4,3},{5,6},{6,5},{7,23},{16,0},{17,18},{... | collective-permute-start | bytes 55304 | tf_op jit(solution)/shard_map/ppermute | solution.py:40
  4.4 1.8 %collective-permute-start.1 = (f32[9,4,128]{2,1,0:T(4,128)S(1)}, f32[9,4,128]{2,1,0:T(4,128)S(1)}, u32[]{:S(2)}, u32[]{:S(2)}) collective-permute-start(f32[9,4,128]{2,1,0:T(4,128)S(1)} %get-tuple-element.32), channel_id=1, source_target_pairs={{0,1},{1,0},{2,3},{3,2},{4,5},{5,4},{6,7},{7,6},{8,9},{9,8},{10,11... | collective-permute-start | bytes 55304 | tf_op jit(solution)/shard_map/ppermute | solution.py:40
  6.5 9.1 %collective-permute-start.3 = (f32[136,128]{1,0:T(8,128)S(1)}, f32[136,128]{1,0:T(8,128)S(1)}, u32[]{:S(2)}, u32[]{:S(2)}) collective-permute-start(f32[136,128]{1,0:T(8,128)S(1)} %get-tuple-element.46), channel_id=1, source_target_pairs={{0,1},{1,0},{8,16},{9,17},{16,8},{17,9},{24,32},{25,33},{32,24},{3... | collective-permute-start | bytes 208904 | tf_op jit(solution)/shard_map/ppermute | solution.py:40
  9.1 8.1 %collective-permute-start.2 = (f32[136,128]{1,0:T(8,128)S(1)}, f32[136,128]{1,0:T(8,128)S(1)}, u32[]{:S(2)}, u32[]{:S(2)}) collective-permute-start(f32[136,128]{1,0:T(8,128)S(1)} %get-tuple-element.38), channel_id=1, source_target_pairs={{0,8},{8,0},{16,24},{24,16},{32,40},{40,32},{48,56},{56,48},{1,9},... | collective-permute-start | bytes 208904 | tf_op jit(solution)/shard_map/ppermute | solution.py:40
  36.6 5.6 %collective-permute-start.4 = (f32[2,56,128]{2,1,0:T(8,128)S(1)}, f32[2,56,128]{2,1,0:T(8,128)S(1)}, u32[]{:S(2)}, u32[]{:S(2)}) collective-permute-start(f32[2,56,128]{2,1,0:T(8,128)S(1)} %get-tuple-element.54), channel_id=1, source_target_pairs={{0,1},{1,0},{2,3},{3,2},{4,5},{5,4},{6,7},{7,6},{8,9},{9,8},{10,11... | collective-permute-start | bytes 172040 | tf_op jit(solution)/shard_map/ppermute | solution.py:40
  42.2 6.7 %collective-permute-start.5 = (f32[56,128]{1,0:T(8,128)S(1)}, f32[56,128]{1,0:T(8,128)S(1)}, u32[]{:S(2)}, u32[]{:S(2)}) collective-permute-start(f32[56,128]{1,0:T(8,128)S(1)} %fusion), channel_id=1, source_target_pairs={{0,8},{8,0},{1,9},{9,1},{2,10},{10,2},{3,11},{11,3},{4,12},{12,4},... | collective-permute-start | bytes 86024 | tf_op jit(solution)/shard_map/ppermute | solution.py:40

commit v10 on v9

--- a/solution.py
+++ b/solution.py
@@ -16,7 +16,7 @@
 SAMPLES = 256
 NODES = 512
 GROUPS = 11
-MESSAGE = 136
+MESSAGE = 128
 F32 = jnp.float32
 VMEM = pl.BlockSpec(memory_space=pltpu.VMEM)
 HBM = pl.BlockSpec(memory_space=pltpu.HBM)
@@ -186,25 +186,37 @@
         sides(even_in, odd_in)
 
     for out, row, step in ((odd, 0, 1), (even, X - 1, -1)):
-        def put(o, part, value):
-            weights[o, part, :] = value
-
-        weigh(kinds[row + step], tables, put)
+        for n in range(2):
+            def put(o, part, value, n=n):
+                weights[n, o, part, :] = value
+
+            weigh(kinds[row + n * step], tables, put)
         for n in range(3):
             for c, value in enumerate(lean(field[row + n * step])):
                 moved[c, n] = value
         second = operate(
-            lambda o: weights[o],
+            lambda o: weights[1, o],
             lambda a, c: moved[c, a if step == 1 else 2 - a],
             jnp.minimum(kinds[row + step], 1.0),
         )
+        for c, value in enumerate(lean(second)):
+            moved[c, 3] = value
+        kind = kinds[row]
+        inside = jnp.minimum(kind, 1.0)
+        known = operate(
+            lambda o: weights[0, o],
+            lambda a, c: moved[c, (a - 1) * step],
+            inside,
+            (1, 2) if step == 1 else (0, 1),
+        )
+        onward = operate(
+            lambda o: weights[0, o], lambda a, c: moved[c, 3], inside, (2,) if step == 1 else (0,)
+        )
         out[0:38, :] = field[row][1:39]
-        out[38:76, :] = field[row + step][1:39]
-        out[76:112, :] = second[2:38]
-        kind = kinds[row]
-        out[112:130, :] = pack(kind[2:20], kind[20:38])
-        out[130:132, :] = lists[0:2]
-        out[132:MESSAGE, :] = jnp.zeros((MESSAGE - 132, W), F32)
+        out[38:74, :] = known[2:38]
+        out[74:108, :] = (2.0 * onward - field[row])[3:37]
+        out[108:126, :] = pack(kind[2:20], kind[20:38])
+        out[126:128, :] = lists[0:2]
 
 
 def mirrored(x, half):
@@ -251,11 +263,11 @@
     return below, row, above
 
 
-def operate(weight, moved, inside):
+def operate(weight, moved, inside, rows=(0, 1, 2)):
     sums = []
     for b in range(3):
         total = None
-        for a in range(3):
+        for a in rows:
             for c in range(3):
                 term = weight(9 * a + 3 * b + c) * moved(a, c)
                 total = term if total is None else total + term
@@ -334,25 +346,24 @@
     live[...] = (sample < limit).astype(F32)
 
 
-def fill_halo(message, inside, tables, halo_kinds, halo_weights, halo_first, edge_second):
+def fill_halo(message, inside, tables, halo_kinds, halo_weights, halo_first, partial):
     held = jnp.where(inside, message[...], 0.0)
-    one, two = [jnp.zeros((n, W), F32) for n in (1, 2)]
-    low, high = unpack(held[112:130])
+    one, two, three = [jnp.zeros((n, W), F32) for n in (1, 2, 3)]
+    low, high = unpack(held[108:126])
     halo_kinds[...] = jnp.concatenate([two, low, high, two], axis=0)
 
     def put(o, part, value):
         halo_weights[o, part, :] = value
 
     weigh(halo_kinds[...], tables, put)
-    for i in range(2):
-        for c, value in enumerate(lean(jnp.concatenate([one, held[38 * i : 38 * i + 38], one], axis=0))):
-            halo_first[c, i] = value
-    for c, value in enumerate(lean(jnp.concatenate([two, held[76:112], two], axis=0))):
-        edge_second[c, 2] = value
+    for c, value in enumerate(lean(jnp.concatenate([one, held[0:38], one], axis=0))):
+        halo_first[c, 0] = value
+    partial[0] = jnp.concatenate([two, held[38:74], two], axis=0)
+    partial[1] = jnp.concatenate([three, held[74:108], three], axis=0)
 
 
 def side(
-    high, kinds, weights, first, second, third, halo_kinds, halo_weights, halo_first, edge_second, edge_third, put
+    high, kinds, weights, first, second, third, halo_kinds, halo_weights, halo_first, edge_second, edge_third, partial, put
 ):
     def beyond(x):
         return x - X if high else -1 - x
@@ -371,18 +382,26 @@
     def at_third(x, c):
         return third[c, x - 2] if 2 <= x < 6 else edge_third[c, beyond(x) + 2]
 
-    def step(at, x):
+    def step(at, x, rows=(0, 1, 2)):
         of, inside = weight(x)
-        return operate(of, lambda a, c: at(x + a - 1, c), inside)
+        return operate(of, lambda a, c: at(x + a - 1, c), inside, rows)
 
     def row(n):
         return X - 1 - n if high else n
 
+    inward, itself = ((0,), (0, 1)) if high else ((2,), (1, 2))
     for n in (-1, 0):
-        for c, value in enumerate(lean(step(at_first, row(n)))):
+        if n < 0:
+            value = partial[0] + step(at_first, row(n), inward)
+        else:
+            value = step(at_first, row(n))
+        for c, value in enumerate(lean(value)):
             edge_second[c, -n] = value
     for n in (-1, 0, 1):
-        value = 2.0 * step(at_second, row(n)) - at_first(row(n), 1)
+        if n < 0:
+            value = partial[1] + 2.0 * step(at_second, row(n), itself)
+        else:
+            value = 2.0 * step(at_second, row(n)) - at_first(row(n), 1)
         for c, value in enumerate(lean(value)):
             edge_third[c, 1 - n] = value
     for n in (0, 1, 2):
@@ -398,38 +417,38 @@
 def lower_kernel(
     kinds, edges, weights, first, second, third, tables,
     lower,
-    halo_kinds, halo_weights, halo_first, edge_second, edge_third,
-):
-    fill_halo(edges, has_odd_pair("x", "zh"), tables, halo_kinds, halo_weights, halo_first, edge_second)
+    halo_kinds, halo_weights, halo_first, edge_second, edge_third, partial,
+):
+    fill_halo(edges, has_odd_pair("x", "zh"), tables, halo_kinds, halo_weights, halo_first, partial)
 
     def put(x, g, value):
         lower[4 * x + g] = value
 
     side(
         False, kinds, weights, first, second, third,
-        halo_kinds, halo_weights, halo_first, edge_second, edge_third, put,
+        halo_kinds, halo_weights, halo_first, edge_second, edge_third, partial, put,
     )
 
 
 def finish_kernel(
     kinds, edges, near, weights, first, second, third, middle, lower, tables, turned, other, live, blocks,
     smooth, payload, lists,
-    halo_kinds, halo_weights, halo_first, edge_second, edge_third, chosen, node_block, sem,
+    halo_kinds, halo_weights, halo_first, edge_second, edge_third, partial, chosen, node_block, sem,
 ):
     copy = pltpu.make_async_copy(blocks.at[0:1], node_block, sem)
     copy.start()
     half = whereabouts()[0]
     lists[0:4] = near[0:4]
     lists[4:8] = jnp.zeros((4, W), F32)
-    lists[2:4] = edges[130:132]
-    fill_halo(edges, True, tables, halo_kinds, halo_weights, halo_first, edge_second)
+    lists[2:4] = edges[126:128]
+    fill_halo(edges, True, tables, halo_kinds, halo_weights, halo_first, partial)
 
     def put(x, g, value):
         smooth[4 * mirrored(x, half) + g] = value
 
     side(
         True, kinds, weights, first, second, third,
-        halo_kinds, halo_weights, halo_first, edge_second, edge_third, put,
+        halo_kinds, halo_weights, halo_first, edge_second, edge_third, partial, put,
     )
     for g in range(4):
         for x in (0, 1, 2):
@@ -628,7 +647,7 @@
         (shape(X, YP, W), shape(X, YP, W), shape(MESSAGE, W), shape(MESSAGE, W), shape(4, W)),
         [VMEM] * 6,
         "edge_x",
-        [pltpu.VMEM((27, YP, W), F32), pltpu.VMEM((3, 3, YP, W), F32)],
+        [pltpu.VMEM((2, 27, YP, W), F32), pltpu.VMEM((3, 4, YP, W), F32)],
     )(odd, even, field, kinds, names, tables)
     odd = permute(odd, ("x", "zh", "core"), odd_along_x)
     even = permute(even, ("x", "zh"), even_pair)
@@ -654,9 +673,10 @@
     halo_scratch = [
         pltpu.VMEM((YP, W), F32),
         pltpu.VMEM((27, YP, W), F32),
+        pltpu.VMEM((3, 1, YP, W), F32),
         pltpu.VMEM((3, 2, YP, W), F32),
         pltpu.VMEM((3, 3, YP, W), F32),
-        pltpu.VMEM((3, 3, YP, W), F32),
+        pltpu.VMEM((2, YP, W), F32),
     ]
     (lower,) = call(lower_kernel, (shape(12, 8, W),), [VMEM] * 7, "lower", halo_scratch)(
         kinds, odd, weights, first, second, third, tables

time: 50.5 us -> 50.6 us (level)
  starting transfers between devices: 16.9 us -> 15.9 us
  waiting for transfers between devices: 6.59 us -> 7.37 us
    ppermute x6, starting transfers between devices: 16.9 us -> 15.9 us  [permute(): return lax.ppermute(value, axes if len(axes) > 1 else axes[0], pairs)]
    ppermute x6, waiting for transfers between devices: 6.59 us -> 7.37 us  [permute(): return lax.ppermute(value, axes if len(axes) > 1 else axes[0], pairs)]
where the time goes in v10:
time: 50.6 us; the launch traced here: 50.3 us
  blocking collectives  17.6 us (35%)
  starting transfers between devices  15.9 us (31%)
  Pallas kernels  8.59 us (17%)
  waiting for transfers between devices  7.37 us (15%)
  between operations  0.72 us (1%)
    all_to_all x1, blocking collectives, shards(): lax.all_to_all(jnp.broadcast_to(payload[None], (16, GROUPS, 4, W)), ('x',...  17.6 us
    ppermute x6, starting transfers between devices, permute(): return lax.ppermute(value, axes if len(axes) > 1 else axes[0], pairs)  15.9 us
    ppermute x6, waiting for transfers between devices, permute(): return lax.ppermute(value, axes if len(axes) > 1 else axes[0], pairs)  7.37 us
    pallas_call x1, Pallas kernels, shards(): call(interior_kernel, (shape(27, X, YP, W), shape(3, X, YP, W), shape(3,...  2.27 us
    pallas_call x1, Pallas kernels, shards(): call(update_kernel, (shape(32, 8, W), shape(2, 2, SAMPLES)), [VMEM] * 8,...  1.45 us
    pallas_call x1, Pallas kernels, shards(): call(finish_kernel, (shape(32, 8, W), shape(GROUPS, 4, W), shape(8, W)),...  1.42 us
    pallas_call x1, Pallas kernels, shards(): call(prepare_kernel, (shape(X, YP, W), shape(X, YP, W), shape(27, 8, W)),...  1.15 us
  transfers between devices with their start and end apart: 6, of which 3 were waited for; matrix products, arithmetic and copies ran while one was open for 0% of the time, Pallas kernels for 8%

profile of v10, /device:TPU:1, one launch (start us, length us, event | category | flops | bytes accessed | tf_op | source)
XLA Modules:
  0.0 50.3 jit_solution(7553542363382938246)
XLA Ops:
  0.6 1.0 %edge_y.1 = (f32[9,4,128]{2,1,0:T(4,128)S(1)}, f32[9,4,128]{2,1,0:T(4,128)S(1)}, f32[8,128]{1,0:T(8,128)S(1)}) custom-call(f32[8,32,128]{2,1,0:T(8,128)} %noise_far.3, s32[8,32,64]{2,1,0:T(8,128)} %classes_far.3, s32[8]{0:T(128)} %owner.1), custom_call_target="tpu_custom_call" | custom-call | tf_op jit(solution)/shard_map/edge_y/pallas_call | solution.py:619
  1.6 2.8 %collective-permute-start = (f32[9,4,128]{2,1,0:T(4,128)S(1)}, f32[9,4,128]{2,1,0:T(4,128)S(1)}, u32[]{:S(2)}, u32[]{:S(2)}) collective-permute-start(f32[9,4,128]{2,1,0:T(4,128)S(1)} %get-tuple-element.31), channel_id=1, source_target_pairs={{0,16},{1,2},{2,1},{3,4},{4,3},{5,6},{6,5},{7,23},{16,0},{17,18},{... | collective-permute-start | bytes 55304 | tf_op jit(solution)/shard_map/ppermute | solution.py:40
  4.4 0.7 %collective-permute-start.1 = (f32[9,4,128]{2,1,0:T(4,128)S(1)}, f32[9,4,128]{2,1,0:T(4,128)S(1)}, u32[]{:S(2)}, u32[]{:S(2)}) collective-permute-start(f32[9,4,128]{2,1,0:T(4,128)S(1)} %get-tuple-element.32), channel_id=1, source_target_pairs={{0,1},{1,0},{2,3},{3,2},{4,5},{5,4},{6,7},{7,6},{8,9},{9,8},{10,11... | collective-permute-start | bytes 55304 | tf_op jit(solution)/shard_map/ppermute | solution.py:40
  5.0 1.2 %prepare.1 = (f32[8,40,128]{2,1,0:T(8,128)S(1)}, f32[8,40,128]{2,1,0:T(8,128)S(1)}, f32[27,8,128]{2,1,0:T(8,128)S(1)}) custom-call(f32[8,32,128]{2,1,0:T(8,128)} %noise_far.3, s32[8,32,64]{2,1,0:T(8,128)} %classes_far.3, f32[8,27]{1,0:T(8,128)} %table.1), custom_call_target="tpu_custom_call" | custom-call | tf_op jit(solution)/shard_map/prepare/pallas_call | solution.py:633
  6.2 0.0 collective-permute-done.odd_in
  6.2 0.0 collective-permute-done.1.even_in
  6.2 0.5 edge_x.1
  6.7 2.6 %collective-permute-start.3 = (f32[128,128]{1,0:T(8,128)S(1)}, f32[128,128]{1,0:T(8,128)S(1)}, u32[]{:S(2)}, u32[]{:S(2)}) collective-permute-start(f32[128,128]{1,0:T(8,128)S(1)} %get-tuple-element.46), channel_id=1, source_target_pairs={{0,1},{1,0},{8,16},{9,17},{16,8},{17,9},{24,32},{25,33},{32,24},{3... | collective-permute-start | bytes 196616 | tf_op jit(solution)/shard_map/ppermute | solution.py:40
  9.2 4.3 %collective-permute-start.2 = (f32[128,128]{1,0:T(8,128)S(1)}, f32[128,128]{1,0:T(8,128)S(1)}, u32[]{:S(2)}, u32[]{:S(2)}) collective-permute-start(f32[128,128]{1,0:T(8,128)S(1)} %get-tuple-element.38), channel_id=1, source_target_pairs={{0,8},{8,0},{16,24},{24,16},{32,40},{40,32},{48,56},{56,48},{1,9},... | collective-permute-start | bytes 196616 | tf_op jit(solution)/shard_map/ppermute | solution.py:40
  13.5 2.3 %interior.1 = (f32[27,8,40,128]{3,2,1,0:T(8,128)S(1)}, f32[3,8,40,128]{3,2,1,0:T(8,128)S(1)}, f32[3,6,40,128]{3,2,1,0:T(8,128)S(1)}, f32[3,4,40,128]{3,2,1,0:T(8...) custom-call(f32[8,40,128]{2,1,0:T(8,128)S(1)} %get-tuple-element.40., ...), custom_call_target="tpu_custom_call" | custom-call | tf_op jit(solution)/shard_map/interior/pallas_call | solution.py:654
  15.8 0.0 collective-permute-done.3.edges
  15.8 0.6 %lower.1 = f32[12,8,128]{2,1,0:T(8,128)S(1)} custom-call(f32[8,40,128]{2,1,0:T(8,128)S(1)} %get-tuple-element.37.kinds, f32[128,128]{1,0:T(8,128)S(1)} %collective-permute-done.3.edges, f32[27,8,40,128]{3,2,1,0:T(8,128)S(1)} %get-tuple-element.41.weights, f32[3,8,40,128]{3,2,1,0:T(8,128)S(1)} %get-tuple-element.42.first, ...), custom_call_target="tpu_custom_call" | custom-call | tf_op jit(solution)/shard_map/lower/pallas_call | solution.py:681
  16.4 0.9 %collective-permute-done.2.edges = f32[128,128]{1,0:T(8,128)S(1)} collective-permute-done((f32[128,128]{1,0:T(8,128)S(1)}, f32[128,128]{1,0:T(8,128)S(1)}, u32[]{:S(2)}, u32[]{:S(2)}) %collective-permute-start.2) | collective-permute-done | bytes 65568 | tf_op jit(solution)/shard_map/ppermute | solution.py:40
  17.3 1.4 %finish.1 = (f32[32,8,128]{2,1,0:T(8,128)S(1)}, f32[11,4,128]{2,1,0:T(4,128)S(1)}, f32[8,128]{1,0:T(8,128)S(1)}) custom-call(f32[8,40,128]{2,1,0:T(8,128)S(1)} %get-tuple-element.37.kinds, f32[128,128]{1,0:T(8,128)S(1)} %collective-permute-done.2.edges, f32[4,128]{1,0:T(4,128)S(1)} %get-tuple-element.39.near, ...), custom_call_target="tpu_custom_call" | custom-call | tf_op jit(solution)/shard_map/finish/pallas_call | solution.py:685
  18.8 17.6 %all_to_all.5.here = f32[16,11,4,128]{3,2,1,0:T(4,128)S(1)} all-to-all(f32[16,11,4,128]{3,2,1,0:T(4,128)S(1)} %broadcast_in_dim.2), channel_id=1, replica_groups=mesh['real'=4,'x'=4,'zh'=2,'y'=4,'core'=2] {'x','y'}, dimensions={0} | all-to-all | bytes 720896 | tf_op jit(solution)/shard_map/all_to_all | solution.py:695
  36.4 0.3 collect.1
  36.7 4.6 %collective-permute-start.4 = (f32[2,56,128]{2,1,0:T(8,128)S(1)}, f32[2,56,128]{2,1,0:T(8,128)S(1)}, u32[]{:S(2)}, u32[]{:S(2)}) collective-permute-start(f32[2,56,128]{2,1,0:T(8,128)S(1)} %get-tuple-element.54), channel_id=1, source_target_pairs={{0,1},{1,0},{2,3},{3,2},{4,5},{5,4},{6,7},{7,6},{8,9},{9,8},{10,11... | collective-permute-start | bytes 172040 | tf_op jit(solution)/shard_map/ppermute | solution.py:40
  41.3 0.9 %collective-permute-done.4.near = f32[2,56,128]{2,1,0:T(8,128)S(1)} collective-permute-done((f32[2,56,128]{2,1,0:T(8,128)S(1)}, f32[2,56,128]{2,1,0:T(8,128)S(1)}, u32[]{:S(2)}, u32[]{:S(2)}) %collective-permute-start.4) | collective-permute-done | bytes 57376 | tf_op jit(solution)/shard_map/ppermute | solution.py:40
  42.2 1.1 %collective-permute-start.5 = (f32[56,128]{1,0:T(8,128)S(1)}, f32[56,128]{1,0:T(8,128)S(1)}, u32[]{:S(2)}, u32[]{:S(2)}) collective-permute-start(f32[56,128]{1,0:T(8,128)S(1)} %fusion), channel_id=1, source_target_pairs={{0,8},{8,0},{1,9},{9,1},{2,10},{10,2},{3,11},{11,3},{4,12},{12,4},... | collective-permute-start | bytes 86024 | tf_op jit(solution)/shard_map/ppermute | solution.py:40
  43.3 5.6 %collective-permute-done.5.far = f32[56,128]{1,0:T(8,128)S(1)} collective-permute-done((f32[56,128]{1,0:T(8,128)S(1)}, f32[56,128]{1,0:T(8,128)S(1)}, u32[]{:S(2)}, u32[]{:S(2)}) %collective-permute-start.5) | collective-permute-done | bytes 28704 | tf_op jit(solution)/shard_map/ppermute | solution.py:40
  48.9 1.5 %update.1 = (f32[32,8,128]{2,1,0:T(8,128)}, f32[2,2,256]{2,1,0:T(2,128)}) custom-call(f32[2,56,128]{2,1,0:T(8,128)S(1)} %get-tuple-element.53.keep, f32[2,56,128]{2,1,0:T(8,128)S(1)} %collective-permute-done.4.near, f32[56,128]{1,0:T(8,128)S(1)} %collective-permute-done.5.far, f32[32,8,128]{2,1,0:T(8,128)S(1)} %get-tuple-element.55.smooth, ...), custom_call_target="tpu_custom_call" | custom-call | tf_op jit(solution)/shard_map/update/pallas_call | solution.py:703
  (2 shorter events, 0.1 us)
Async XLA Ops:
  1.6 4.6 %collective-permute-start = (f32[9,4,128]{2,1,0:T(4,128)S(1)}, f32[9,4,128]{2,1,0:T(4,128)S(1)}, u32[]{:S(2)}, u32[]{:S(2)}) collective-permute-start(f32[9,4,128]{2,1,0:T(4,128)S(1)} %get-tuple-element.31), channel_id=1, source_target_pairs={{0,16},{1,2},{2,1},{3,4},{4,3},{5,6},{6,5},{7,23},{16,0},{17,18},{... | collective-permute-start | bytes 55304 | tf_op jit(solution)/shard_map/ppermute | solution.py:40
  4.4 1.8 %collective-permute-start.1 = (f32[9,4,128]{2,1,0:T(4,128)S(1)}, f32[9,4,128]{2,1,0:T(4,128)S(1)}, u32[]{:S(2)}, u32[]{:S(2)}) collective-permute-start(f32[9,4,128]{2,1,0:T(4,128)S(1)} %get-tuple-element.32), channel_id=1, source_target_pairs={{0,1},{1,0},{2,3},{3,2},{4,5},{5,4},{6,7},{7,6},{8,9},{9,8},{10,11... | collective-permute-start | bytes 55304 | tf_op jit(solution)/shard_map/ppermute | solution.py:40
  6.7 9.1 %collective-permute-start.3 = (f32[128,128]{1,0:T(8,128)S(1)}, f32[128,128]{1,0:T(8,128)S(1)}, u32[]{:S(2)}, u32[]{:S(2)}) collective-permute-start(f32[128,128]{1,0:T(8,128)S(1)} %get-tuple-element.46), channel_id=1, source_target_pairs={{0,1},{1,0},{8,16},{9,17},{16,8},{17,9},{24,32},{25,33},{32,24},{3... | collective-permute-start | bytes 196616 | tf_op jit(solution)/shard_map/ppermute | solution.py:40
  9.2 8.0 %collective-permute-start.2 = (f32[128,128]{1,0:T(8,128)S(1)}, f32[128,128]{1,0:T(8,128)S(1)}, u32[]{:S(2)}, u32[]{:S(2)}) collective-permute-start(f32[128,128]{1,0:T(8,128)S(1)} %get-tuple-element.38), channel_id=1, source_target_pairs={{0,8},{8,0},{16,24},{24,16},{32,40},{40,32},{48,56},{56,48},{1,9},... | collective-permute-start | bytes 196616 | tf_op jit(solution)/shard_map/ppermute | solution.py:40
  36.7 5.5 %collective-permute-start.4 = (f32[2,56,128]{2,1,0:T(8,128)S(1)}, f32[2,56,128]{2,1,0:T(8,128)S(1)}, u32[]{:S(2)}, u32[]{:S(2)}) collective-permute-start(f32[2,56,128]{2,1,0:T(8,128)S(1)} %get-tuple-element.54), channel_id=1, source_target_pairs={{0,1},{1,0},{2,3},{3,2},{4,5},{5,4},{6,7},{7,6},{8,9},{9,8},{10,11... | collective-permute-start | bytes 172040 | tf_op jit(solution)/shard_map/ppermute | solution.py:40
  42.2 6.7 %collective-permute-start.5 = (f32[56,128]{1,0:T(8,128)S(1)}, f32[56,128]{1,0:T(8,128)S(1)}, u32[]{:S(2)}, u32[]{:S(2)}) collective-permute-start(f32[56,128]{1,0:T(8,128)S(1)} %fusion), channel_id=1, source_target_pairs={{0,8},{8,0},{1,9},{9,1},{2,10},{10,2},{3,11},{11,3},{4,12},{12,4},... | collective-permute-start | bytes 86024 | tf_op jit(solution)/shard_map/ppermute | solution.py:40

commit v11 on v10

--- a/solution.py
+++ b/solution.py
@@ -481,10 +481,11 @@
         told = jnp.where(live[...] > 0.0, sums[r], 0.0)
         tiles += [told[:, 0:W], told[:, W : 2 * W]]
     tiles.append(other[:, 0:W])
-    for n, tile in enumerate(tiles):
-        payload[2 * n] = tile[0:4]
-        payload[2 * n + 1] = tile[4:8]
-    payload[10] = other[0:4, W : 2 * W]
+    for peer in range(16):
+        for n, tile in enumerate(tiles):
+            payload[peer, 2 * n] = tile[0:4]
+            payload[peer, 2 * n + 1] = tile[4:8]
+        payload[peer, 10] = other[0:4, W : 2 * W]
 
 
 def collect_kernel(lists, here, keep, send):
@@ -684,7 +685,7 @@
     index_scratch = [pltpu.SMEM((1, W), jnp.int32), pltpu.SemaphoreType.DMA]
     smooth, payload, lists = call(
         finish_kernel,
-        (shape(32, 8, W), shape(GROUPS, 4, W), shape(8, W)),
+        (shape(32, 8, W), shape(16, GROUPS, 4, W), shape(8, W)),
         [VMEM] * 14,
         "finish",
         halo_scratch + [pltpu.VMEM((64, W), F32)] + index_scratch,
@@ -692,9 +693,7 @@
         kinds, even, lists, weights, first, second, third, middle, lower, tables, turned,
         other, live, blocks,
     )
-    here = lax.all_to_all(
-        jnp.broadcast_to(payload[None], (16, GROUPS, 4, W)), ("x", "y"), 0, 0, tiled=True
-    )
+    here = lax.all_to_all(payload, ("x", "y"), 0, 0, tiled=True)
     keep, send = call(
         collect_kernel, (shape(2, 56, W), shape(2, 56, W)), [VMEM] * 2, "collect"
     )(lists, here)

time: 50.6 us -> 50.5 us (level)
  no operation moved by 1% of the time
where the time goes in v11:
time: 50.5 us; the launch traced here: 50.3 us
  blocking collectives  17.7 us (35%)
  starting transfers between devices  15.9 us (31%)
  Pallas kernels  8.6 us (17%)
  waiting for transfers between devices  7.37 us (15%)
  between operations  0.71 us (1%)
    all_to_all x1, blocking collectives, shards(): here = lax.all_to_all(payload, ('x', 'y'), 0, 0, tiled=True)  17.7 us
    ppermute x6, starting transfers between devices, permute(): return lax.ppermute(value, axes if len(axes) > 1 else axes[0], pairs)  15.9 us
    ppermute x6, waiting for transfers between devices, permute(): return lax.ppermute(value, axes if len(axes) > 1 else axes[0], pairs)  7.37 us
    pallas_call x1, Pallas kernels, shards(): call(interior_kernel, (shape(27, X, YP, W), shape(3, X, YP, W), shape(3,...  2.27 us
    pallas_call x1, Pallas kernels, shards(): call(update_kernel, (shape(32, 8, W), shape(2, 2, SAMPLES)), [VMEM] * 8,...  1.46 us
    pallas_call x1, Pallas kernels, shards(): call(finish_kernel, (shape(32, 8, W), shape(16, GROUPS, 4, W), shape(8, W...  1.43 us
    pallas_call x1, Pallas kernels, shards(): call(prepare_kernel, (shape(X, YP, W), shape(X, YP, W), shape(27, 8, W)),...  1.15 us
  transfers between devices with their start and end apart: 6, of which 3 were waited for; matrix products, arithmetic and copies ran while one was open for 0% of the time, Pallas kernels for 8%

profile of v11, /device:TPU:1, one launch (start us, length us, event | category | flops | bytes accessed | tf_op | source)
XLA Modules:
  0.0 50.3 jit_solution(11605100076971416631)
XLA Ops:
  0.6 1.0 %edge_y.1 = (f32[9,4,128]{2,1,0:T(4,128)S(1)}, f32[9,4,128]{2,1,0:T(4,128)S(1)}, f32[8,128]{1,0:T(8,128)S(1)}) custom-call(f32[8,32,128]{2,1,0:T(8,128)} %noise_far.3, s32[8,32,64]{2,1,0:T(8,128)} %classes_far.3, s32[8]{0:T(128)} %owner.1), custom_call_target="tpu_custom_call" | custom-call | tf_op jit(solution)/shard_map/edge_y/pallas_call | solution.py:620
  1.6 2.8 %collective-permute-start = (f32[9,4,128]{2,1,0:T(4,128)S(1)}, f32[9,4,128]{2,1,0:T(4,128)S(1)}, u32[]{:S(2)}, u32[]{:S(2)}) collective-permute-start(f32[9,4,128]{2,1,0:T(4,128)S(1)} %get-tuple-element.31), channel_id=1, source_target_pairs={{0,16},{1,2},{2,1},{3,4},{4,3},{5,6},{6,5},{7,23},{16,0},{17,18},{... | collective-permute-start | bytes 55304 | tf_op jit(solution)/shard_map/ppermute | solution.py:40
  4.4 0.7 %collective-permute-start.1 = (f32[9,4,128]{2,1,0:T(4,128)S(1)}, f32[9,4,128]{2,1,0:T(4,128)S(1)}, u32[]{:S(2)}, u32[]{:S(2)}) collective-permute-start(f32[9,4,128]{2,1,0:T(4,128)S(1)} %get-tuple-element.32), channel_id=1, source_target_pairs={{0,1},{1,0},{2,3},{3,2},{4,5},{5,4},{6,7},{7,6},{8,9},{9,8},{10,11... | collective-permute-start | bytes 55304 | tf_op jit(solution)/shard_map/ppermute | solution.py:40
  5.0 1.2 %prepare.1 = (f32[8,40,128]{2,1,0:T(8,128)S(1)}, f32[8,40,128]{2,1,0:T(8,128)S(1)}, f32[27,8,128]{2,1,0:T(8,128)S(1)}) custom-call(f32[8,32,128]{2,1,0:T(8,128)} %noise_far.3, s32[8,32,64]{2,1,0:T(8,128)} %classes_far.3, f32[8,27]{1,0:T(8,128)} %table.1), custom_call_target="tpu_custom_call" | custom-call | tf_op jit(solution)/shard_map/prepare/pallas_call | solution.py:634
  6.2 0.0 collective-permute-done.odd_in
  6.2 0.0 collective-permute-done.1.even_in
  6.2 0.5 edge_x.1
  6.7 2.6 %collective-permute-start.3 = (f32[128,128]{1,0:T(8,128)S(1)}, f32[128,128]{1,0:T(8,128)S(1)}, u32[]{:S(2)}, u32[]{:S(2)}) collective-permute-start(f32[128,128]{1,0:T(8,128)S(1)} %get-tuple-element.46), channel_id=1, source_target_pairs={{0,1},{1,0},{8,16},{9,17},{16,8},{17,9},{24,32},{25,33},{32,24},{3... | collective-permute-start | bytes 196616 | tf_op jit(solution)/shard_map/ppermute | solution.py:40
  9.2 4.3 %collective-permute-start.2 = (f32[128,128]{1,0:T(8,128)S(1)}, f32[128,128]{1,0:T(8,128)S(1)}, u32[]{:S(2)}, u32[]{:S(2)}) collective-permute-start(f32[128,128]{1,0:T(8,128)S(1)} %get-tuple-element.38), channel_id=1, source_target_pairs={{0,8},{8,0},{16,24},{24,16},{32,40},{40,32},{48,56},{56,48},{1,9},... | collective-permute-start | bytes 196616 | tf_op jit(solution)/shard_map/ppermute | solution.py:40
  13.5 2.3 %interior.1 = (f32[27,8,40,128]{3,2,1,0:T(8,128)S(1)}, f32[3,8,40,128]{3,2,1,0:T(8,128)S(1)}, f32[3,6,40,128]{3,2,1,0:T(8,128)S(1)}, f32[3,4,40,128]{3,2,1,0:T(8...) custom-call(f32[8,40,128]{2,1,0:T(8,128)S(1)} %get-tuple-element.40., ...), custom_call_target="tpu_custom_call" | custom-call | tf_op jit(solution)/shard_map/interior/pallas_call | solution.py:655
  15.8 0.0 collective-permute-done.3.edges
  15.8 0.6 %lower.1 = f32[12,8,128]{2,1,0:T(8,128)S(1)} custom-call(f32[8,40,128]{2,1,0:T(8,128)S(1)} %get-tuple-element.37.kinds, f32[128,128]{1,0:T(8,128)S(1)} %collective-permute-done.3.edges, f32[27,8,40,128]{3,2,1,0:T(8,128)S(1)} %get-tuple-element.41.weights, f32[3,8,40,128]{3,2,1,0:T(8,128)S(1)} %get-tuple-element.42.first, ...), custom_call_target="tpu_custom_call" | custom-call | tf_op jit(solution)/shard_map/lower/pallas_call | solution.py:682
  16.4 0.9 %collective-permute-done.2.edges = f32[128,128]{1,0:T(8,128)S(1)} collective-permute-done((f32[128,128]{1,0:T(8,128)S(1)}, f32[128,128]{1,0:T(8,128)S(1)}, u32[]{:S(2)}, u32[]{:S(2)}) %collective-permute-start.2) | collective-permute-done | bytes 65568 | tf_op jit(solution)/shard_map/ppermute | solution.py:40
  17.3 1.4 %finish.1 = (f32[32,8,128]{2,1,0:T(8,128)S(1)}, f32[16,11,4,128]{3,2,1,0:T(4,128)S(1)}, f32[8,128]{1,0:T(8,128)S(1)}) custom-call(f32[8,40,128]{2,1,0:T(8,128)S(1)} %get-tuple-element.37.kinds, f32[128,128]{1,0:T(8,128)S(1)} %collective-permute-done.2.edges, f32[4,128]{1,0:T(4,128)S(1)} %get-tuple-element.39.near, ...), custom_call_target="tpu_custom_call" | custom-call | tf_op jit(solution)/shard_map/finish/pallas_call | solution.py:686
  18.7 17.7 %all_to_all.5.here = f32[16,11,4,128]{3,2,1,0:T(4,128)S(1)} all-to-all(f32[16,11,4,128]{3,2,1,0:T(4,128)S(1)} %get-tuple-element.52), channel_id=1, replica_groups=mesh['real'=4,'x'=4,'zh'=2,'y'=4,'core'=2] {'x','y'}, dimensions={0} | all-to-all | bytes 720896 | tf_op jit(solution)/shard_map/all_to_all | solution.py:696
  36.4 0.3 collect.1
  36.6 4.6 %collective-permute-start.4 = (f32[2,56,128]{2,1,0:T(8,128)S(1)}, f32[2,56,128]{2,1,0:T(8,128)S(1)}, u32[]{:S(2)}, u32[]{:S(2)}) collective-permute-start(f32[2,56,128]{2,1,0:T(8,128)S(1)} %get-tuple-element.54), channel_id=1, source_target_pairs={{0,1},{1,0},{2,3},{3,2},{4,5},{5,4},{6,7},{7,6},{8,9},{9,8},{10,11... | collective-permute-start | bytes 172040 | tf_op jit(solution)/shard_map/ppermute | solution.py:40
  41.2 0.9 %collective-permute-done.4.near = f32[2,56,128]{2,1,0:T(8,128)S(1)} collective-permute-done((f32[2,56,128]{2,1,0:T(8,128)S(1)}, f32[2,56,128]{2,1,0:T(8,128)S(1)}, u32[]{:S(2)}, u32[]{:S(2)}) %collective-permute-start.4) | collective-permute-done | bytes 57376 | tf_op jit(solution)/shard_map/ppermute | solution.py:40
  42.1 1.1 %collective-permute-start.5 = (f32[56,128]{1,0:T(8,128)S(1)}, f32[56,128]{1,0:T(8,128)S(1)}, u32[]{:S(2)}, u32[]{:S(2)}) collective-permute-start(f32[56,128]{1,0:T(8,128)S(1)} %fusion), channel_id=1, source_target_pairs={{0,8},{8,0},{1,9},{9,1},{2,10},{10,2},{3,11},{11,3},{4,12},{12,4},... | collective-permute-start | bytes 86024 | tf_op jit(solution)/shard_map/ppermute | solution.py:40
  43.2 5.6 %collective-permute-done.5.far = f32[56,128]{1,0:T(8,128)S(1)} collective-permute-done((f32[56,128]{1,0:T(8,128)S(1)}, f32[56,128]{1,0:T(8,128)S(1)}, u32[]{:S(2)}, u32[]{:S(2)}) %collective-permute-start.5) | collective-permute-done | bytes 28704 | tf_op jit(solution)/shard_map/ppermute | solution.py:40
  48.8 1.5 %update.1 = (f32[32,8,128]{2,1,0:T(8,128)}, f32[2,2,256]{2,1,0:T(2,128)}) custom-call(f32[2,56,128]{2,1,0:T(8,128)S(1)} %get-tuple-element.53.keep, f32[2,56,128]{2,1,0:T(8,128)S(1)} %collective-permute-done.4.near, f32[56,128]{1,0:T(8,128)S(1)} %collective-permute-done.5.far, f32[32,8,128]{2,1,0:T(8,128)S(1)} %get-tuple-element.55.smooth, ...), custom_call_target="tpu_custom_call" | custom-call | tf_op jit(solution)/shard_map/update/pallas_call | solution.py:702
  (1 shorter events, 0.0 us)
Async XLA Ops:
  1.6 4.6 %collective-permute-start = (f32[9,4,128]{2,1,0:T(4,128)S(1)}, f32[9,4,128]{2,1,0:T(4,128)S(1)}, u32[]{:S(2)}, u32[]{:S(2)}) collective-permute-start(f32[9,4,128]{2,1,0:T(4,128)S(1)} %get-tuple-element.31), channel_id=1, source_target_pairs={{0,16},{1,2},{2,1},{3,4},{4,3},{5,6},{6,5},{7,23},{16,0},{17,18},{... | collective-permute-start | bytes 55304 | tf_op jit(solution)/shard_map/ppermute | solution.py:40
  4.4 1.8 %collective-permute-start.1 = (f32[9,4,128]{2,1,0:T(4,128)S(1)}, f32[9,4,128]{2,1,0:T(4,128)S(1)}, u32[]{:S(2)}, u32[]{:S(2)}) collective-permute-start(f32[9,4,128]{2,1,0:T(4,128)S(1)} %get-tuple-element.32), channel_id=1, source_target_pairs={{0,1},{1,0},{2,3},{3,2},{4,5},{5,4},{6,7},{7,6},{8,9},{9,8},{10,11... | collective-permute-start | bytes 55304 | tf_op jit(solution)/shard_map/ppermute | solution.py:40
  6.7 9.1 %collective-permute-start.3 = (f32[128,128]{1,0:T(8,128)S(1)}, f32[128,128]{1,0:T(8,128)S(1)}, u32[]{:S(2)}, u32[]{:S(2)}) collective-permute-start(f32[128,128]{1,0:T(8,128)S(1)} %get-tuple-element.46), channel_id=1, source_target_pairs={{0,1},{1,0},{8,16},{9,17},{16,8},{17,9},{24,32},{25,33},{32,24},{3... | collective-permute-start | bytes 196616 | tf_op jit(solution)/shard_map/ppermute | solution.py:40
  9.2 8.0 %collective-permute-start.2 = (f32[128,128]{1,0:T(8,128)S(1)}, f32[128,128]{1,0:T(8,128)S(1)}, u32[]{:S(2)}, u32[]{:S(2)}) collective-permute-start(f32[128,128]{1,0:T(8,128)S(1)} %get-tuple-element.38), channel_id=1, source_target_pairs={{0,8},{8,0},{16,24},{24,16},{32,40},{40,32},{48,56},{56,48},{1,9},... | collective-permute-start | bytes 196616 | tf_op jit(solution)/shard_map/ppermute | solution.py:40
  36.6 5.5 %collective-permute-start.4 = (f32[2,56,128]{2,1,0:T(8,128)S(1)}, f32[2,56,128]{2,1,0:T(8,128)S(1)}, u32[]{:S(2)}, u32[]{:S(2)}) collective-permute-start(f32[2,56,128]{2,1,0:T(8,128)S(1)} %get-tuple-element.54), channel_id=1, source_target_pairs={{0,1},{1,0},{2,3},{3,2},{4,5},{5,4},{6,7},{7,6},{8,9},{9,8},{10,11... | collective-permute-start | bytes 172040 | tf_op jit(solution)/shard_map/ppermute | solution.py:40
  42.1 6.7 %collective-permute-start.5 = (f32[56,128]{1,0:T(8,128)S(1)}, f32[56,128]{1,0:T(8,128)S(1)}, u32[]{:S(2)}, u32[]{:S(2)}) collective-permute-start(f32[56,128]{1,0:T(8,128)S(1)} %fusion), channel_id=1, source_target_pairs={{0,8},{8,0},{1,9},{9,1},{2,10},{10,2},{3,11},{11,3},{4,12},{12,4},... | collective-permute-start | bytes 86024 | tf_op jit(solution)/shard_map/ppermute | solution.py:40
